TPU v7x, 32 devices: a whole 2x2x4 slice. The times are simulated.
32 devices in a mesh: grp: 4 (over x, core), ctx: 8 (over z, y).
Axes of the slice: x: 2, y: 2, z: 4, core: 2. Of those that a mesh axis runs over, the one named last changes fastest.
Arguments:
- tokens: bfloat16 [8192, 768], P(('grp', 'ctx')), may hold values from -6 to 6
- ln1_gain: bfloat16 [768], replicated, may hold values from 0.5 to 1.5
- ln1_bias: bfloat16 [768], replicated, may hold values from -1.75 to 1.75
- qkv_weight: bfloat16 [768, 2304], replicated, may hold values from -0.21875 to 0.21875
- qkv_bias: bfloat16 [2304], replicated, may hold values from -1.75 to 1.75
- out_weight: bfloat16 [768, 768], replicated, may hold values from -2 to 2
- out_bias: bfloat16 [768], replicated, may hold values from -1.75 to 1.75
- ln2_gain: bfloat16 [768], replicated, may hold values from 0.5 to 1.5
- ln2_bias: bfloat16 [768], replicated, may hold values from -1.75 to 1.75
- fc_weight: bfloat16 [768, 3072], replicated, may hold values from -0.21875 to 0.21875
- fc_bias: bfloat16 [3072], replicated, may hold values from -1.75 to 1.75
- proj_weight: bfloat16 [3072, 768], replicated, may hold values from -0.109375 to 0.109375
- proj_bias: bfloat16 [768], replicated, may hold values from -1.75 to 1.75
- doc_blocks: int32 [4, 5], P('grp'), may hold values from 0 to 128, as said below
- cotangent: bfloat16 [8192, 768], P(('grp', 'ctx')), may hold values from -6 to 6
Outputs:
- output: float32 [8192, 768], P(('grp', 'ctx'))
- grad_tokens: float32 [8192, 768], P(('grp', 'ctx'))
- grad_ln1_gain: float32 [768], P('ctx')
- grad_ln1_bias: float32 [768], P('ctx')
- grad_qkv_weight: float32 [768, 2304], P('ctx')
- grad_qkv_bias: float32 [2304], P('ctx')
- grad_out_weight: float32 [768, 768], P('ctx')
- grad_out_bias: float32 [768], P('ctx')
- grad_ln2_gain: float32 [768], P('ctx')
- grad_ln2_bias: float32 [768], P('ctx')
- grad_fc_weight: float32 [768, 3072], P('ctx')
- grad_fc_bias: float32 [3072], P('ctx')
- grad_proj_weight: float32 [3072, 768], P('ctx')
- grad_proj_bias: float32 [768], P('ctx')
Inputs may be any that keep to these rules, and one draw needn't show every extreme that they name: `doc_blocks`: each group's row holds one or more entries of 128; its other entries are 32 or 0, and the row sums to 256.
All inputs are finite; a program needn't handle non-finite values.
Results may differ from a plain program's by a relative error of at most 0.01.
Values may be sent and summed in bfloat16 or wider, within the bound.
No kernel may reach another device: no remote copies, remote signals or barrier semaphores. Data moves between devices by JAX's collectives and lax.ppermute only.
A program may use at most 320 MiB of HBM per device.

v0:
```python
import functools
import math

import jax
import jax.numpy as jnp
from jax import lax
from jax.experimental import pallas as pl
from jax.experimental.pallas import tpu as pltpu
from jax.sharding import Mesh
from jax.sharding import PartitionSpec as P

HEADS = 12
SEQ_LEN = 2048
FAR = 1e30
F32 = jnp.float32
BF16 = jnp.bfloat16
GRP = ("gx", "core")
CTX = ("hg", "part")
VMEM_BYTES = 56 * 1024 * 1024


class Sizes:
    def __init__(self, rows, width, hidden, docs, n_ctx, n_grp):
        self.rows, self.width, self.hidden, self.docs = rows, width, hidden, docs
        self.n_ctx, self.n_grp = n_ctx, n_grp
        self.head = width // HEADS
        self.block = min(rows // 2, SEQ_LEN // n_ctx)
        self.parts = rows // self.block
        self.groups = n_ctx // self.parts
        self.grain = self.block // 4
        self.grains = rows // self.grain
        self.per = -(-HEADS // self.groups)
        self.used = self.per * self.head
        self.lanes = -(-((self.per + 1) * self.head) // 128) * 128
        self.span = n_ctx * self.block
        self.tile = 256
        self.steps = self.span // self.tile
        self.gx = n_grp // 2
        self.scale = self.head ** (-0.5)
        band, share = width // n_ctx, hidden // (n_ctx * n_grp)
        self.aligned = band % 32 == 0 and share % 32 == 0 and share * n_ctx == width
        self.packed = band % (16 * self.gx) == 0 and 3 * self.lanes == width


def dot(a, b):
    return lax.dot_general(a, b, (((1,), (0,)), ((), ())), preferred_element_type=F32)


def dot_nt(a, b):
    return lax.dot_general(a, b, (((1,), (1,)), ((), ())), preferred_element_type=F32)


def dot_tn(a, b):
    return lax.dot_general(a, b, (((0,), (0,)), ((), ())), preferred_element_type=F32)


def dot_split(mask, value, transposed):
    high = value.astype(BF16)
    low = (value - high.astype(F32)).astype(BF16)
    mul = dot_tn if transposed else dot
    return mul(mask, high) + mul(mask, low)


def shift(value, axis, size, step):
    return lax.ppermute(value, axis, [(i, (i + step) % size) for i in range(size)])


def cost(flops, *arrays):
    size = sum(math.prod(a.shape) * a.dtype.itemsize for a in arrays)
    return pl.CostEstimate(flops=int(flops), bytes_accessed=int(size), transcendentals=0)


def whole_call(body, outs, n_scalars, args, name, scratch=(), flops=0):
    shapes = [jax.ShapeDtypeStruct(s, t) for s, t in outs]
    specs = [pl.BlockSpec(memory_space=pltpu.SMEM)] * n_scalars
    specs += [pl.BlockSpec(memory_space=pltpu.VMEM)] * (len(args) - n_scalars)
    return pl.pallas_call(
        body,
        out_shape=shapes,
        in_specs=specs,
        out_specs=[pl.BlockSpec(memory_space=pltpu.VMEM)] * len(outs),
        scratch_shapes=list(scratch),
        compiler_params=pltpu.CompilerParams(vmem_limit_bytes=VMEM_BYTES),
        cost_estimate=cost(flops, *args, *shapes),
        name=name,
    )(*args)


def source_grain(sz, doc_ref, place):
    is_long = [(doc_ref[0, d] == sz.block).astype(jnp.int32) for d in range(sz.docs)]
    longs = sum(is_long)
    seen_long, seen_short, begin, source = 0, 0, 0, 0
    for d in range(sz.docs):
        count = doc_ref[0, d] // sz.grain
        first = jnp.where(is_long[d] == 1, 4 * seen_long, 4 * longs + seen_short)
        inside = (place >= first) & (place < first + count)
        source = source + jnp.where(inside, begin + place - first, 0)
        seen_long = seen_long + is_long[d]
        seen_short = seen_short + jnp.where(is_long[d] == 1, 0, count)
        begin = begin + count
    return source


def part_is_long(sz, doc_ref, part):
    longs = sum((doc_ref[0, d] == sz.block).astype(jnp.int32) for d in range(sz.docs))
    return part < longs


def sort_rows(sz, place, docs, tokens, cotangent):
    def body(place_ref, doc_ref, tok_ref, cot_ref, *outs):
        part = place_ref[1]
        for s in range(sz.parts):
            base = 4 * ((part + s) % sz.parts)
            for a in range(4):
                src = source_grain(sz, doc_ref, base + a)
                at = pl.ds(a * sz.grain, sz.grain)
                outs[s][at, :] = tok_ref[src]
                outs[sz.parts + s][at, :] = cot_ref[src]

    shape = (sz.grains, sz.grain, sz.width)
    out = whole_call(
        body,
        [((sz.block, sz.width), BF16)] * (2 * sz.parts),
        2,
        (place, docs, tokens.reshape(shape), cotangent.reshape(shape)),
        "sort_rows",
    )
    return out[: sz.parts], out[sz.parts :]


def normalize(x):
    center = x - jnp.mean(x, axis=-1, keepdims=True)
    spread = jnp.mean(center * center, axis=-1, keepdims=True)
    r = lax.rsqrt(spread + 1e-05)
    return center * r, r


def pair_masks(sz, step, long_part):
    keys = (step + 1) * sz.tile
    q_row = step * sz.tile + lax.broadcasted_iota(jnp.int32, (sz.tile, 1), 0)
    k_row = lax.broadcasted_iota(jnp.int32, (1, keys), 1)
    q_doc = jnp.where(long_part, 0, (q_row % sz.block) // sz.grain)
    k_doc = jnp.where(long_part, 0, (k_row % sz.block) // sz.grain)
    k_in = jnp.where(long_part, k_row % sz.block, k_row % sz.grain)
    first = (k_row < sz.block) & (k_in == 0)
    same = q_doc == k_doc
    visible = same & (k_row <= q_row)
    select = same & (k_row < q_row) & jnp.logical_not(first)
    return visible, select


def slot_mask(sz, slot):
    lane = lax.broadcasted_iota(jnp.int32, (1, sz.lanes), 1)
    return lane // sz.head == slot


def lower_mask(sz):
    row = lax.broadcasted_iota(jnp.int32, (sz.tile, sz.tile), 0)
    col = lax.broadcasted_iota(jnp.int32, (sz.tile, sz.tile), 1)
    return jnp.where(row > col, 1.0, 0.0).astype(BF16)


def penalty_of(sz, step, long_part, lower, q_slot, k, carry):
    visible, select = pair_masks(sz, step, long_part)
    positive = jnp.maximum(dot_nt(q_slot, k), 0.0)
    chosen = jnp.where(select, positive * positive * (1.0 / sz.block), 0.0)
    penalty = dot_split(lower, chosen, False) + carry
    return jnp.where(visible, penalty, FAR), chosen, positive, select


def attend_forward(sz, place, docs, chunks, gain, bias, w_sel, b_sel):
    n_in = len(chunks)
    lw = sz.lanes

    def body(place_ref, doc_ref, *refs):
        xs = refs[:n_in]
        gain_ref, bias_ref, w_ref, b_ref = refs[n_in : n_in + 4]
        qkv_ref, normed_ref, hat_ref, lse_ref, out_ref, carry_ref = refs[n_in + 4 : n_in + 10]
        att_refs = refs[n_in + 10 : n_in + 10 + sz.groups]
        hg, part = place_ref[0], place_ref[1]
        long_part = part_is_long(sz, doc_ref, part)
        for k in range(sz.groups):
            for s in range(sz.parts):
                at = ((hg - k) % sz.groups) * sz.parts + (part - s) % sz.parts
                at = pl.ds(pl.multiple_of(at * sz.block, sz.block), sz.block)
                hat, _ = normalize(xs[k * sz.parts + s][...].astype(F32))
                normed = (hat * gain_ref[...] + bias_ref[...]).astype(BF16)
                hat_ref[at, :] = hat.astype(BF16)
                normed_ref[at, :] = normed
                qkv_ref[at, :] = (dot(normed, w_ref[...]) + b_ref[...]).astype(BF16)
        lower = lower_mask(sz)
        lane = lax.broadcasted_iota(jnp.int32, (1, 128), 1)
        carry_ref[...] = jnp.zeros_like(carry_ref)
        for step in range(sz.steps):
            keys = (step + 1) * sz.tile
            rows = slice(step * sz.tile, keys)
            q = qkv_ref[rows, :lw] * sz.scale
            k = qkv_ref[:keys, lw : 2 * lw]
            v = qkv_ref[:keys, 2 * lw :]
            q_slot = jnp.where(slot_mask(sz, sz.per), q, 0)
            pen, chosen, _, _ = penalty_of(
                sz, step, long_part, lower, q_slot, k, carry_ref[step : step + 1, :keys]
            )
            if step + 1 < sz.steps:
                carry_ref[step + 1 : step + 2, :keys] = carry_ref[step : step + 1, :keys] + jnp.sum(
                    chosen, axis=0, keepdims=True
                )
            total = jnp.zeros((sz.tile, lw), F32)
            lse = jnp.zeros((sz.tile, 128), F32)
            for h in range(sz.per):
                mask = slot_mask(sz, h)
                logits = dot_nt(jnp.where(mask, q, 0), k) - pen
                top = jnp.max(logits, axis=1, keepdims=True)
                weights = jnp.exp(logits - top)
                weight = jnp.sum(weights, axis=1, keepdims=True)
                mixed = dot(weights.astype(BF16), v) / weight
                total = jnp.where(mask, mixed, total)
                lse = jnp.where(lane == h, top + jnp.log(weight), lse)
            out_ref[rows, :] = total
            lse_ref[rows, :] = lse
        for k in range(sz.groups):
            at = pl.multiple_of(((hg + k) % sz.groups) * sz.rows, sz.rows)
            att_refs[k][...] = out_ref[pl.ds(at, sz.rows), : sz.used].astype(BF16)

    outs = [
        ((sz.span, 3 * lw), BF16),
        ((sz.span, sz.width), BF16),
        ((sz.span, sz.width), BF16),
        ((sz.span, 128), F32),
        ((sz.span, lw), F32),
        ((sz.steps, sz.span), F32),
    ] + [((sz.rows, sz.used), BF16)] * sz.groups
    out = whole_call(body, outs, 2, (place, docs, *chunks, gain, bias, w_sel, b_sel), "attend_forward", flops=9e9)
    return out[:6], out[6:]


def attend_backward(sz, place, docs, saved, w_sel, grads):
    lw = sz.lanes
    qkv, _, hat, lse, att, carry = saved

    def body(place_ref, doc_ref, qkv_ref, hat_ref, lse_ref, att_ref, carry_ref, w_ref, *refs):
        grad_refs = refs[: sz.groups]
        outs = refs[sz.groups :]
        dqkv_ref, sums_ref, lnsum_ref = outs[:3]
        dnorm_ref, dout, dk_sum, dv_sum, behind = outs[3:]
        hg, part = place_ref[0], place_ref[1]
        long_part = part_is_long(sz, doc_ref, part)
        dout[...] = jnp.zeros_like(dout)
        for k in range(sz.groups):
            at = pl.multiple_of(((hg - k) % sz.groups) * sz.rows, sz.rows)
            dout[pl.ds(at, sz.rows), : sz.used] = grad_refs[k][...]
        dk_sum[...] = jnp.zeros_like(dk_sum)
        dv_sum[...] = jnp.zeros_like(dv_sum)
        behind[...] = jnp.zeros_like(behind)
        lower = lower_mask(sz)
        for step in reversed(range(sz.steps)):
            keys = (step + 1) * sz.tile
            rows = slice(step * sz.tile, keys)
            q = qkv_ref[rows, :lw] * sz.scale
            k = qkv_ref[:keys, lw : 2 * lw]
            v = qkv_ref[:keys, 2 * lw :]
            d_rows = dout[rows, :]
            dot_rows = d_rows.astype(F32) * att_ref[rows, :]
            last = slot_mask(sz, sz.per)
            q_slot = jnp.where(last, q, 0)
            pen, _, positive, select = penalty_of(
                sz, step, long_part, lower, q_slot, k, carry_ref[step : step + 1, :keys]
            )
            dpen = jnp.zeros((sz.tile, keys), F32)
            dq = jnp.zeros((sz.tile, lw), F32)
            for h in range(sz.per):
                mask = slot_mask(sz, h)
                q_h = jnp.where(mask, q, 0)
                d_h = jnp.where(mask, d_rows, 0)
                probs = jnp.exp(dot_nt(q_h, k) - pen - lse_ref[rows, h : h + 1])
                delta = jnp.sum(jnp.where(mask, dot_rows, 0.0), axis=1, keepdims=True)
                ds = probs * (dot_nt(d_h, v) - delta)
                dpen = dpen - ds
                ds_low = ds.astype(BF16)
                dq = jnp.where(mask, dot(ds_low, k), dq)
                dk_sum[:keys, :] += dot_tn(ds_low, q_h)
                dv_sum[:keys, :] += dot_tn(probs.astype(BF16), d_h)
            dchosen = dot_split(lower, dpen, True) + behind[:1, :keys]
            behind[:1, :keys] += jnp.sum(dpen, axis=0, keepdims=True)
            ds_low = jnp.where(select, positive * dchosen * (2.0 / sz.block), 0.0).astype(BF16)
            dq = jnp.where(last, dot(ds_low, k), dq)
            dk_sum[:keys, :] += dot_tn(ds_low, q_slot)
            dqkv_ref[rows, :lw] = (dq * sz.scale).astype(BF16)
        dqkv_ref[:, lw : 2 * lw] = dk_sum[...].astype(BF16)
        dqkv_ref[:, 2 * lw :] = dv_sum[...].astype(BF16)
        sums_ref[...] = jnp.sum(dqkv_ref[...].astype(F32), axis=0, keepdims=True)
        gain_sum = jnp.zeros((1, sz.width), F32)
        bias_sum = jnp.zeros((1, sz.width), F32)
        for i in range(sz.n_ctx):
            at = slice(i * sz.block, (i + 1) * sz.block)
            dnorm = dot_nt(dqkv_ref[at, :], w_ref[...])
            dnorm_ref[i] = dnorm.astype(BF16)
            bias_sum += jnp.sum(dnorm, axis=0, keepdims=True)
            gain_sum += jnp.sum(dnorm * hat_ref[at, :].astype(F32), axis=0, keepdims=True)
        lnsum_ref[0:1, :] = gain_sum
        lnsum_ref[1:2, :] = bias_sum

    outs = [((sz.span, 3 * lw), BF16), ((1, 3 * lw), F32), ((2, sz.width), F32)]
    outs += [((sz.n_ctx, sz.block, sz.width), BF16)]
    scratch = [
        pltpu.VMEM((sz.span, lw), BF16),
        pltpu.VMEM((sz.span, lw), F32),
        pltpu.VMEM((sz.span, lw), F32),
        pltpu.VMEM((8, sz.span), F32),
    ]
    out = whole_call(
        body, outs, 2, (place, docs, qkv, hat, lse, att, carry, w_sel, *grads), "attend_backward", scratch, 17e9
    )
    return out


def project_out(sz, place, att, tokens, out_weight, out_bias, gain, bias):
    def body(place_ref, *refs):
        att_refs = refs[: sz.groups]
        tok_refs = refs[sz.groups : sz.groups + sz.parts]
        w_ref, b_ref, gain_ref, bias_ref, middle_ref, second_ref = refs[sz.groups + sz.parts :]
        hg, part = place_ref[0], place_ref[1]
        for s in range(sz.parts):
            at = pl.ds(pl.multiple_of(((part - s) % sz.parts) * sz.block, sz.block), sz.block)
            middle_ref[at, :] = tok_refs[s][...].astype(F32) + b_ref[...]
        total = middle_ref[...]
        for k in range(sz.groups):
            at = pl.multiple_of(((hg - k) % sz.groups) * sz.used, 16)
            total += dot(att_refs[k][...], w_ref[pl.ds(at, sz.used), :])
        middle_ref[...] = total
        hat, _ = normalize(total)
        second_ref[...] = (hat * gain_ref[...] + bias_ref[...]).astype(BF16)

    outs = [((sz.rows, sz.width), F32), ((sz.rows, sz.width), BF16)]
    return whole_call(
        body, outs, 1, (place, *att, *tokens, out_weight, out_bias, gain, bias), "project_out"
    )


def feed_forward(sz, second, cot, fc, fc_bias, proj, name):
    n = len(second)
    units = fc.shape[1]
    root = math.sqrt(2.0 / math.pi)

    def body(*refs):
        second_refs, cot_refs = refs[:n], refs[n : 2 * n]
        fc_ref, bias_ref, proj_ref = refs[2 * n : 2 * n + 3]
        outs = refs[2 * n + 3 :]
        act_refs, grad_refs, back_refs, sums_ref = outs[:n], outs[n : 2 * n], outs[2 * n : 3 * n], outs[3 * n]
        total = jnp.zeros((1, units), F32)
        for i in range(n):
            hidden = dot(second_refs[i][...], fc_ref[...]) + bias_ref[...]
            square = hidden * hidden
            t = jnp.tanh(root * (hidden + 0.044715 * hidden * square))
            half = 0.5 * (1.0 + t)
            act_refs[i][...] = (hidden * half).astype(BF16)
            slope = half + 0.5 * hidden * (1.0 - t * t) * (root * (1.0 + 3.0 * 0.044715 * square))
            grad = (dot_nt(cot_refs[i][...], proj_ref[...]) * slope).astype(BF16)
            grad_refs[i][...] = grad
            back_refs[i][...] = dot_nt(grad, fc_ref[...]).astype(BF16)
            total += jnp.sum(grad.astype(F32), axis=0, keepdims=True)
        sums_ref[...] = total

    outs = [((sz.rows, units), BF16)] * (2 * n) + [((sz.rows, sz.width), BF16)] * n + [((1, units), F32)]
    out = whole_call(body, outs, 0, (*second, *cot, fc, fc_bias, proj), name)
    return out[:n], out[n : 2 * n], out[2 * n : 3 * n], out[3 * n]


def middle_backward(sz, place, back, middle, cot, out_weight, gain):
    n_back = len(back)

    def body(place_ref, *refs):
        back_refs = refs[:n_back]
        cot_refs = refs[n_back : n_back + sz.parts]
        rest = refs[n_back + sz.parts :]
        middle_ref, w_ref, gain_ref = rest[:3]
        branch_ref, sums_ref = rest[3:5]
        gm_refs = rest[5 : 5 + sz.parts]
        datt_refs = rest[5 + sz.parts : 5 + sz.parts + sz.groups]
        total = rest[-1]
        hg, part = place_ref[0], place_ref[1]
        cot_sum = jnp.zeros((1, sz.width), F32)
        for s in range(sz.parts):
            at = pl.ds(pl.multiple_of(((part - s) % sz.parts) * sz.block, sz.block), sz.block)
            block = cot_refs[s][...].astype(F32)
            total[at, :] = block
            cot_sum += jnp.sum(block, axis=0, keepdims=True)
        e = back_refs[0][...].astype(F32)
        for ref in back_refs[1:]:
            e += ref[...].astype(F32)
        hat, r = normalize(middle_ref[...])
        eg = e * gain_ref[...]
        inner = eg - jnp.mean(eg, axis=-1, keepdims=True)
        inner -= hat * jnp.mean(eg * hat, axis=-1, keepdims=True)
        grad = total[...] + r * inner
        total[...] = grad
        branch = grad.astype(BF16)
        branch_ref[...] = branch
        for s in range(sz.parts):
            at = pl.ds(pl.multiple_of(((part + s) % sz.parts) * sz.block, sz.block), sz.block)
            gm_refs[s][...] = total[at, :]
        for k in range(sz.groups):
            at = pl.multiple_of(((hg + k) % sz.groups) * sz.used, 16)
            datt_refs[k][...] = dot_nt(branch, w_ref[pl.ds(at, sz.used), :]).astype(BF16)
        sums_ref[0:1, :] = jnp.sum(e * hat, axis=0, keepdims=True)
        sums_ref[1:2, :] = jnp.sum(e, axis=0, keepdims=True)
        sums_ref[2:3, :] = jnp.sum(branch.astype(F32), axis=0, keepdims=True)
        sums_ref[3:4, :] = cot_sum

    outs = [((sz.rows, sz.width), BF16), ((4, sz.width), F32)]
    outs += [((sz.block, sz.width), F32)] * sz.parts
    outs += [((sz.rows, sz.used), BF16)] * sz.groups
    out = whole_call(
        body,
        outs,
        1,
        (place, *back, *cot, middle, out_weight, gain),
        "middle_backward",
        [pltpu.VMEM((sz.rows, sz.width), F32)],
        4 * sz.rows * sz.width * sz.width,
    )
    split = 2 + sz.parts
    return out[0], out[1], out[2:split], out[split:]


def weight_terms(sz, place, left, right, name):
    n = len(left)
    width = sz.width
    rows = left[0].shape[1] // sz.n_ctx

    if not sz.aligned:
        both = dot_tn(jnp.concatenate(left, axis=0), jnp.concatenate(right, axis=0)).astype(BF16)
        both = both.reshape(sz.groups, sz.parts, -1, width)
        pieces = []
        for s in range(sz.parts):
            piece = lax.dynamic_index_in_dim(both, (place[1] + s) % sz.parts, 1, keepdims=False)
            pieces.append(jnp.roll(piece, -place[0], axis=0))
        return pieces

    def body(place_ref, *refs):
        piece_refs = refs[2 * n : -1]
        held = refs[-1]
        hg, part = place_ref[0], place_ref[1]
        held[...] = sum(dot_tn(a[...], b[...]) for a, b in zip(refs[:n], refs[n : 2 * n])).astype(BF16)
        for s in range(sz.parts):
            for k in range(sz.groups):
                to = ((hg + k) % sz.groups) * sz.parts + (part + s) % sz.parts
                at = pl.multiple_of(to * rows, 16)
                piece_refs[s][k] = held[pl.ds(at, rows), :]

    return whole_call(
        body,
        [((sz.groups, rows, width), BF16)] * sz.parts,
        1,
        (place, *left, *right),
        name,
        [pltpu.VMEM((left[0].shape[1], width), BF16)],
    )


def feed_forward_out(sz, act, proj):
    n = len(act)

    def body(*refs):
        for i in range(n):
            refs[n + 1 + i][...] = dot(refs[i][...], refs[n][...]).astype(BF16)

    return whole_call(body, [((sz.rows, sz.width), BF16)] * n, 0, (*act, proj), "feed_forward_out")


def out_weights(sz, place, att, branch):
    half = sz.width // 2

    def body(place_ref, *refs):
        branch_ref, own_ref, other_ref = refs[sz.groups :]
        hg, core = place_ref[0], place_ref[2]
        for k in range(sz.groups):
            at = pl.multiple_of(((hg - k) % sz.groups) * sz.used, 16)

            @pl.when(at < sz.width)
            def _():
                grad_w = dot_tn(refs[k][...], branch_ref[...]).astype(BF16)
                left, right = grad_w[:, :half], grad_w[:, half:]
                own_ref[pl.ds(at, sz.used), :] = jnp.where(core == 0, left, right)
                other_ref[pl.ds(at, sz.used), :] = jnp.where(core == 0, right, left)

    return whole_call(body, [((sz.width, half), BF16)] * 2, 1, (place, *att, branch), "out_weights")


def sum_near(sz, pieces):
    if not sz.aligned:
        total = sum(p.astype(F32) for p in pieces).astype(BF16)
        return [total[k] for k in range(sz.groups)]
    n = len(pieces)

    def body(*refs):
        for k in range(sz.groups):
            total = refs[0][k].astype(F32)
            for s in range(1, n):
                total += refs[s][k].astype(F32)
            refs[n + k][...] = total.astype(BF16)

    return whole_call(body, [(pieces[0].shape[1:], BF16)] * sz.groups, 0, tuple(pieces), "sum_near")


def pack_sums(sz, place, terms, tail):
    rows, lanes = terms[0][0].shape[1:]
    full = rows * len(terms) + tail.shape[1]
    if not sz.packed:
        sums = [sum(t.astype(F32) for t in pair).astype(BF16) for pair in terms]
        sums = jnp.concatenate(sums + [tail], axis=1).reshape((sz.groups, sz.parts, full, lanes))
        sums = jnp.roll(sums, (-place[0], -place[1]), axis=(0, 1))
        return [sums[:, s] for s in range(sz.parts)]
    flat = [t for pair in terms for t in pair]
    per = len(terms[0])

    def body(place_ref, *refs):
        tail_ref = refs[len(flat)]
        outs = refs[len(flat) + 1 :]
        for k in range(sz.groups):
            for s in range(sz.parts):
                to = ((place_ref[0] + k) % sz.groups) * sz.parts + (place_ref[1] + s) % sz.parts
                for i in range(len(terms)):
                    total = sum(refs[i * per + j][to].astype(F32) for j in range(per))
                    outs[s][k, i * rows : (i + 1) * rows, :] = total.astype(BF16)
                outs[s][k, rows * len(terms) :, :] = tail_ref[to]

    return whole_call(
        body, [((sz.groups, full, lanes), BF16)] * sz.parts, 1, (place, *flat, tail), "pack_sums"
    )


def add_halves(value):
    half = value.shape[-2] // 2
    value = value.astype(F32)
    return value[..., :half, :] + value[..., half:, :]


def split_halves(value, axis):
    high = value.astype(BF16)
    return jnp.concatenate([high, (value - high.astype(F32)).astype(BF16)], axis=axis)


def sum_packed(sz, pieces, rows):
    if not sz.packed:
        total = sum(p[:, : 2 * rows].astype(F32) for p in pieces).astype(BF16)
        tail = split_halves(sum(add_halves(p[:, 2 * rows :]) for p in pieces), 1)
        total = jnp.concatenate([total, tail], axis=1)
        return [total[k] for k in range(sz.groups)]
    n = len(pieces)

    def body(*refs):
        for k in range(sz.groups):
            out = refs[n + k]
            out[: 2 * rows, :] = sum(r[k, : 2 * rows, :].astype(F32) for r in refs[:n]).astype(BF16)
            out[2 * rows :, :] = split_halves(sum(add_halves(r[k, 2 * rows :, :]) for r in refs[:n]), 0)

    return whole_call(body, [(pieces[0].shape[1:], BF16)] * sz.groups, 0, tuple(pieces), "sum_packed")


def unpack_sums(sz, place, blocks, rows):
    full, lanes = blocks[0].shape
    if not sz.packed:
        got = jnp.stack(blocks)
        sel = jnp.roll(got[::-1, :rows], place[0] + 1, axis=0)
        total = got[:, rows : 2 * rows].astype(F32).sum(axis=0).astype(BF16)
        return jnp.concatenate([sel, total[None]], axis=0), add_halves(got[:, 2 * rows :]).sum(axis=0)

    def body(place_ref, *refs):
        sel_ref, small_ref = refs[sz.groups :]
        for k in range(sz.groups):
            sel_ref[(place_ref[0] - k) % sz.groups] = refs[k][:rows, :]
        total = sum(r[rows : 2 * rows, :].astype(F32) for r in refs[: sz.groups])
        sel_ref[sz.groups] = total.astype(BF16)
        small_ref[...] = sum(add_halves(r[2 * rows :, :]) for r in refs[: sz.groups])

    return whole_call(
        body,
        [((sz.groups + 1, rows, lanes), BF16), (((full - 2 * rows) // 2, lanes), F32)],
        1,
        (place, *blocks),
        "unpack_sums",
    )


def join_shares(sz, place, fc_shares, proj_shares):
    band, width = sz.width // sz.n_ctx, sz.width
    share = sz.hidden // (sz.n_ctx * sz.n_grp)
    n = sz.n_grp

    def body(place_ref, *refs):
        fc_ref, proj_ref, held, held_proj = refs[2 * n :]
        core, gx = place_ref[2], place_ref[3]
        for c in range(2):
            for k in range(sz.gx):
                at = ((gx - k) % sz.gx) * 2 + (core + c) % 2
                held[at] = refs[c * sz.gx + k][...]
                held_proj[at] = refs[n + c * sz.gx + k][...]
        for j in range(sz.n_ctx):
            cut = slice(j * share, (j + 1) * share)
            fc_ref[:, j * share * n : (j + 1) * share * n] = jnp.concatenate(
                [held[q, :, cut].astype(F32) for q in range(n)], axis=1
            )
        for q in range(n):
            proj_ref[q * share : (q + 1) * share, :] = held_proj[q].astype(F32)

    if not sz.aligned:
        fc = order_grp(sz, place, fc_shares).reshape(n, band, sz.n_ctx, share)
        fc = fc.transpose(1, 2, 0, 3).reshape(band, sz.hidden)
        return fc, order_grp(sz, place, proj_shares).reshape(n * share, width)
    return whole_call(
        body,
        [((band, sz.hidden), F32), ((n * share, width), F32)],
        1,
        (place, *fc_shares, *proj_shares),
        "join_shares",
        [pltpu.VMEM((n,) + fc_shares[0].shape, BF16), pltpu.VMEM((n,) + proj_shares[0].shape, BF16)],
    )


def order_grp(sz, place, values):
    held = jnp.stack(values).reshape((2, sz.gx) + values[0].shape)
    held = jnp.roll(held[:, ::-1], place[3] + 1, axis=1)
    return jnp.roll(held, place[2], axis=0).swapaxes(0, 1).astype(F32)


def qkv_weights(sz, place, normed, dqkv):
    w3 = 3 * sz.lanes
    half = w3 // 2

    def body(place_ref, normed_ref, dqkv_ref, own_ref, other_ref):
        core = place_ref[2]
        grad = dot_tn(normed_ref[...], dqkv_ref[...]).astype(BF16)
        own_ref[...] = jnp.where(core == 0, grad[:, :half], grad[:, half:])
        other_ref[...] = jnp.where(core == 0, grad[:, half:], grad[:, :half])

    return whole_call(body, [((sz.width, half), BF16)] * 2, 1, (place, normed, dqkv), "qkv_weights")


def join_heads(sz, place, pieces):
    rows, lanes = pieces[0].shape[1:]
    w3 = 3 * sz.lanes
    if not sz.packed:
        held = order_grp(sz, place, pieces)
        sel = held[:, :, : sz.groups].transpose(2, 0, 3, 1, 4).reshape(sz.groups, sz.gx * rows, w3)
        out = held[:, :, sz.groups].transpose(0, 2, 1, 3).reshape(sz.gx * rows, 2 * lanes)
        return join_slots(sz, sel), out

    def body(place_ref, *refs):
        sel_ref, out_ref, held = refs[sz.n_grp :]
        core, gx = place_ref[2], place_ref[3]
        for c in range(2):
            for k in range(sz.gx):
                held[((gx - k) % sz.gx) * 2 + (core + c) % 2] = refs[c * sz.gx + k][...]
        for x in range(sz.gx):
            at_rows = slice(x * rows, (x + 1) * rows)
            both = [
                jnp.concatenate([held[2 * x, g], held[2 * x + 1, g]], axis=1).astype(F32)
                for g in range(sz.groups)
            ]
            for third in range(3):
                at = third * sz.lanes
                own = jnp.concatenate([b[:, at : at + sz.used] for b in both], axis=1)[:, : sz.width]
                first = sum(b[:, at + sz.used : at + sz.used + sz.head] for b in both)
                rest = jnp.zeros((rows, sz.width - sz.head), F32)
                sel_ref[at_rows, third * sz.width : (third + 1) * sz.width] = own + jnp.concatenate(
                    [first, rest], axis=1
                )
            for c in range(2):
                out_ref[at_rows, c * lanes : (c + 1) * lanes] = held[2 * x + c, sz.groups].astype(F32)

    return whole_call(
        body,
        [((sz.gx * rows, 3 * sz.width), F32), ((sz.gx * rows, sz.width), F32)],
        1,
        (place, *pieces),
        "join_heads",
        [pltpu.VMEM((sz.n_grp,) + pieces[0].shape, BF16)],
    )


def join_slots(sz, sel):
    n = sel.shape[1]
    thirds = sel.reshape(sz.groups, n, 3, sz.lanes)
    own = thirds[..., : sz.used].transpose(2, 1, 0, 3).reshape(3, n, sz.groups * sz.used)
    own = own[..., : sz.width]
    first = thirds[..., sz.used : sz.used + sz.head].sum(axis=0).transpose(1, 0, 2)
    own = own.at[:, :, : sz.head].add(first)
    return own.transpose(1, 0, 2).reshape(n, 3 * sz.width)


def finish_tokens(sz, place, docs, dnorm, tokens, grad_middle, gain):
    def body(place_ref, doc_ref, d_ref, *refs):
        tok_refs = refs[: sz.parts]
        gm_refs = refs[sz.parts : 2 * sz.parts]
        gain_ref, out_ref, held = refs[2 * sz.parts :]
        part = place_ref[1]
        for s in range(sz.parts):
            base = (part - s) % sz.parts
            e = d_ref[base].astype(F32)
            for k in range(1, sz.groups):
                e += d_ref[k * sz.parts + base].astype(F32)
            hat, r = normalize(tok_refs[(-s) % sz.parts][...].astype(F32))
            eg = e * gain_ref[...]
            inner = eg - jnp.mean(eg, axis=-1, keepdims=True)
            inner -= hat * jnp.mean(eg * hat, axis=-1, keepdims=True)
            held[...] = gm_refs[s][...] + r * inner
            for a in range(4):
                src = source_grain(sz, doc_ref, 4 * base + a)
                out_ref[src] = held[pl.ds(a * sz.grain, sz.grain), :]

    out = whole_call(
        body,
        [((sz.grains, sz.grain, sz.width), F32)],
        2,
        (place, docs, dnorm, *tokens, *grad_middle, gain),
        "finish_tokens",
        [pltpu.VMEM((sz.block, sz.width), F32)],
    )
    return out[0].reshape(sz.rows, sz.width)


def finish_middle(sz, place, mixed, middle, proj_bias):
    n = len(mixed)

    def body(place_ref, *refs):
        middle_ref, bias_ref = refs[n : n + 2]
        outs = refs[n + 2 :]
        part = place_ref[1]
        for s in range(sz.parts):
            at = pl.ds(pl.multiple_of(((part + s) % sz.parts) * sz.block, sz.block), sz.block)
            total = middle_ref[at, :] + bias_ref[...]
            for ref in refs[:n]:
                total += ref[at, :].astype(F32)
            outs[s][...] = total

    return whole_call(
        body,
        [((sz.block, sz.width), F32)] * sz.parts,
        1,
        (place, *mixed, middle, proj_bias),
        "finish_middle",
    )


def unsort_rows(sz, place, docs, blocks):
    def body(place_ref, doc_ref, *refs):
        out_ref = refs[-1]
        part = place_ref[1]
        for s in range(sz.parts):
            base = 4 * ((part - s) % sz.parts)
            for a in range(4):
                src = source_grain(sz, doc_ref, base + a)
                out_ref[src] = refs[s][pl.ds(a * sz.grain, sz.grain), :]

    out = whole_call(
        body,
        [((sz.grains, sz.grain, sz.width), F32)],
        2,
        (place, docs, *blocks),
        "unsort_rows",
    )
    return out[0].reshape(sz.rows, sz.width)


def order_rows(sz, place, blocks):
    def body(place_ref, *refs):
        for s in range(sz.parts):
            at = pl.multiple_of(((place_ref[1] - s) % sz.parts) * sz.block, sz.block)
            refs[-1][pl.ds(at, sz.block), :] = refs[s][...]

    return whole_call(body, [((sz.rows, sz.width), BF16)], 1, (place, *blocks), "order_rows")[0]


def gather_rows(sz, block):
    near = [block, shift(block, "core", 2, 1)]
    far = []
    for k in range(1, sz.gx):
        along = shift(block, "gx", sz.gx, k)
        far += [along, shift(along, "core", 2, 1)]
    return near, far


def return_rows(sz, near, far, later):
    terms = [near[0], shift(near[1], "core", 2, 1)]
    for k in range(1, sz.gx):
        mine, other = far[2 * k - 2 : 2 * k]
        mine = (mine.astype(F32) + shift(other, "core", 2, 1).astype(F32)).astype(BF16)
        mine, later = lax.optimization_barrier((mine, later))
        terms.append(shift(mine, "gx", sz.gx, -k))
    return terms, later


def all_grp(sz, value):
    along = [value] + [shift(value, "gx", sz.gx, k) for k in range(1, sz.gx)]
    return along + [shift(v, "core", 2, 1) for v in along]


def after(gate, value):
    return lax.optimization_barrier((gate, value))[1]


def head_columns(sz, weight, hg):
    lead = weight.shape[:-1]
    pieces = []
    for third in range(3):
        full = weight[..., third * sz.width : (third + 1) * sz.width]
        spare = sz.groups * sz.used - sz.width
        if spare:
            full = jnp.pad(full, [(0, 0)] * len(lead) + [(0, spare)])
        own = lax.dynamic_slice_in_dim(full, hg * sz.used, sz.used, axis=len(lead))
        first = full[..., : sz.head] if third < 2 else jnp.zeros(lead + (sz.head,), weight.dtype)
        rest = sz.lanes - sz.used - sz.head
        pieces += [own, first]
        if rest:
            pieces.append(jnp.zeros(lead + (rest,), weight.dtype))
    return jnp.concatenate(pieces, axis=-1)


def weight_shares(sz, place, qkv_weight, fc_weight, proj_weight):
    share = sz.hidden // (sz.n_ctx * sz.n_grp)
    units = sz.n_ctx * share
    if not sz.aligned:
        mine = place[3] * 2 + place[2]
        w_sel = head_columns(sz, qkv_weight, place[0])
        fc = fc_weight.reshape(sz.width, sz.n_ctx, sz.n_grp, share)
        fc = lax.dynamic_index_in_dim(fc, mine, 2, keepdims=False).reshape(sz.width, units)
        proj = proj_weight.reshape(sz.n_ctx, sz.n_grp, share, sz.width)
        proj = lax.dynamic_index_in_dim(proj, mine, 1, keepdims=False).reshape(units, sz.width)
        return w_sel, fc, proj

    def body(place_ref, qkv_ref, fc_in, proj_in, sel_ref, fc_ref, proj_ref):
        hg, mine = place_ref[0], place_ref[3] * 2 + place_ref[2]
        for third in range(3):
            to, base = third * sz.lanes, third * sz.width
            end = jnp.zeros((sz.width, sz.lanes - sz.used), BF16)
            if third < 2:
                end = qkv_ref[:, base : base + 128][:, : sz.head]
                if sz.lanes - sz.used > sz.head:
                    end = jnp.concatenate(
                        [end, jnp.zeros((sz.width, sz.lanes - sz.used - sz.head), BF16)], axis=1
                    )
            for g in range(sz.groups):

                @pl.when(hg == g)
                def _():
                    own = qkv_ref[:, base : base + sz.width][:, g * sz.used : (g + 1) * sz.used]
                    sel_ref[:, to : to + sz.lanes] = jnp.concatenate([own, end], axis=1)

        wide = share * sz.n_grp
        for q in range(sz.n_grp):

            @pl.when(mine == q)
            def _():
                fc_ref[...] = jnp.concatenate(
                    [
                        fc_in[:, j * wide : (j + 1) * wide][:, q * share : (q + 1) * share]
                        for j in range(sz.n_ctx)
                    ],
                    axis=1,
                )

        for j in range(sz.n_ctx):
            at = pl.multiple_of(j * wide + mine * share, 16)
            proj_ref[j * share : (j + 1) * share, :] = proj_in[pl.ds(at, share), :]

    return whole_call(
        body,
        [((sz.width, 3 * sz.lanes), BF16), ((sz.width, units), BF16), ((units, sz.width), BF16)],
        1,
        (place, qkv_weight, fc_weight, proj_weight),
        "weight_shares",
    )


def body(
    tokens,
    ln1_gain,
    ln1_bias,
    qkv_weight,
    qkv_bias,
    out_weight,
    out_bias,
    ln2_gain,
    ln2_bias,
    fc_weight,
    fc_bias,
    proj_weight,
    proj_bias,
    doc_blocks,
    cotangent,
):
    rows, width = tokens.shape
    hidden = fc_weight.shape[1]
    n_ctx = lax.axis_size("hg") * lax.axis_size("part")
    n_grp = lax.axis_size("gx") * 2
    sz = Sizes(rows, width, hidden, doc_blocks.shape[1], n_ctx, n_grp)
    hg, part = lax.axis_index("hg"), lax.axis_index("part")
    gx, core = lax.axis_index("gx"), lax.axis_index("core")
    place = jnp.stack([hg, part, core, gx]).astype(jnp.int32)
    mine = gx * 2 + core

    def vector(v):
        return v.astype(F32)[None, :]

    gain1, bias1 = vector(ln1_gain), vector(ln1_bias)
    gain2, bias2 = vector(ln2_gain), vector(ln2_bias)
    share = hidden // (n_ctx * n_grp)
    b_sel = head_columns(sz, vector(qkv_bias), hg)
    fc_b = lax.dynamic_index_in_dim(
        vector(fc_bias).reshape(1, n_ctx, n_grp, share), mine, 2, keepdims=False
    ).reshape(1, n_ctx * share)
    spare = sz.groups * sz.used - sz.width
    w_out = jnp.pad(out_weight, ((0, spare), (0, 0))) if spare else out_weight

    tok_parts, cot_parts = sort_rows(sz, place, doc_blocks, tokens, cotangent)
    tok_mine = [tok_parts[0]] + [shift(tok_parts[s], "part", sz.parts, s) for s in range(1, sz.parts)]
    order = sorted(range(1, sz.groups), key=lambda k: -min(k, sz.groups - k))
    chunks = {(0, s): tok_mine[s] for s in range(sz.parts)}
    for s in range(sz.parts):
        for k in order:
            chunks[k, s] = shift(tok_mine[s], "hg", sz.groups, k)
    chunks = [chunks[k, s] for k in range(sz.groups) for s in range(sz.parts)]

    cot_parts, qkv_weight, fc_weight, proj_weight = after(
        chunks[order[0] * sz.parts], (cot_parts, qkv_weight, fc_weight, proj_weight)
    )
    cot_mine = [cot_parts[0]] + [shift(cot_parts[s], "part", sz.parts, s) for s in range(1, sz.parts)]
    cot_rows = order_rows(sz, place, cot_mine)
    cot_near, cot_far = gather_rows(sz, cot_rows)
    w_sel, fc, proj = weight_shares(sz, place, qkv_weight, fc_weight, proj_weight)

    chunks = after(cot_rows, chunks)
    saved, att_out = attend_forward(sz, place, doc_blocks, chunks, gain1, bias1, w_sel, b_sel)
    att = [att_out[0]] + [shift(att_out[k], "hg", sz.groups, k) for k in range(1, sz.groups)]

    middle, second = project_out(sz, place, after(cot_far, att), tok_mine, w_out, vector(out_bias), gain2, bias2)

    sec_near, sec_far = gather_rows(sz, second)
    act_n, gh_n, back_n, fc_sum_n = feed_forward(sz, sec_near, cot_near, fc, fc_b, proj, "feed_forward_near")
    act_f, gh_f, back_f, fc_sum_f = feed_forward(
        sz, after(back_n, sec_far), cot_far, fc, fc_b, proj, "feed_forward_far"
    )
    fc_sum = fc_sum_n + fc_sum_f
    back, act_f = return_rows(sz, back_n, back_f, act_f)
    proj_pieces = weight_terms(sz, place, act_n + act_f, cot_near + cot_far, "proj_terms")
    gh_f = after(proj_pieces, gh_f)
    fc_pieces = weight_terms(sz, place, sec_near + sec_far, gh_n + gh_f, "fc_terms")
    mixed = feed_forward_out(sz, act_n + after(fc_pieces, act_f), proj)
    back = after(mixed, back)
    branch, mid_sums, gm_parts, datt_out = middle_backward(
        sz, place, back, middle, cot_mine, w_out, gain2
    )
    datt = [datt_out[0]] + [shift(datt_out[k], "hg", sz.groups, k) for k in range(1, sz.groups)]

    band = width // n_ctx
    half = width // 2
    n_rows = band // sz.gx
    def near_sums(pieces):
        return sum_near(
            sz, [pieces[0]] + [shift(pieces[s], "part", sz.parts, s) for s in range(1, sz.parts)]
        )

    def far_sum(near):
        total = near[0].astype(F32)
        for k in range(1, sz.groups):
            total = total + shift(near[k], "hg", sz.groups, k).astype(F32)
        return total.astype(BF16)

    proj_share = far_sum(near_sums(proj_pieces))
    fc_near = near_sums(fc_pieces)
    fc_share = far_sum(fc_near)
    grad_fc, grad_proj = join_shares(sz, place, all_grp(sz, fc_share), all_grp(sz, proj_share))

    def over_grp(own, other):
        both = own.astype(F32) + shift(other, "core", 2, 1).astype(F32)
        both = both.astype(BF16).reshape(n_ctx, sz.gx, n_rows, own.shape[1])
        pieces = []
        for k in range(sz.gx):
            piece = lax.dynamic_index_in_dim(both, (gx + k) % sz.gx, 1, keepdims=False)
            pieces.append(shift(piece, "gx", sz.gx, k) if k else piece)
        return pieces

    d_out = out_weights(sz, place, att, branch)
    out_terms = over_grp(*d_out)
    datt = after((proj_share, fc_near, d_out), datt)

    mixed, _ = return_rows(sz, mixed[:2], mixed[2:], place)
    out_parts = finish_middle(sz, place, mixed, middle, vector(proj_bias))
    out_mine = [out_parts[0]] + [shift(out_parts[s], "part", sz.parts, s) for s in range(1, sz.parts)]
    output = unsort_rows(sz, place, doc_blocks, out_mine)

    dqkv, qkv_sum, ln1_sums, dnorm = attend_backward(sz, place, doc_blocks, saved, w_sel, datt)
    dnorm = lax.all_to_all(after(fc_share, dnorm), CTX, 0, 0, tiled=True)
    gm_mine = [gm_parts[0]] + [shift(gm_parts[s], "part", sz.parts, s) for s in range(1, sz.parts)]
    dnorm = after((output, grad_fc), dnorm)
    grad_tokens = finish_tokens(sz, place, doc_blocks, dnorm, tok_parts, gm_mine, gain1)

    w3 = 3 * sz.lanes
    w_half = w3 // 2
    sel_terms = over_grp(*qkv_weights(sz, place, saved[1], dqkv))

    placed = jnp.zeros((sz.groups, 1, w3), F32)
    placed = lax.dynamic_update_slice(placed, qkv_sum[None], (hg, 0, 0))
    fc_placed = jnp.zeros((n_ctx, n_grp, share), F32)
    fc_placed = lax.dynamic_update_slice(fc_placed, fc_sum.reshape(n_ctx, 1, share), (0, mine, 0))
    vectors = [
        ln1_sums[0],
        ln1_sums[1],
        join_slots(sz, placed)[0],
        mid_sums[2],
        mid_sums[0],
        mid_sums[1],
        fc_placed.reshape(-1),
        mid_sums[3],
    ]
    small = jnp.concatenate([v.reshape(n_ctx, -1) for v in vectors], axis=1)
    small = small + shift(small, "core", 2, 1)
    small = small + sum(shift(small, "gx", sz.gx, k) for k in range(1, sz.gx))
    n_small = small.shape[1]
    small = jnp.pad(small, ((0, 0), (0, -n_small % (8 * w_half)))).reshape(n_ctx, -1, w_half)
    pieces = pack_sums(sz, place, [sel_terms, out_terms], split_halves(small, 1))
    pieces = [pieces[0]] + [shift(pieces[s], "part", sz.parts, s) for s in range(1, sz.parts)]
    blocks = sum_packed(sz, pieces, n_rows)
    blocks = [blocks[0]] + [shift(blocks[k], "hg", sz.groups, k) for k in range(1, sz.groups)]
    sums, small = unpack_sums(sz, place, after(grad_tokens, blocks), n_rows)
    grad_qkv, grad_out = join_heads(sz, place, all_grp(sz, sums))

    small = small.reshape(-1)
    cuts, at = [], 0
    for v in vectors:
        n = v.shape[0] // n_ctx
        cuts.append(small[at : at + n])
        at += n
    g_ln1_gain, g_ln1_bias, g_qkv_bias, g_out_bias, g_ln2_gain, g_ln2_bias, g_fc_bias, g_proj_bias = cuts
    return (
        output,
        grad_tokens,
        g_ln1_gain,
        g_ln1_bias,
        grad_qkv,
        g_qkv_bias,
        grad_out,
        g_out_bias,
        g_ln2_gain,
        g_ln2_bias,
        grad_fc,
        g_fc_bias,
        grad_proj,
        g_proj_bias,
    )


def solution(mesh):
    n_grp, n_ctx = mesh.devices.shape
    split = P(GRP + CTX, None)

    def run(tokens, *rest):
        rows = tokens.shape[0] // (n_grp * n_ctx)
        parts = rows // min(rows // 2, SEQ_LEN // n_ctx)
        fine = Mesh(mesh.devices.reshape(n_grp // 2, 2, n_ctx // parts, parts), GRP + CTX)
        each = jax.shard_map(
            body,
            mesh=fine,
            in_specs=(split,) + (P(),) * 12 + (P(GRP, None), split),
            out_specs=(
                split,
                split,
                P(CTX),
                P(CTX),
                P(CTX, None),
                P(CTX),
                P(CTX, None),
                P(CTX),
                P(CTX),
                P(CTX),
                P(CTX, None),
                P(CTX),
                P(CTX, None),
                P(CTX),
            ),
            check_vma=False,
        )
        return each(tokens, *rest)

    return run
```

profile of v0, /device:TPU:1, one launch (start us, length us, event | category | flops | bytes accessed | tf_op | source)
XLA Modules:
  0.0 274.6 jit_solution(1526220942050173664)
XLA Ops:
  1.3 2.2 sort_rows.1
  3.5 3.1 %collective-permute-start = (bf16[128,768]{1,0:T(8,128)(2,1)}, bf16[128,768]{1,0:T(8,128)(2,1)S(1)}, u32[]{:S(2)}, u32[]{:S(2)}) collective-permute-start(bf16[128,768]{1,0:T(8,128)(2,1)} %get-tuple-element.151.refs_0_.refs_4_), channel_id=1, source_target_pairs={{0,4},{2,6},{4,0},{6,2},{1,5},{3,7},{5,1},{7,3},{8,12},{10,14},{12... | collective-permute-start | bytes 589832 | tf_op jit(solution)/shard_map/ppermute | solution.py:65
  7.9 2.0 collective-permute-start.8
  11.8 8.1 %collective-permute-done.refs_4_ = bf16[128,768]{1,0:T(8,128)(2,1)S(1)} collective-permute-done((bf16[128,768]{1,0:T(8,128)(2,1)}, bf16[128,768]{1,0:T(8,128)(2,1)S(1)}, u32[]{:S(2)}, u32[]{:S(2)}) %collective-permute-start) | collective-permute-done | bytes 196640 | tf_op jit(solution)/shard_map/ppermute | solution.py:65
  20.9 3.7 %collective-permute-done.1.refs_1_.refs_4_ = bf16[128,768]{1,0:T(8,128)(2,1)S(1)} collective-permute-done((bf16[128,768]{1,0:T(8,128)(2,1)}, bf16[128,768]{1,0:T(8,128)(2,1)S(1)}, u32[]{:S(2)}, u32[]{:S(2)}) %collective-permute-start.1) | collective-permute-done | bytes 196640 | tf_op jit(solution)/shard_map/ppermute | solution.py:65
  25.4 1.8 order_rows.1.refs_2_.refs_4_
  29.5 2.4 collective-permute-start.7
  33.5 7.9 %weight_shares.1 = (bf16[768,768]{1,0:T(8,128)(2,1)}, bf16[768,768]{1,0:T(8,128)(2,1)}, bf16[768,768]{1,0:T(8,128)(2,1)}) custom-call(s32[4]{0:T(128)} %pad_add_fusion.place_ref, bf16[768,2304]{1,0:T(8,128)(2,1)} %qkv_ref, bf16[768,3072]{1,0:T(8,128)(2,1)} %fc_in, bf16[3072,768]{1,0:T(8,128)(2,1)} %proj_in), custom_call_target="tpu_custom_call" | custom-call | bytes 16515088 | tf_op jit(solution)/shard_map/weight_shares/pallas_call | solution.py:77
  41.5 3.4 %collective-permute-done.7.refs_5_ = bf16[128,768]{1,0:T(8,128)(2,1)S(1)} collective-permute-done((bf16[128,768]{1,0:T(8,128)(2,1)S(1)}, bf16[128,768]{1,0:T(8,128)(2,1)S(1)}, u32[]{:S(2)}, u32[]{:S(2)}) %collective-permute-start.7) | collective-permute-done | bytes 196640 | tf_op jit(solution)/shard_map/ppermute | solution.py:65
  44.9 2.4 collective-permute-start.3
  47.4 11.1 %attend_forward.1 = (bf16[1024,768]{1,0:T(8,128)(2,1)}, bf16[1024,768]{1,0:T(8,128)(2,1)}, bf16[1024,768]{1,0:T(8,128)(2,1)}, f32[1024,128]{1,0:T(8,128)}, f32[1...) custom-call(s32[4]{0:T(128)} %pad_add_fusion.place_ref, ...), custom_call_target="tpu_custom_call" | custom-call | flops 8999999488 | bytes 9462820 | tf_op jit(solution)/shard_map/attend_forward/pallas_call | solution.py:77
  58.5 3.5 %collective-permute-start.10 = (bf16[256,192]{1,0:T(8,128)(2,1)}, bf16[256,192]{1,0:T(8,128)(2,1)S(1)}, u32[]{:S(2)}, u32[]{:S(2)}) collective-permute-start(bf16[256,192]{1,0:T(8,128)(2,1)} %get-tuple-element.164), channel_id=1, source_target_pairs={{0,2},{2,4},{4,6},{6,0},{1,3},{3,5},{5,7},{7,1},{8,10},{10,12},{12... | collective-permute-start | bytes 294920 | tf_op jit(solution)/shard_map/ppermute | solution.py:65
  66.4 6.2 %collective-permute-done.11.refs_2_ = bf16[256,192]{1,0:T(8,128)(2,1)S(1)} collective-permute-done((bf16[256,192]{1,0:T(8,128)(2,1)}, bf16[256,192]{1,0:T(8,128)(2,1)S(1)}, u32[]{:S(2)}, u32[]{:S(2)}) %collective-permute-start.11) | collective-permute-done | bytes 98336 | tf_op jit(solution)/shard_map/ppermute | solution.py:65
  73.3 3.3 %project_out.1 = (f32[256,768]{1,0:T(8,128)}, bf16[256,768]{1,0:T(8,128)(2,1)}) custom-call(s32[4]{0:T(128)} %pad_add_fusion.place_ref, bf16[256,192]{1,0:T(8,128)(2,1)} %get-tuple-element.167.refs_0_, bf16[256,192]{1,0:T(8,128)(2,1)} %copy-done.15, bf16[256,192]{1,0:T(8,128)(2,1)} %copy-done.16, bf16[256,192]{1,0:T(8,128)(2,1)} %copy-done.17, ...), custom_call_target="tpu_custom_call" | custom-call | bytes 3154960 | tf_op jit(solution)/shard_map/project_out/pallas_call | solution.py:77
  77.8 9.1 %collective-permute-done.15.refs_0_.refs_2_ = bf16[256,768]{1,0:T(8,128)(2,1)S(1)} collective-permute-done((bf16[256,768]{1,0:T(8,128)(2,1)}, bf16[256,768]{1,0:T(8,128)(2,1)S(1)}, u32[]{:S(2)}, u32[]{:S(2)}) %collective-permute-start.15) | collective-permute-done | bytes 393248 | tf_op jit(solution)/shard_map/ppermute | solution.py:65
  90.0 5.8 %feed_forward_near.1 = (bf16[256,768]{1,0:T(8,128)(2,1)}, bf16[256,768]{1,0:T(8,128)(2,1)}, bf16[256,768]{1,0:T(8,128)(2,1)}, bf16[256,768]{1,0:T(8,128)(2,1)}, ...) custom-call(bf16[256,768]{1,0:T(8,128)(2,1)} %get-tuple-element.171.refs_0_, ...), custom_call_target="tpu_custom_call" | custom-call | bytes 6297600 | tf_op jit(solution)/shard_map/feed_forward_near/pallas_call | solution.py:77
  96.6 5.7 %feed_forward_far.1 = (bf16[256,768]{1,0:T(8,128)(2,1)}, bf16[256,768]{1,0:T(8,128)(2,1)}, bf16[256,768]{1,0:T(8,128)(2,1)}, bf16[256,768]{1,0:T(8,128)(2,1)}, b...) custom-call(bf16[256,768]{1,0:T(8,128)(2,1)} %copy-done.4, bf16[256,768]{1,0:T(8,128)(2,1)} %copy-done.6, ...), custom_call_target="tpu_custom_call" | custom-call | bytes 6297600 | tf_op jit(solution)/shard_map/feed_forward_far/pallas_call | solution.py:77
  102.4 1.9 collective-permute-done.17
  105.4 4.3 %proj_terms.1 = (bf16[4,96,768]{2,1,0:T(8,128)(2,1)}, bf16[4,96,768]{2,1,0:T(8,128)(2,1)}) custom-call(s32[4]{0:T(128)} %pad_add_fusion.place_ref, bf16[256,768]{1,0:T(8,128)(2,1)} %get-tuple-element.174.refs_0_, bf16[256,768]{1,0:T(8,128)(2,1)} %get-tuple-element.175.refs_1_, bf16[256,768]{1,0:T(8,128)(2,1)} %get-tuple-element.196.refs_2_, ...), custom_call_target="tpu_custom_call" | custom-call | bytes 4325392 | tf_op jit(solution)/shard_map/proj_terms/pallas_call | solution.py:77
  111.0 4.4 %fc_terms.1 = (bf16[4,96,768]{2,1,0:T(8,128)(2,1)}, bf16[4,96,768]{2,1,0:T(8,128)(2,1)}) custom-call(s32[4]{0:T(128)} %pad_add_fusion.place_ref, bf16[256,768]{1,0:T(8,128)(2,1)} %get-tuple-element.171.refs_0_, bf16[256,768]{1,0:T(8,128)(2,1)} %copy-done.5, bf16[256,768]{1,0:T(8,128)(2,1)} %copy-done.4, bf16[256,768]{1,0:T(8,128)(2,1)} %copy-done.6, ...), custom_call_target="tpu_custom_call" | custom-call | bytes 4325392 | tf_op jit(solution)/shard_map/fc_terms/pallas_call | solution.py:77
  116.7 8.0 %collective-permute-done.29.refs_1_ = bf16[4,96,768]{2,1,0:T(8,128)(2,1)S(1)} collective-permute-done((bf16[4,96,768]{2,1,0:T(8,128)(2,1)}, bf16[4,96,768]{2,1,0:T(8,128)(2,1)S(1)}, u32[]{:S(2)}, u32[]{:S(2)}) %collective-permute-start.29) | collective-permute-done | bytes 589856 | tf_op jit(solution)/shard_map/ppermute | solution.py:65
  125.5 2.1 sum_near.3
  127.6 3.1 %collective-permute-start.30 = (bf16[96,768]{1,0:T(8,128)(2,1)}, bf16[96,768]{1,0:T(8,128)(2,1)S(1)}, u32[]{:S(2)}, u32[]{:S(2)}) collective-permute-start(bf16[96,768]{1,0:T(8,128)(2,1)} %get-tuple-element.211), channel_id=1, source_target_pairs={{0,2},{2,4},{4,6},{6,0},{1,3},{3,5},{5,7},{7,1},{8,10},{10,12},{12... | collective-permute-start | bytes 442376 | tf_op jit(solution)/shard_map/ppermute | solution.py:65
  133.0 3.9 %feed_forward_out.1 = (bf16[256,768]{1,0:T(8,128)(2,1)}, bf16[256,768]{1,0:T(8,128)(2,1)}, bf16[256,768]{1,0:T(8,128)(2,1)}, bf16[256,768]{1,0:T(8,128)(2,1)}) custom-call(bf16[256,768]{1,0:T(8,128)(2,1)} %get-tuple-element.174.refs_0_, bf16[256,768]{1,0:T(8,128)(2,1)} %get-tuple-element.175.refs_1_, bf16[256,768]{1,0:T(8,128)(2,1)} %get-tuple-element.196.refs_2_, ...), custom_call_target="tpu_custom_call" | custom-call | bytes 4325376 | tf_op jit(solution)/shard_map/feed_forward_out/pallas_call | solution.py:77
  137.0 2.1 collective-permute-start.19
  139.1 4.3 %middle_backward.1 = (bf16[256,768]{1,0:T(8,128)(2,1)}, f32[4,768]{1,0:T(4,128)}, f32[128,768]{1,0:T(8,128)}, f32[128,768]{1,0:T(8,128)}, bf16[256,192]{1,0:T(8,...) custom-call(s32[4]{0:T(128)} %pad_add_fusion.place_ref, ...), custom_call_target="tpu_custom_call" | custom-call | flops 603979776 | bytes 5127184 | tf_op jit(solution)/shard_map/middle_backward/pallas_call | solution.py:77
  143.4 3.4 %out_weights.1 = (bf16[768,384]{1,0:T(8,128)(2,1)}, bf16[768,384]{1,0:T(8,128)(2,1)}) custom-call(s32[4]{0:T(128)} %pad_add_fusion.place_ref, bf16[256,192]{1,0:T(8,128)(2,1)} %get-tuple-element.167.refs_0_, bf16[256,192]{1,0:T(8,128)(2,1)} %copy-done.15, bf16[256,192]{1,0:T(8,128)(2,1)} %copy-done.16, bf16[256,192]{1,0:T(8,128)(2,1)} %copy-done.17, ...), custom_call_target="tpu_custom_call" | custom-call | bytes 1966096 | tf_op jit(solution)/shard_map/out_weights/pallas_call | solution.py:77
  147.7 2.1 sum_near.2
  154.2 6.6 %collective-permute-done.39.refs_2_ = bf16[256,192]{1,0:T(8,128)(2,1)S(1)} collective-permute-done((bf16[256,192]{1,0:T(8,128)(2,1)S(1)}, bf16[256,192]{1,0:T(8,128)(2,1)S(1)}, u32[]{:S(2)}, u32[]{:S(2)}) %collective-permute-start.39) | collective-permute-done | bytes 98336 | tf_op jit(solution)/shard_map/ppermute | solution.py:65
  160.8 3.4 %collective-permute-start.25 = (bf16[96,768]{1,0:T(8,128)(2,1)}, bf16[96,768]{1,0:T(8,128)(2,1)S(1)}, u32[]{:S(2)}, u32[]{:S(2)}) collective-permute-start(bf16[96,768]{1,0:T(8,128)(2,1)} %get-tuple-element.209), channel_id=1, source_target_pairs={{0,6},{2,0},{4,2},{6,4},{1,7},{3,1},{5,3},{7,5},{8,14},{10,8},{12,... | collective-permute-start | bytes 442376 | tf_op jit(solution)/shard_map/ppermute | solution.py:65
  164.2 17.8 %attend_backward.1 = (bf16[1024,768]{1,0:T(8,128)(2,1)}, f32[1,768]{1,0:T(1,128)}, f32[2,768]{1,0:T(2,128)}, bf16[8,128,768]{2,1,0:T(8,128)(2,1)}) custom-call(s32[4]{0:T(128)} %pad_add_fusion.place_ref, s32[1,5]{1,0:T(1,128)} %doc_ref.9, bf16[1024,768]{1,0:T(8,128)(2,1)} %get-tuple-element.215.qkv_ref, bf16[1024,768]{1,0:T(8,128)(2,1)} %get-tuple-element.216.hat_ref, ...), custom_call_target="tpu_custom_call" | custom-call | flops 16999999488 | bytes 9462820 | tf_op jit(solution)/shard_map/attend_backward/pallas_call | solution.py:77
  182.2 8.9 %all-to-all-start = ((bf16[8,128,768]{2,1,0:T(8,128)(2,1)}), bf16[8,128,768]{2,1,0:T(8,128)(2,1)S(1)}, u32[]{:S(2)}, u32[]{:S(2)}) async-start(bf16[8,128,768]{2,1,0:T(8,128)(2,1)} %get-tuple-element.236), calls=%async_computation | async-start | bytes 3145728 | tf_op jit(solution)/shard_map/all_to_all | solution.py:994
  193.6 4.4 %qkv_weights.1 = (bf16[768,384]{1,0:T(8,128)(2,1)}, bf16[768,384]{1,0:T(8,128)(2,1)}) custom-call(s32[4]{0:T(128)} %pad_add_fusion.place_ref, bf16[1024,768]{1,0:T(8,128)(2,1)} %get-tuple-element.240.normed_ref, bf16[1024,768]{1,0:T(8,128)(2,1)} %get-tuple-element.241.dqkv_ref), custom_call_target="tpu_custom_call" | custom-call | bytes 4325392 | tf_op jit(solution)/shard_map/qkv_weights/pallas_call | solution.py:77
  205.8 10.6 %collective-permute-done.45.refs_3_ = bf16[8,48,384]{2,1,0:T(8,128)(2,1)S(1)} collective-permute-done((bf16[8,48,384]{2,1,0:T(8,128)(2,1)S(1)}, bf16[8,48,384]{2,1,0:T(8,128)(2,1)S(1)}, u32[]{:S(2)}, u32[]{:S(2)}) %collective-permute-start.45) | collective-permute-done | bytes 294944 | tf_op jit(solution)/shard_map/ppermute | solution.py:65
  216.4 6.3 %collective-permute-done.43.refs_1_ = bf16[8,48,384]{2,1,0:T(8,128)(2,1)S(1)} collective-permute-done((bf16[8,48,384]{2,1,0:T(8,128)(2,1)S(1)}, bf16[8,48,384]{2,1,0:T(8,128)(2,1)S(1)}, u32[]{:S(2)}, u32[]{:S(2)}) %collective-permute-start.43) | collective-permute-done | bytes 294944 | tf_op jit(solution)/shard_map/ppermute | solution.py:65
  223.4 2.2 pack_sums.1
  225.7 1.7 collective-permute-start.48
  229.9 2.5 finish_middle.1
  233.9 2.3 collective-permute-start.34
  237.5 4.1 %collective-permute-done.26.refs_1_ = bf16[96,768]{1,0:T(8,128)(2,1)S(1)} collective-permute-done((bf16[96,768]{1,0:T(8,128)(2,1)S(1)}, bf16[96,768]{1,0:T(8,128)(2,1)S(1)}, u32[]{:S(2)}, u32[]{:S(2)}) %collective-permute-start.26) | collective-permute-done | bytes 147488 | tf_op jit(solution)/shard_map/ppermute | solution.py:65
  243.2 1.9 sum_packed.1
  246.3 2.1 collective-permute-start.50
  249.6 3.1 %join_shares.1 = (f32[96,3072]{1,0:T(8,128)}, f32[384,768]{1,0:T(8,128)}) custom-call(s32[4]{0:T(128)} %pad_add_fusion.place_ref, bf16[96,768]{1,0:T(8,128)(2,1)} %copy-done.14, bf16[96,768]{1,0:T(8,128)(2,1)} %copy-done.36, bf16[96,768]{1,0:T(8,128)(2,1)} %copy-done.37, bf16[96,768]{1,0:T(8,128)(2,1)} %copy-done.39, bf16[96,768]{1,0:T(8,128)(2,1)} %copy-done.13, ...), custom_call_target="tpu_custom_call" | custom-call | bytes 3538960 | tf_op jit(solution)/shard_map/join_shares/pallas_call | solution.py:77
  253.5 2.3 unsort_rows.1
  257.0 3.3 %finish_tokens.1 = f32[8,32,768]{2,1,0:T(8,128)} custom-call(s32[4]{0:T(128)} %pad_add_fusion.place_ref, s32[1,5]{1,0:T(1,128)} %doc_ref.9, bf16[8,128,768]{2,1,0:T(8,128)(2,1)} %copy-done, bf16[128,768]{1,0:T(8,128)(2,1)} %get-tuple-element.151.refs_0_.refs_4_, bf16[128,768]{1,0:T(8,128)(2,1)} %get-tuple-element.150.refs_1_, ...), custom_call_target="tpu_custom_call" | custom-call | bytes 3542052 | tf_op jit(solution)/shard_map/finish_tokens/pallas_call | solution.py:77
  261.0 1.7 unpack_sums.1
  268.2 1.8 collective-permute-start.54
  271.9 2.4 join_heads.1
  (284 shorter events, 62.0 us)
Async XLA Ops:
  3.5 16.4 %collective-permute-start = (bf16[128,768]{1,0:T(8,128)(2,1)}, bf16[128,768]{1,0:T(8,128)(2,1)S(1)}, u32[]{:S(2)}, u32[]{:S(2)}) collective-permute-start(bf16[128,768]{1,0:T(8,128)(2,1)} %get-tuple-element.151.refs_0_.refs_4_), channel_id=1, source_target_pairs={{0,4},{2,6},{4,0},{6,2},{1,5},{3,7},{5,1},{7,3},{8,12},{10,14},{12... | collective-permute-start | bytes 589832 | tf_op jit(solution)/shard_map/ppermute | solution.py:65
  6.6 25.3 %collective-permute-start.5 = (bf16[128,768]{1,0:T(8,128)(2,1)}, bf16[128,768]{1,0:T(8,128)(2,1)S(1)}, u32[]{:S(2)}, u32[]{:S(2)}) collective-permute-start(bf16[128,768]{1,0:T(8,128)(2,1)} %get-tuple-element.151.refs_0_.refs_4_), channel_id=1, source_target_pairs={{0,2},{2,4},{4,6},{6,0},{1,3},{3,5},{5,7},{7,1},{8,10},{10,12},{12... | collective-permute-start | bytes 589832 | tf_op jit(solution)/shard_map/ppermute | solution.py:65
  7.9 33.5 %collective-permute-start.8 = (bf16[128,768]{1,0:T(8,128)(2,1)}, bf16[128,768]{1,0:T(8,128)(2,1)S(1)}, u32[]{:S(2)}, u32[]{:S(2)}) collective-permute-start(bf16[128,768]{1,0:T(8,128)(2,1)} %get-tuple-element.151.refs_0_.refs_4_), channel_id=1, source_target_pairs={{0,6},{2,0},{4,2},{6,4},{1,7},{3,1},{5,3},{7,5},{8,14},{10,8},{12,... | collective-permute-start | bytes 589832 | tf_op jit(solution)/shard_map/ppermute | solution.py:65
  9.9 19.6 %collective-permute-start.4 = (bf16[128,768]{1,0:T(8,128)(2,1)}, bf16[128,768]{1,0:T(8,128)(2,1)S(1)}, u32[]{:S(2)}, u32[]{:S(2)}) collective-permute-start(bf16[128,768]{1,0:T(8,128)(2,1)} %get-tuple-element.150.refs_1_), channel_id=1, source_target_pairs={{0,1},{1,0},{2,3},{3,2},{4,5},{5,4},{6,7},{7,6},{8,9},{9,8},{10,11... | collective-permute-start | bytes 589832 | tf_op jit(solution)/shard_map/ppermute | solution.py:65
  27.2 17.8 %collective-permute-start.2 = (bf16[256,768]{1,0:T(8,128)(2,1)}, bf16[256,768]{1,0:T(8,128)(2,1)S(1)}, u32[]{:S(2)}, u32[]{:S(2)}) collective-permute-start(bf16[256,768]{1,0:T(8,128)(2,1)} %order_rows.1.refs_2_.refs_4_), channel_id=1, source_target_pairs={{0,16},{16,0},{1,17},{17,1},{2,18},{18,2},{3,19},{19,3},{4,20},{20... | collective-permute-start | bytes 1179656 | tf_op jit(solution)/shard_map/ppermute | solution.py:65
  29.5 12.0 %collective-permute-start.6 = (bf16[128,768]{1,0:T(8,128)(2,1)S(1)}, bf16[128,768]{1,0:T(8,128)(2,1)S(1)}, u32[]{:S(2)}, u32[]{:S(2)}) collective-permute-start(bf16[128,768]{1,0:T(8,128)(2,1)S(1)} %collective-permute-done.4.refs_1_.refs_5_), channel_id=1, source_target_pairs={{0,2},{2,4},{4,6},{6,0},{1,3},{3,5},{5,7},{7,1},{8,10},{10,12},{12... | collective-permute-start | bytes 589832 | tf_op jit(solution)/shard_map/ppermute | solution.py:65
  29.5 15.4 %collective-permute-start.7 = (bf16[128,768]{1,0:T(8,128)(2,1)S(1)}, bf16[128,768]{1,0:T(8,128)(2,1)S(1)}, u32[]{:S(2)}, u32[]{:S(2)}) collective-permute-start(bf16[128,768]{1,0:T(8,128)(2,1)S(1)} %collective-permute-done.4.refs_1_.refs_5_), channel_id=1, source_target_pairs={{0,4},{2,6},{4,0},{6,2},{1,5},{3,7},{5,1},{7,3},{8,12},{10,14},{12... | collective-permute-start | bytes 589832 | tf_op jit(solution)/shard_map/ppermute | solution.py:65
  32.0 13.0 %collective-permute-start.9 = (bf16[128,768]{1,0:T(8,128)(2,1)S(1)}, bf16[128,768]{1,0:T(8,128)(2,1)S(1)}, u32[]{:S(2)}, u32[]{:S(2)}) collective-permute-start(bf16[128,768]{1,0:T(8,128)(2,1)S(1)} %collective-permute-done.4.refs_1_.refs_5_), channel_id=1, source_target_pairs={{0,6},{2,0},{4,2},{6,4},{1,7},{3,1},{5,3},{7,5},{8,14},{10,8},{12,... | collective-permute-start | bytes 589832 | tf_op jit(solution)/shard_map/ppermute | solution.py:65
  44.9 27.7 %collective-permute-start.3 = (bf16[256,768]{1,0:T(8,128)(2,1)S(1)}, bf16[256,768]{1,0:T(8,128)(2,1)S(1)}, u32[]{:S(2)}, u32[]{:S(2)}) collective-permute-start(bf16[256,768]{1,0:T(8,128)(2,1)S(1)} %collective-permute-done.2.refs_2_.refs_6_), channel_id=1, source_target_pairs={{0,8},{8,0},{1,9},{9,1},{2,10},{10,2},{3,11},{11,3},{4,12},{12,4},... | collective-permute-start | bytes 1179656 | tf_op jit(solution)/shard_map/ppermute | solution.py:65
  58.5 7.9 %collective-permute-start.10 = (bf16[256,192]{1,0:T(8,128)(2,1)}, bf16[256,192]{1,0:T(8,128)(2,1)S(1)}, u32[]{:S(2)}, u32[]{:S(2)}) collective-permute-start(bf16[256,192]{1,0:T(8,128)(2,1)} %get-tuple-element.164), channel_id=1, source_target_pairs={{0,2},{2,4},{4,6},{6,0},{1,3},{3,5},{5,7},{7,1},{8,10},{10,12},{12... | collective-permute-start | bytes 294920 | tf_op jit(solution)/shard_map/ppermute | solution.py:65
  62.1 10.6 %collective-permute-start.11 = (bf16[256,192]{1,0:T(8,128)(2,1)}, bf16[256,192]{1,0:T(8,128)(2,1)S(1)}, u32[]{:S(2)}, u32[]{:S(2)}) collective-permute-start(bf16[256,192]{1,0:T(8,128)(2,1)} %get-tuple-element.165), channel_id=1, source_target_pairs={{0,4},{2,6},{4,0},{6,2},{1,5},{3,7},{5,1},{7,3},{8,12},{10,14},{12... | collective-permute-start | bytes 294920 | tf_op jit(solution)/shard_map/ppermute | solution.py:65
  63.1 9.5 %collective-permute-start.12 = (bf16[256,192]{1,0:T(8,128)(2,1)}, bf16[256,192]{1,0:T(8,128)(2,1)S(1)}, u32[]{:S(2)}, u32[]{:S(2)}) collective-permute-start(bf16[256,192]{1,0:T(8,128)(2,1)} %get-tuple-element.166), channel_id=1, source_target_pairs={{0,6},{2,0},{4,2},{6,4},{1,7},{3,1},{5,3},{7,5},{8,14},{10,8},{12,... | collective-permute-start | bytes 294920 | tf_op jit(solution)/shard_map/ppermute | solution.py:65
  76.6 10.3 %collective-permute-start.15 = (bf16[256,768]{1,0:T(8,128)(2,1)}, bf16[256,768]{1,0:T(8,128)(2,1)S(1)}, u32[]{:S(2)}, u32[]{:S(2)}) collective-permute-start(bf16[256,768]{1,0:T(8,128)(2,1)} %get-tuple-element.171.refs_0_), channel_id=1, source_target_pairs={{0,16},{16,0},{1,17},{17,1},{2,18},{18,2},{3,19},{19,3},{4,20},{20... | collective-permute-start | bytes 1179656 | tf_op jit(solution)/shard_map/ppermute | solution.py:65
  76.9 12.2 %collective-permute-start.14 = (bf16[256,768]{1,0:T(8,128)(2,1)S(1)}, bf16[256,768]{1,0:T(8,128)(2,1)S(1)}, u32[]{:S(2)}, u32[]{:S(2)}) collective-permute-start(bf16[256,768]{1,0:T(8,128)(2,1)S(1)} %copy-done.1), channel_id=1, source_target_pairs={{0,8},{8,0},{1,9},{9,1},{2,10},{10,2},{3,11},{11,3},{4,12},{12,4},... | collective-permute-start | bytes 1179656 | tf_op jit(solution)/shard_map/ppermute | solution.py:65
  77.8 11.3 %collective-permute-start.13 = (bf16[256,768]{1,0:T(8,128)(2,1)}, bf16[256,768]{1,0:T(8,128)(2,1)S(1)}, u32[]{:S(2)}, u32[]{:S(2)}) collective-permute-start(bf16[256,768]{1,0:T(8,128)(2,1)} %get-tuple-element.171.refs_0_), channel_id=1, source_target_pairs={{0,8},{8,0},{1,9},{9,1},{2,10},{10,2},{3,11},{11,3},{4,12},{12,4},... | collective-permute-start | bytes 1179656 | tf_op jit(solution)/shard_map/ppermute | solution.py:65
  86.9 8.9 %collective-permute-start.16 = (bf16[256,768]{1,0:T(8,128)(2,1)S(1)}, bf16[256,768]{1,0:T(8,128)(2,1)S(1)}, u32[]{:S(2)}, u32[]{:S(2)}) collective-permute-start(bf16[256,768]{1,0:T(8,128)(2,1)S(1)} %collective-permute-done.15.refs_0_.refs_2_), channel_id=1, source_target_pairs={{0,8},{8,0},{1,9},{9,1},{2,10},{10,2},{3,11},{11,3},{4,12},{12,4},... | collective-permute-start | bytes 1179656 | tf_op jit(solution)/shard_map/ppermute | solution.py:65
  109.7 15.0 %collective-permute-start.29 = (bf16[4,96,768]{2,1,0:T(8,128)(2,1)}, bf16[4,96,768]{2,1,0:T(8,128)(2,1)S(1)}, u32[]{:S(2)}, u32[]{:S(2)}) collective-permute-start(bf16[4,96,768]{2,1,0:T(8,128)(2,1)} %get-tuple-element.189), channel_id=1, source_target_pairs={{0,1},{1,0},{2,3},{3,2},{4,5},{5,4},{6,7},{7,6},{8,9},{9,8},{10,11... | collective-permute-start | bytes 1769480 | tf_op jit(solution)/shard_map/ppermute | solution.py:65
  115.4 31.5 %collective-permute-start.22 = (bf16[4,96,768]{2,1,0:T(8,128)(2,1)}, bf16[4,96,768]{2,1,0:T(8,128)(2,1)S(1)}, u32[]{:S(2)}, u32[]{:S(2)}) collective-permute-start(bf16[4,96,768]{2,1,0:T(8,128)(2,1)} %get-tuple-element.195), channel_id=1, source_target_pairs={{0,1},{1,0},{2,3},{3,2},{4,5},{5,4},{6,7},{7,6},{8,9},{9,8},{10,11... | collective-permute-start | bytes 1769480 | tf_op jit(solution)/shard_map/ppermute | solution.py:65
  115.7 15.7 %collective-permute-start.36 = (bf16[256,768]{1,0:T(8,128)(2,1)S(1)}, bf16[256,768]{1,0:T(8,128)(2,1)S(1)}, u32[]{:S(2)}, u32[]{:S(2)}) collective-permute-start(bf16[256,768]{1,0:T(8,128)(2,1)S(1)} %copy-done.57), channel_id=1, source_target_pairs={{0,8},{8,0},{1,9},{9,1},{2,10},{10,2},{3,11},{11,3},{4,12},{12,4},... | collective-permute-start | bytes 1179656 | tf_op jit(solution)/shard_map/ppermute | solution.py:65
  116.4 20.5 %collective-permute-start.37 = (bf16[256,768]{1,0:T(8,128)(2,1)S(1)}, bf16[256,768]{1,0:T(8,128)(2,1)S(1)}, u32[]{:S(2)}, u32[]{:S(2)}) collective-permute-start(bf16[256,768]{1,0:T(8,128)(2,1)S(1)} %add_convert_fusion.3), channel_id=1, source_target_pairs={{0,16},{16,0},{1,17},{17,1},{2,18},{18,2},{3,19},{19,3},{4,20},{20... | collective-permute-start | bytes 1179656 | tf_op jit(solution)/shard_map/ppermute | solution.py:65
  127.6 22.1 %collective-permute-start.30 = (bf16[96,768]{1,0:T(8,128)(2,1)}, bf16[96,768]{1,0:T(8,128)(2,1)S(1)}, u32[]{:S(2)}, u32[]{:S(2)}) collective-permute-start(bf16[96,768]{1,0:T(8,128)(2,1)} %get-tuple-element.211), channel_id=1, source_target_pairs={{0,2},{2,4},{4,6},{6,0},{1,3},{3,5},{5,7},{7,1},{8,10},{10,12},{12... | collective-permute-start | bytes 442376 | tf_op jit(solution)/shard_map/ppermute | solution.py:65
  130.7 20.4 %collective-permute-start.31 = (bf16[96,768]{1,0:T(8,128)(2,1)}, bf16[96,768]{1,0:T(8,128)(2,1)S(1)}, u32[]{:S(2)}, u32[]{:S(2)}) collective-permute-start(bf16[96,768]{1,0:T(8,128)(2,1)} %get-tuple-element.212), channel_id=1, source_target_pairs={{0,4},{2,6},{4,0},{6,2},{1,5},{3,7},{5,1},{7,3},{8,12},{10,14},{12... | collective-permute-start | bytes 442376 | tf_op jit(solution)/shard_map/ppermute | solution.py:65
  131.4 21.0 %collective-permute-start.32 = (bf16[96,768]{1,0:T(8,128)(2,1)}, bf16[96,768]{1,0:T(8,128)(2,1)S(1)}, u32[]{:S(2)}, u32[]{:S(2)}) collective-permute-start(bf16[96,768]{1,0:T(8,128)(2,1)} %get-tuple-element.213), channel_id=1, source_target_pairs={{0,6},{2,0},{4,2},{6,4},{1,7},{3,1},{5,3},{7,5},{8,14},{10,8},{12,... | collective-permute-start | bytes 442376 | tf_op jit(solution)/shard_map/ppermute | solution.py:65
  137.0 61.8 %collective-permute-start.19 = (bf16[256,768]{1,0:T(8,128)(2,1)}, bf16[256,768]{1,0:T(8,128)(2,1)S(1)}, u32[]{:S(2)}, u32[]{:S(2)}) collective-permute-start(bf16[256,768]{1,0:T(8,128)(2,1)} %get-tuple-element.201), channel_id=1, source_target_pairs={{0,8},{8,0},{1,9},{9,1},{2,10},{10,2},{3,11},{11,3},{4,12},{12,4},... | collective-permute-start | bytes 1179656 | tf_op jit(solution)/shard_map/ppermute | solution.py:65
  146.9 6.9 %collective-permute-start.38 = (bf16[256,192]{1,0:T(8,128)(2,1)}, bf16[256,192]{1,0:T(8,128)(2,1)S(1)}, u32[]{:S(2)}, u32[]{:S(2)}) collective-permute-start(bf16[256,192]{1,0:T(8,128)(2,1)} %get-tuple-element.228), channel_id=1, source_target_pairs={{0,2},{2,4},{4,6},{6,0},{1,3},{3,5},{5,7},{7,1},{8,10},{10,12},{12... | collective-permute-start | bytes 294920 | tf_op jit(solution)/shard_map/ppermute | solution.py:65
  149.8 11.0 %collective-permute-start.39 = (bf16[256,192]{1,0:T(8,128)(2,1)S(1)}, bf16[256,192]{1,0:T(8,128)(2,1)S(1)}, u32[]{:S(2)}, u32[]{:S(2)}) collective-permute-start(bf16[256,192]{1,0:T(8,128)(2,1)S(1)} %copy-done.66), channel_id=1, source_target_pairs={{0,4},{2,6},{4,0},{6,2},{1,5},{3,7},{5,1},{7,3},{8,12},{10,14},{12... | collective-permute-start | bytes 294920 | tf_op jit(solution)/shard_map/ppermute | solution.py:65
  151.1 9.7 %collective-permute-start.40 = (bf16[256,192]{1,0:T(8,128)(2,1)S(1)}, bf16[256,192]{1,0:T(8,128)(2,1)S(1)}, u32[]{:S(2)}, u32[]{:S(2)}) collective-permute-start(bf16[256,192]{1,0:T(8,128)(2,1)S(1)} %copy-done.64), channel_id=1, source_target_pairs={{0,6},{2,0},{4,2},{6,4},{1,7},{3,1},{5,3},{7,5},{8,14},{10,8},{12,... | collective-permute-start | bytes 294920 | tf_op jit(solution)/shard_map/ppermute | solution.py:65
  152.4 49.3 %collective-permute-start.44 = (bf16[768,384]{1,0:T(8,128)(2,1)S(1)}, bf16[768,384]{1,0:T(8,128)(2,1)S(1)}, u32[]{:S(2)}, u32[]{:S(2)}) collective-permute-start(bf16[768,384]{1,0:T(8,128)(2,1)S(1)} %copy-done.55), channel_id=1, source_target_pairs={{0,8},{8,0},{1,9},{9,1},{2,10},{10,2},{3,11},{11,3},{4,12},{12,4},... | collective-permute-start | bytes 1769480 | tf_op jit(solution)/shard_map/ppermute | solution.py:65
  153.8 28.3 %collective-permute-start.23 = (bf16[96,768]{1,0:T(8,128)(2,1)}, bf16[96,768]{1,0:T(8,128)(2,1)S(1)}, u32[]{:S(2)}, u32[]{:S(2)}) collective-permute-start(bf16[96,768]{1,0:T(8,128)(2,1)} %get-tuple-element.207), channel_id=1, source_target_pairs={{0,2},{2,4},{4,6},{6,0},{1,3},{3,5},{5,7},{7,1},{8,10},{10,12},{12... | collective-permute-start | bytes 442376 | tf_op jit(solution)/shard_map/ppermute | solution.py:65
  160.8 21.2 %collective-permute-start.24 = (bf16[96,768]{1,0:T(8,128)(2,1)}, bf16[96,768]{1,0:T(8,128)(2,1)S(1)}, u32[]{:S(2)}, u32[]{:S(2)}) collective-permute-start(bf16[96,768]{1,0:T(8,128)(2,1)} %get-tuple-element.208), channel_id=1, source_target_pairs={{0,4},{2,6},{4,0},{6,2},{1,5},{3,7},{5,1},{7,3},{8,12},{10,14},{12... | collective-permute-start | bytes 442376 | tf_op jit(solution)/shard_map/ppermute | solution.py:65
  160.8 21.2 %collective-permute-start.25 = (bf16[96,768]{1,0:T(8,128)(2,1)}, bf16[96,768]{1,0:T(8,128)(2,1)S(1)}, u32[]{:S(2)}, u32[]{:S(2)}) collective-permute-start(bf16[96,768]{1,0:T(8,128)(2,1)} %get-tuple-element.209), channel_id=1, source_target_pairs={{0,6},{2,0},{4,2},{6,4},{1,7},{3,1},{5,3},{7,5},{8,14},{10,8},{12,... | collective-permute-start | bytes 442376 | tf_op jit(solution)/shard_map/ppermute | solution.py:65
  182.2 73.6 %all-to-all-start = ((bf16[8,128,768]{2,1,0:T(8,128)(2,1)}), bf16[8,128,768]{2,1,0:T(8,128)(2,1)S(1)}, u32[]{:S(2)}, u32[]{:S(2)}) async-start(bf16[8,128,768]{2,1,0:T(8,128)(2,1)} %get-tuple-element.236), calls=%async_computation | async-start | bytes 3145728 | tf_op jit(solution)/shard_map/all_to_all | solution.py:994
  192.3 6.1 %collective-permute-start.46 = (f32[8,1248]{1,0:T(8,128)S(1)}, f32[8,1248]{1,0:T(8,128)S(1)}, u32[]{:S(2)}, u32[]{:S(2)}) collective-permute-start(f32[8,1248]{1,0:T(8,128)S(1)} %concatenate.12), channel_id=1, source_target_pairs={{0,8},{8,0},{1,9},{9,1},{2,10},{10,2},{3,11},{11,3},{4,12},{12,4},... | collective-permute-start | bytes 119816 | tf_op jit(solution)/shard_map/ppermute | solution.py:65
  193.5 34.9 %collective-permute-start.18 = (bf16[256,768]{1,0:T(8,128)(2,1)}, bf16[256,768]{1,0:T(8,128)(2,1)S(1)}, u32[]{:S(2)}, u32[]{:S(2)}) collective-permute-start(bf16[256,768]{1,0:T(8,128)(2,1)} %get-tuple-element.199), channel_id=1, source_target_pairs={{0,8},{8,0},{1,9},{9,1},{2,10},{10,2},{3,11},{11,3},{4,12},{12,4},... | collective-permute-start | bytes 1179656 | tf_op jit(solution)/shard_map/ppermute | solution.py:65
  198.9 29.5 %collective-permute-start.20 = (bf16[256,768]{1,0:T(8,128)(2,1)S(1)}, bf16[256,768]{1,0:T(8,128)(2,1)S(1)}, u32[]{:S(2)}, u32[]{:S(2)}) collective-permute-start(bf16[256,768]{1,0:T(8,128)(2,1)S(1)} %add_convert_fusion.2), channel_id=1, source_target_pairs={{0,16},{16,0},{1,17},{17,1},{2,18},{18,2},{3,19},{19,3},{4,20},{20... | collective-permute-start | bytes 1179656 | tf_op jit(solution)/shard_map/ppermute | solution.py:65
  202.7 13.7 %collective-permute-start.45 = (bf16[8,48,384]{2,1,0:T(8,128)(2,1)S(1)}, bf16[8,48,384]{2,1,0:T(8,128)(2,1)S(1)}, u32[]{:S(2)}, u32[]{:S(2)}) collective-permute-start(bf16[8,48,384]{2,1,0:T(8,128)(2,1)S(1)} %get-tuple-element.270), channel_id=1, source_target_pairs={{0,16},{16,0},{1,17},{17,1},{2,18},{18,2},{3,19},{19,3},{4,20},{20... | collective-permute-start | bytes 884744 | tf_op jit(solution)/shard_map/ppermute | solution.py:65
  203.9 18.8 %collective-permute-start.43 = (bf16[8,48,384]{2,1,0:T(8,128)(2,1)S(1)}, bf16[8,48,384]{2,1,0:T(8,128)(2,1)S(1)}, u32[]{:S(2)}, u32[]{:S(2)}) collective-permute-start(bf16[8,48,384]{2,1,0:T(8,128)(2,1)S(1)} %get-tuple-element.272), channel_id=1, source_target_pairs={{0,16},{16,0},{1,17},{17,1},{2,18},{18,2},{3,19},{19,3},{4,20},{20... | collective-permute-start | bytes 884744 | tf_op jit(solution)/shard_map/ppermute | solution.py:65
  225.7 16.8 %collective-permute-start.48 = (bf16[4,112,384]{2,1,0:T(8,128)(2,1)}, bf16[4,112,384]{2,1,0:T(8,128)(2,1)S(1)}, u32[]{:S(2)}, u32[]{:S(2)}) collective-permute-start(bf16[4,112,384]{2,1,0:T(8,128)(2,1)} %get-tuple-element.250), channel_id=1, source_target_pairs={{0,1},{1,0},{2,3},{3,2},{4,5},{5,4},{6,7},{7,6},{8,9},{9,8},{10,11... | collective-permute-start | bytes 1032200 | tf_op jit(solution)/shard_map/ppermute | solution.py:65
  227.4 8.8 %collective-permute-start.33 = (bf16[96,768]{1,0:T(8,128)(2,1)S(1)}, bf16[96,768]{1,0:T(8,128)(2,1)S(1)}, u32[]{:S(2)}, u32[]{:S(2)}) collective-permute-start(bf16[96,768]{1,0:T(8,128)(2,1)S(1)} %add_convert_fusion.4.refs_4_), channel_id=1, source_target_pairs={{0,16},{16,0},{1,17},{17,1},{2,18},{18,2},{3,19},{19,3},{4,20},{20... | collective-permute-start | bytes 442376 | tf_op jit(solution)/shard_map/ppermute | solution.py:65
  232.4 20.3 %collective-permute-start.21 = (f32[128,768]{1,0:T(8,128)}, f32[128,768]{1,0:T(8,128)S(1)}, u32[]{:S(2)}, u32[]{:S(2)}) collective-permute-start(f32[128,768]{1,0:T(8,128)} %get-tuple-element.205), channel_id=1, source_target_pairs={{0,1},{1,0},{2,3},{3,2},{4,5},{5,4},{6,7},{7,6},{8,9},{9,8},{10,11... | collective-permute-start | bytes 1179656 | tf_op jit(solution)/shard_map/ppermute | solution.py:65
  232.4 23.3 %collective-permute-start.41 = (f32[128,768]{1,0:T(8,128)S(1)}, f32[128,768]{1,0:T(8,128)S(1)}, u32[]{:S(2)}, u32[]{:S(2)}) collective-permute-start(f32[128,768]{1,0:T(8,128)S(1)} %copy-done.56), channel_id=1, source_target_pairs={{0,1},{1,0},{2,3},{3,2},{4,5},{5,4},{6,7},{7,6},{8,9},{9,8},{10,11... | collective-permute-start | bytes 1179656 | tf_op jit(solution)/shard_map/ppermute | solution.py:65
  237.2 7.9 %collective-permute-start.27 = (bf16[96,768]{1,0:T(8,128)(2,1)S(1)}, bf16[96,768]{1,0:T(8,128)(2,1)S(1)}, u32[]{:S(2)}, u32[]{:S(2)}) collective-permute-start(bf16[96,768]{1,0:T(8,128)(2,1)S(1)} %add_convert_fusion.5.refs_0_), channel_id=1, source_target_pairs={{0,8},{8,0},{1,9},{9,1},{2,10},{10,2},{3,11},{11,3},{4,12},{12,4},... | collective-permute-start | bytes 442376 | tf_op jit(solution)/shard_map/ppermute | solution.py:65
  242.5 5.9 %collective-permute-start.28 = (bf16[96,768]{1,0:T(8,128)(2,1)S(1)}, bf16[96,768]{1,0:T(8,128)(2,1)S(1)}, u32[]{:S(2)}, u32[]{:S(2)}) collective-permute-start(bf16[96,768]{1,0:T(8,128)(2,1)S(1)} %collective-permute-done.26.refs_1_), channel_id=1, source_target_pairs={{0,8},{8,0},{1,9},{9,1},{2,10},{10,2},{3,11},{11,3},{4,12},{12,4},... | collective-permute-start | bytes 442376 | tf_op jit(solution)/shard_map/ppermute | solution.py:65
  245.0 15.3 %collective-permute-start.49 = (bf16[112,384]{1,0:T(8,128)(2,1)}, bf16[112,384]{1,0:T(8,128)(2,1)S(1)}, u32[]{:S(2)}, u32[]{:S(2)}) collective-permute-start(bf16[112,384]{1,0:T(8,128)(2,1)} %get-tuple-element.252), channel_id=1, source_target_pairs={{0,2},{2,4},{4,6},{6,0},{1,3},{3,5},{5,7},{7,1},{8,10},{10,12},{12... | collective-permute-start | bytes 258056 | tf_op jit(solution)/shard_map/ppermute | solution.py:65
  246.3 14.1 %collective-permute-start.50 = (bf16[112,384]{1,0:T(8,128)(2,1)}, bf16[112,384]{1,0:T(8,128)(2,1)S(1)}, u32[]{:S(2)}, u32[]{:S(2)}) collective-permute-start(bf16[112,384]{1,0:T(8,128)(2,1)} %get-tuple-element.253), channel_id=1, source_target_pairs={{0,4},{2,6},{4,0},{6,2},{1,5},{3,7},{5,1},{7,3},{8,12},{10,14},{12... | collective-permute-start | bytes 258056 | tf_op jit(solution)/shard_map/ppermute | solution.py:65
  248.4 12.0 %collective-permute-start.51 = (bf16[112,384]{1,0:T(8,128)(2,1)}, bf16[112,384]{1,0:T(8,128)(2,1)S(1)}, u32[]{:S(2)}, u32[]{:S(2)}) collective-permute-start(bf16[112,384]{1,0:T(8,128)(2,1)} %get-tuple-element.254), channel_id=1, source_target_pairs={{0,6},{2,0},{4,2},{6,4},{1,7},{3,1},{5,3},{7,5},{8,14},{10,8},{12,... | collective-permute-start | bytes 258056 | tf_op jit(solution)/shard_map/ppermute | solution.py:65
  262.7 5.5 %collective-permute-start.52 = (bf16[5,48,384]{2,1,0:T(8,128)(2,1)}, bf16[5,48,384]{2,1,0:T(8,128)(2,1)S(1)}, u32[]{:S(2)}, u32[]{:S(2)}) collective-permute-start(bf16[5,48,384]{2,1,0:T(8,128)(2,1)} %get-tuple-element.260.refs_0_), channel_id=1, source_target_pairs={{0,16},{16,0},{1,17},{17,1},{2,18},{18,2},{3,19},{19,3},{4,20},{20... | collective-permute-start | bytes 552968 | tf_op jit(solution)/shard_map/ppermute | solution.py:65
  263.4 7.2 %collective-permute-start.53 = (bf16[5,48,384]{2,1,0:T(8,128)(2,1)}, bf16[5,48,384]{2,1,0:T(8,128)(2,1)S(1)}, u32[]{:S(2)}, u32[]{:S(2)}) collective-permute-start(bf16[5,48,384]{2,1,0:T(8,128)(2,1)} %get-tuple-element.260.refs_0_), channel_id=1, source_target_pairs={{0,8},{8,0},{1,9},{9,1},{2,10},{10,2},{3,11},{11,3},{4,12},{12,4},... | collective-permute-start | bytes 552968 | tf_op jit(solution)/shard_map/ppermute | solution.py:65
  (77 other events, 683.8 us)
where the time goes:
time: 280 us; the launch traced here: 275 us
  Pallas kernels  104 us (37%)
  starting transfers between devices  72 us (26%)
  waiting for transfers between devices  71.3 us (25%)
  local copies, waits for them, and re-layouts  22.6 us (8%)
  other arithmetic  3.07 us (1%)
    pallas_call x24, Pallas kernels, whole_call(): pl.pallas_call(body, out_shape=shapes, in_specs=specs, out_specs=[pl.Bloc...  104 us
    ppermute x55, waiting for transfers between devices, shift(): lax.ppermute(value, axis, [(i, (i + step) % size) for i in range(size)])  71.3 us
    ppermute x55, starting transfers between devices, shift(): lax.ppermute(value, axis, [(i, (i + step) % size) for i in range(size)])  63 us
    unnamed x139, local copies, waits for them, and re-layouts  10.8 us
    all_to_all x1, starting transfers between devices, body(): dnorm = lax.all_to_all(after(fc_share, dnorm), CTX, 0, 0, tiled=True)  8.94 us
  transfers between devices with their start and end apart: 56, of which 15 were waited for; matrix products, arithmetic and copies ran while one was open for 5% of the time, Pallas kernels for 31%

commit v1 on v0

v1 whole, which is shorter than its diff:
```python
import functools
import math

import jax
import jax.numpy as jnp
from jax import lax
from jax.experimental import pallas as pl
from jax.experimental.pallas import tpu as pltpu
from jax.sharding import Mesh
from jax.sharding import PartitionSpec as P

HEADS = 12
SEQ_LEN = 2048
FAR = 1e30
F32 = jnp.float32
BF16 = jnp.bfloat16
GRP = ("gx", "core")
CTX = ("hg", "part")
VMEM_BYTES = 56 * 1024 * 1024


QUARTER, PART, CORE, GX, HG, ROW = range(6)


class Sizes:
    def __init__(self, rows, width, hidden, docs, n_ctx, n_grp):
        self.rows, self.width, self.hidden, self.docs = rows, width, hidden, docs
        self.n_ctx, self.n_grp = n_ctx, n_grp
        self.head = width // HEADS
        self.block = min(rows // 2, SEQ_LEN // n_ctx)
        self.parts = rows // self.block
        self.groups = n_ctx // self.parts
        self.grain = self.block // 4
        self.grains = rows // self.grain
        self.per = -(-HEADS // self.groups)
        self.used = self.per * self.head
        self.lanes = -(-((self.per + 1) * self.head) // 128) * 128
        self.span = n_ctx * self.block
        self.half = self.groups // 2
        self.tile = 256
        self.steps = self.span // self.tile
        self.gx = n_grp // 2
        self.scale = self.head ** (-0.5)
        band, share = width // n_ctx, hidden // (n_ctx * n_grp)
        self.aligned = band % 32 == 0 and share % 32 == 0 and share * n_ctx == width
        self.packed = band % (32 * self.gx // 2) == 0 and 3 * self.lanes == width


def peer(sz, quarter, at, sign):
    return (((quarter >> 1) + sign * (at >> 1)) % sz.half) * 2 + ((quarter + at) & 1)


def dot(a, b):
    return lax.dot_general(a, b, (((1,), (0,)), ((), ())), preferred_element_type=F32)


def dot_nt(a, b):
    return lax.dot_general(a, b, (((1,), (1,)), ((), ())), preferred_element_type=F32)


def dot_tn(a, b):
    return lax.dot_general(a, b, (((0,), (0,)), ((), ())), preferred_element_type=F32)


def dot_split(mask, value, transposed):
    high = value.astype(BF16)
    low = (value - high.astype(F32)).astype(BF16)
    mul = dot_tn if transposed else dot
    return mul(mask, high) + mul(mask, low)


def shift(value, axis, size, step):
    return lax.ppermute(value, axis, [(i, (i + step) % size) for i in range(size)])


def to_peer(sz, value, at):
    if at == 0:
        return value
    pairs = []
    for core in range(2):
        for hg in range(sz.groups):
            to = (hg // sz.half) * sz.half + (hg + at // 2) % sz.half
            pairs.append((core * sz.groups + hg, ((core + at) % 2) * sz.groups + to))
    return lax.ppermute(value, ("core", "hg"), pairs)


def owner_pairs(sz, t):
    pairs = []
    for core in range(2):
        for hg in range(sz.groups):
            for row in range(sz.parts):
                part = (row + t) % sz.parts
                to_hg = (part % 2) * sz.half + hg // 2
                to_row = (part // 2) * 2 + core
                to = ((hg % 2) * sz.groups + to_hg) * sz.parts + to_row
                pairs.append(((core * sz.groups + hg) * sz.parts + row, to))
    return pairs


def to_owner(sz, blocks):
    return [lax.ppermute(b, ("core",) + CTX, owner_pairs(sz, t)) for t, b in enumerate(blocks)]


def from_owner(sz, blocks):
    return [
        lax.ppermute(b, ("core",) + CTX, [(b_, a_) for a_, b_ in owner_pairs(sz, t)])
        for t, b in enumerate(blocks)
    ]


def cost(flops, *arrays):
    size = sum(math.prod(a.shape) * a.dtype.itemsize for a in arrays)
    return pl.CostEstimate(flops=int(flops), bytes_accessed=int(size), transcendentals=0)


def whole_call(body, outs, n_scalars, args, name, scratch=(), flops=0):
    shapes = [jax.ShapeDtypeStruct(s, t) for s, t in outs]
    specs = [pl.BlockSpec(memory_space=pltpu.SMEM)] * n_scalars
    specs += [pl.BlockSpec(memory_space=pltpu.VMEM)] * (len(args) - n_scalars)
    return pl.pallas_call(
        body,
        out_shape=shapes,
        in_specs=specs,
        out_specs=[pl.BlockSpec(memory_space=pltpu.VMEM)] * len(outs),
        scratch_shapes=list(scratch),
        compiler_params=pltpu.CompilerParams(vmem_limit_bytes=VMEM_BYTES),
        cost_estimate=cost(flops, *args, *shapes),
        name=name,
    )(*args)


def source_grain(sz, doc_ref, place):
    is_long = [(doc_ref[0, d] == sz.block).astype(jnp.int32) for d in range(sz.docs)]
    longs = sum(is_long)
    seen_long, seen_short, begin, source = 0, 0, 0, 0
    for d in range(sz.docs):
        count = doc_ref[0, d] // sz.grain
        first = jnp.where(is_long[d] == 1, 4 * seen_long, 4 * longs + seen_short)
        inside = (place >= first) & (place < first + count)
        source = source + jnp.where(inside, begin + place - first, 0)
        seen_long = seen_long + is_long[d]
        seen_short = seen_short + jnp.where(is_long[d] == 1, 0, count)
        begin = begin + count
    return source


def part_is_long(sz, doc_ref, part):
    longs = sum((doc_ref[0, d] == sz.block).astype(jnp.int32) for d in range(sz.docs))
    return part < longs


def sort_rows(sz, place, docs, tokens, cotangent):
    def body(place_ref, doc_ref, tok_ref, cot_ref, *outs):
        for t in range(sz.parts):
            for a in range(4):
                src = source_grain(sz, doc_ref, 4 * ((place_ref[ROW] + t) % sz.parts) + a)
                at = pl.ds(a * sz.grain, sz.grain)
                outs[t][at, :] = tok_ref[src]
                outs[sz.parts + t][at, :] = cot_ref[src]

    shape = (sz.grains, sz.grain, sz.width)
    out = whole_call(
        body,
        [((sz.block, sz.width), BF16)] * (2 * sz.parts),
        2,
        (place, docs, tokens.reshape(shape), cotangent.reshape(shape)),
        "sort_rows",
    )
    return out[: sz.parts], out[sz.parts :]


def block_rows(sz, place_ref, quarter, t):
    at = quarter * sz.parts + (place_ref[PART] - t) % sz.parts
    return pl.ds(pl.multiple_of(at * sz.block, sz.block), sz.block)


def normalize(x):
    center = x - jnp.mean(x, axis=-1, keepdims=True)
    spread = jnp.mean(center * center, axis=-1, keepdims=True)
    r = lax.rsqrt(spread + 1e-05)
    return center * r, r


def pair_masks(sz, step, long_part):
    keys = (step + 1) * sz.tile
    q_row = step * sz.tile + lax.broadcasted_iota(jnp.int32, (sz.tile, 1), 0)
    k_row = lax.broadcasted_iota(jnp.int32, (1, keys), 1)
    q_doc = jnp.where(long_part, 0, (q_row % sz.block) // sz.grain)
    k_doc = jnp.where(long_part, 0, (k_row % sz.block) // sz.grain)
    k_in = jnp.where(long_part, k_row % sz.block, k_row % sz.grain)
    first = (k_row < sz.block) & (k_in == 0)
    same = q_doc == k_doc
    visible = same & (k_row <= q_row)
    select = same & (k_row < q_row) & jnp.logical_not(first)
    return visible, select


def slot_mask(sz, slot):
    lane = lax.broadcasted_iota(jnp.int32, (1, sz.lanes), 1)
    return lane // sz.head == slot


def lower_mask(sz):
    row = lax.broadcasted_iota(jnp.int32, (sz.tile, sz.tile), 0)
    col = lax.broadcasted_iota(jnp.int32, (sz.tile, sz.tile), 1)
    return jnp.where(row > col, 1.0, 0.0).astype(BF16)


def penalty_of(sz, step, long_part, lower, q_slot, k, carry):
    visible, select = pair_masks(sz, step, long_part)
    positive = jnp.maximum(dot_nt(q_slot, k), 0.0)
    chosen = jnp.where(select, positive * positive * (1.0 / sz.block), 0.0)
    penalty = dot_split(lower, chosen, False) + carry
    return jnp.where(visible, penalty, FAR), chosen, positive, select


def attend_forward(sz, place, docs, chunks, gain, bias, w_sel, b_sel):
    lw = sz.lanes
    n = len(chunks)

    def body(place_ref, doc_ref, *refs):
        xs = refs[:n]
        gain_ref, bias_ref, w_ref, b_ref = refs[n : n + 4]
        qkv_ref, normed_ref, hat_ref, lse_ref, out_ref, carry_ref = refs[n + 4 : n + 10]
        att_refs = refs[n + 10 :]
        quarter = place_ref[QUARTER]
        long_part = part_is_long(sz, doc_ref, place_ref[PART])
        for i in range(n):
            hat, _ = normalize(xs[i][...].astype(F32))
            normed = (hat * gain_ref[...] + bias_ref[...]).astype(BF16)
            packed = (dot(normed, w_ref[...]) + b_ref[...]).astype(BF16)
            low = hat.astype(BF16)
            for t in range(sz.parts):
                at = block_rows(sz, place_ref, peer(sz, quarter, i, -1), t)
                here = slice(t * sz.block, (t + 1) * sz.block)
                hat_ref[at, :] = low[here]
                normed_ref[at, :] = normed[here]
                qkv_ref[at, :] = packed[here]
        lower = lower_mask(sz)
        lane = lax.broadcasted_iota(jnp.int32, (1, 128), 1)
        carry_ref[...] = jnp.zeros_like(carry_ref)
        for step in range(sz.steps):
            keys = (step + 1) * sz.tile
            rows = slice(step * sz.tile, keys)
            q = qkv_ref[rows, :lw] * sz.scale
            k = qkv_ref[:keys, lw : 2 * lw]
            v = qkv_ref[:keys, 2 * lw :]
            q_slot = jnp.where(slot_mask(sz, sz.per), q, 0)
            pen, chosen, _, _ = penalty_of(
                sz, step, long_part, lower, q_slot, k, carry_ref[step : step + 1, :keys]
            )
            if step + 1 < sz.steps:
                carry_ref[step + 1 : step + 2, :keys] = carry_ref[step : step + 1, :keys] + jnp.sum(
                    chosen, axis=0, keepdims=True
                )
            total = jnp.zeros((sz.tile, lw), F32)
            lse = jnp.zeros((sz.tile, 128), F32)
            for h in range(sz.per):
                mask = slot_mask(sz, h)
                logits = dot_nt(jnp.where(mask, q, 0), k) - pen
                top = jnp.max(logits, axis=1, keepdims=True)
                weights = jnp.exp(logits - top)
                weight = jnp.sum(weights, axis=1, keepdims=True)
                mixed = dot(weights.astype(BF16), v) / weight
                total = jnp.where(mask, mixed, total)
                lse = jnp.where(lane == h, top + jnp.log(weight), lse)
            out_ref[rows, :] = total
            lse_ref[rows, :] = lse
        for i in range(n):
            for t in range(sz.parts):
                at = block_rows(sz, place_ref, peer(sz, quarter, i, 1), t)
                att_refs[i][t * sz.block : (t + 1) * sz.block, :] = out_ref[at, : sz.used].astype(BF16)

    outs = [
        ((sz.span, 3 * lw), BF16),
        ((sz.span, sz.width), BF16),
        ((sz.span, sz.width), BF16),
        ((sz.span, 128), F32),
        ((sz.span, lw), F32),
        ((sz.steps, sz.span), F32),
    ] + [((sz.rows, sz.used), BF16)] * sz.groups
    out = whole_call(body, outs, 2, (place, docs, *chunks, gain, bias, w_sel, b_sel), "attend_forward", flops=9e9)
    return out[:6], out[6:]


def attend_backward(sz, place, docs, saved, w_sel, grads):
    lw = sz.lanes
    qkv, _, hat, lse, att, carry = saved

    def body(place_ref, doc_ref, qkv_ref, hat_ref, lse_ref, att_ref, carry_ref, w_ref, *refs):
        grad_refs = refs[: sz.groups]
        outs = refs[sz.groups :]
        dqkv_ref, sums_ref, lnsum_ref = outs[:3]
        dnorm_refs = outs[3 : 3 + sz.groups]
        dout, dk_sum, dv_sum, behind = outs[3 + sz.groups :]
        quarter = place_ref[QUARTER]
        long_part = part_is_long(sz, doc_ref, place_ref[PART])
        dout[...] = jnp.zeros_like(dout)
        for i in range(sz.groups):
            for t in range(sz.parts):
                at = block_rows(sz, place_ref, peer(sz, quarter, i, -1), t)
                dout[at, : sz.used] = grad_refs[i][t * sz.block : (t + 1) * sz.block, :]
        dk_sum[...] = jnp.zeros_like(dk_sum)
        dv_sum[...] = jnp.zeros_like(dv_sum)
        behind[...] = jnp.zeros_like(behind)
        lower = lower_mask(sz)
        for step in reversed(range(sz.steps)):
            keys = (step + 1) * sz.tile
            rows = slice(step * sz.tile, keys)
            q = qkv_ref[rows, :lw] * sz.scale
            k = qkv_ref[:keys, lw : 2 * lw]
            v = qkv_ref[:keys, 2 * lw :]
            d_rows = dout[rows, :]
            dot_rows = d_rows.astype(F32) * att_ref[rows, :]
            last = slot_mask(sz, sz.per)
            q_slot = jnp.where(last, q, 0)
            pen, _, positive, select = penalty_of(
                sz, step, long_part, lower, q_slot, k, carry_ref[step : step + 1, :keys]
            )
            dpen = jnp.zeros((sz.tile, keys), F32)
            dq = jnp.zeros((sz.tile, lw), F32)
            for h in range(sz.per):
                mask = slot_mask(sz, h)
                q_h = jnp.where(mask, q, 0)
                d_h = jnp.where(mask, d_rows, 0)
                probs = jnp.exp(dot_nt(q_h, k) - pen - lse_ref[rows, h : h + 1])
                delta = jnp.sum(jnp.where(mask, dot_rows, 0.0), axis=1, keepdims=True)
                ds = probs * (dot_nt(d_h, v) - delta)
                dpen = dpen - ds
                ds_low = ds.astype(BF16)
                dq = jnp.where(mask, dot(ds_low, k), dq)
                dk_sum[:keys, :] += dot_tn(ds_low, q_h)
                dv_sum[:keys, :] += dot_tn(probs.astype(BF16), d_h)
            dchosen = dot_split(lower, dpen, True) + behind[:1, :keys]
            behind[:1, :keys] += jnp.sum(dpen, axis=0, keepdims=True)
            ds_low = jnp.where(select, positive * dchosen * (2.0 / sz.block), 0.0).astype(BF16)
            dq = jnp.where(last, dot(ds_low, k), dq)
            dk_sum[:keys, :] += dot_tn(ds_low, q_slot)
            dqkv_ref[rows, :lw] = (dq * sz.scale).astype(BF16)
        dqkv_ref[:, lw : 2 * lw] = dk_sum[...].astype(BF16)
        dqkv_ref[:, 2 * lw :] = dv_sum[...].astype(BF16)
        sums_ref[...] = jnp.sum(dqkv_ref[...].astype(F32), axis=0, keepdims=True)
        gain_sum = jnp.zeros((1, sz.width), F32)
        bias_sum = jnp.zeros((1, sz.width), F32)
        for i in range(sz.groups):
            for t in range(sz.parts):
                at = block_rows(sz, place_ref, peer(sz, quarter, i, 1), t)
                dnorm = dot_nt(dqkv_ref[at, :], w_ref[...])
                dnorm_refs[i][t * sz.block : (t + 1) * sz.block, :] = dnorm.astype(BF16)
                bias_sum += jnp.sum(dnorm, axis=0, keepdims=True)
                gain_sum += jnp.sum(dnorm * hat_ref[at, :].astype(F32), axis=0, keepdims=True)
        lnsum_ref[0:1, :] = gain_sum
        lnsum_ref[1:2, :] = bias_sum

    outs = [((sz.span, 3 * lw), BF16), ((1, 3 * lw), F32), ((2, sz.width), F32)]
    outs += [((sz.rows, sz.width), BF16)] * sz.groups
    scratch = [
        pltpu.VMEM((sz.span, lw), BF16),
        pltpu.VMEM((sz.span, lw), F32),
        pltpu.VMEM((sz.span, lw), F32),
        pltpu.VMEM((8, sz.span), F32),
    ]
    out = whole_call(
        body, outs, 2, (place, docs, qkv, hat, lse, att, carry, w_sel, *grads), "attend_backward", scratch, 17e9
    )
    return out[0], out[1], out[2], out[3:]


def project_out(sz, place, att, tokens, out_weight, out_bias, gain, bias):
    def body(place_ref, *refs):
        att_refs = refs[: sz.groups]
        tok_ref, w_ref, b_ref, gain_ref, bias_ref, middle_ref, second_ref = refs[sz.groups :]
        total = tok_ref[...].astype(F32) + b_ref[...]
        for k in range(sz.groups):
            at = pl.multiple_of(peer(sz, place_ref[QUARTER], k, -1) * sz.used, 16)
            total += dot(att_refs[k][...], w_ref[pl.ds(at, sz.used), :])
        middle_ref[...] = total
        hat, _ = normalize(total)
        second_ref[...] = (hat * gain_ref[...] + bias_ref[...]).astype(BF16)

    outs = [((sz.rows, sz.width), F32), ((sz.rows, sz.width), BF16)]
    return whole_call(
        body, outs, 1, (place, *att, tokens, out_weight, out_bias, gain, bias), "project_out"
    )


def feed_forward(sz, second, cot, fc, fc_bias, proj, name):
    n = len(second)
    units = fc.shape[1]
    root = math.sqrt(2.0 / math.pi)

    def body(*refs):
        second_refs, cot_refs = refs[:n], refs[n : 2 * n]
        fc_ref, bias_ref, proj_ref = refs[2 * n : 2 * n + 3]
        outs = refs[2 * n + 3 :]
        act_refs, grad_refs, back_refs, sums_ref = outs[:n], outs[n : 2 * n], outs[2 * n : 3 * n], outs[3 * n]
        total = jnp.zeros((1, units), F32)
        for i in range(n):
            hidden = dot(second_refs[i][...], fc_ref[...]) + bias_ref[...]
            square = hidden * hidden
            t = jnp.tanh(root * (hidden + 0.044715 * hidden * square))
            half = 0.5 * (1.0 + t)
            act_refs[i][...] = (hidden * half).astype(BF16)
            slope = half + 0.5 * hidden * (1.0 - t * t) * (root * (1.0 + 3.0 * 0.044715 * square))
            grad = (dot_nt(cot_refs[i][...], proj_ref[...]) * slope).astype(BF16)
            grad_refs[i][...] = grad
            back_refs[i][...] = dot_nt(grad, fc_ref[...]).astype(BF16)
            total += jnp.sum(grad.astype(F32), axis=0, keepdims=True)
        sums_ref[...] = total

    outs = [((sz.rows, units), BF16)] * (2 * n) + [((sz.rows, sz.width), BF16)] * n + [((1, units), F32)]
    out = whole_call(body, outs, 0, (*second, *cot, fc, fc_bias, proj), name)
    return out[:n], out[n : 2 * n], out[2 * n : 3 * n], out[3 * n]


def middle_backward(sz, place, back, middle, cot, out_weight, gain):
    n_back = len(back)

    def body(place_ref, *refs):
        back_refs = refs[:n_back]
        cot_ref, middle_ref, w_ref, gain_ref, grad_ref, branch_ref, sums_ref = refs[n_back : n_back + 7]
        datt_refs = refs[n_back + 7 :]
        cot = cot_ref[...].astype(F32)
        e = back_refs[0][...].astype(F32)
        for ref in back_refs[1:]:
            e += ref[...].astype(F32)
        hat, r = normalize(middle_ref[...])
        eg = e * gain_ref[...]
        inner = eg - jnp.mean(eg, axis=-1, keepdims=True)
        inner -= hat * jnp.mean(eg * hat, axis=-1, keepdims=True)
        grad = cot + r * inner
        grad_ref[...] = grad
        branch = grad.astype(BF16)
        branch_ref[...] = branch
        for k in range(sz.groups):
            at = pl.multiple_of(peer(sz, place_ref[QUARTER], k, 1) * sz.used, 16)
            datt_refs[k][...] = dot_nt(branch, w_ref[pl.ds(at, sz.used), :]).astype(BF16)
        sums_ref[0:1, :] = jnp.sum(e * hat, axis=0, keepdims=True)
        sums_ref[1:2, :] = jnp.sum(e, axis=0, keepdims=True)
        sums_ref[2:3, :] = jnp.sum(branch.astype(F32), axis=0, keepdims=True)
        sums_ref[3:4, :] = jnp.sum(cot, axis=0, keepdims=True)

    outs = [((sz.rows, sz.width), F32), ((sz.rows, sz.width), BF16), ((4, sz.width), F32)]
    outs += [((sz.rows, sz.used), BF16)] * sz.groups
    out = whole_call(body, outs, 1, (place, *back, cot, middle, out_weight, gain), "middle_backward")
    return out[0], out[1], out[2], out[3:]


def feed_forward_weights(sz, place, second, grad_hidden, act, cot):
    n = len(second)
    width, units = sz.width, act[0].shape[1]
    band, share = width // sz.n_ctx, units // sz.n_ctx
    both = band * units // width + share

    if not sz.aligned:
        second, grad_hidden, act, cot = (jnp.concatenate(v, axis=0) for v in (second, grad_hidden, act, cot))
        d_fc = dot_tn(second, grad_hidden).astype(BF16).reshape(sz.groups, sz.parts, -1, width)
        d_proj = dot_tn(act, cot).astype(BF16).reshape(sz.groups, sz.parts, -1, width)
        total = jnp.roll(jnp.concatenate([d_fc, d_proj], axis=2), -place[ROW], axis=1)
        return [total[:, s] for s in range(sz.parts)]

    def body(place_ref, *refs):
        second_refs, grad_refs, act_refs, cot_refs = (refs[i * n : (i + 1) * n] for i in range(4))
        outs, held = refs[4 * n : -1], refs[-1]
        held[:width, :] = sum(dot_tn(x[...], g[...]) for x, g in zip(second_refs, grad_refs)).astype(BF16)
        held[width:, :] = sum(dot_tn(a[...], c[...]) for a, c in zip(act_refs, cot_refs)).astype(BF16)
        for s in range(sz.parts):
            for g in range(sz.groups):
                to = g * sz.parts + (place_ref[ROW] + s) % sz.parts
                outs[s][g, :band, :] = held[pl.ds(pl.multiple_of(to * band, 16), band), :]
                outs[s][g, band:, :] = held[pl.ds(pl.multiple_of(width + to * share, 16), share), :]

    return whole_call(
        body,
        [((sz.groups, both, width), BF16)] * sz.parts,
        1,
        (place, *second, *grad_hidden, *act, *cot),
        "feed_forward_weights",
        [pltpu.VMEM((width + units, width), BF16)],
    )


def feed_forward_out(sz, act, proj):
    n = len(act)

    def body(*refs):
        for i in range(n):
            refs[n + 1 + i][...] = dot(refs[i][...], refs[n][...]).astype(BF16)

    return whole_call(body, [((sz.rows, sz.width), BF16)] * n, 0, (*act, proj), "feed_forward_out")


def out_weights(sz, place, att, branch):
    half = sz.width // 2

    def body(place_ref, *refs):
        branch_ref, own_ref, other_ref = refs[sz.groups :]
        core = place_ref[CORE]
        for k in range(sz.groups):
            at = pl.multiple_of(peer(sz, place_ref[QUARTER], k, -1) * sz.used, 16)

            @pl.when(at < sz.width)
            def _():
                grad_w = dot_tn(refs[k][...], branch_ref[...]).astype(BF16)
                left, right = grad_w[:, :half], grad_w[:, half:]
                own_ref[pl.ds(at, sz.used), :] = jnp.where(core == 0, left, right)
                other_ref[pl.ds(at, sz.used), :] = jnp.where(core == 0, right, left)

    return whole_call(body, [((sz.width, half), BF16)] * 2, 1, (place, *att, branch), "out_weights")


def sum_arrays(sz, pieces, name):
    def body(*refs):
        refs[-1][...] = sum(r[...].astype(F32) for r in refs[:-1]).astype(BF16)

    return whole_call(body, [(pieces[0].shape, BF16)], 0, tuple(pieces), name)[0]


def sum_first(sz, value, name):
    def body(ref, out_ref):
        out_ref[...] = sum(ref[k].astype(F32) for k in range(value.shape[0])).astype(BF16)

    return whole_call(body, [(value.shape[1:], BF16)], 0, (value,), name)[0]


def pack_sums(sz, place, sel, out, tail):
    rows, lanes = sel[0].shape[1:]
    n_tail = tail.shape[1]
    full = rows + n_tail + rows // 2
    if not sz.packed:
        sel = sum(t.astype(F32) for t in sel).astype(BF16)
        out = sum(t.astype(F32) for t in out).astype(BF16)
        out = jnp.concatenate([out[:, : rows // 2], out[:, rows // 2 :]], axis=2)
        both = jnp.concatenate([sel, tail, out], axis=1).reshape((sz.groups, sz.parts, full, lanes))
        both = jnp.roll(both, (-place[HG], -place[ROW]), axis=(0, 1))
        return [both[:, s] for s in range(sz.parts)]
    n = len(sel)

    def body(place_ref, *refs):
        tail_ref, outs = refs[2 * n], refs[2 * n + 1 :]
        for k in range(sz.groups):
            for s in range(sz.parts):
                to = ((place_ref[HG] + k) % sz.groups) * sz.parts + (place_ref[ROW] + s) % sz.parts
                outs[s][k, :rows, :] = sum(r[to].astype(F32) for r in refs[:n]).astype(BF16)
                outs[s][k, rows : rows + n_tail, :] = tail_ref[to]
                total = sum(r[to].astype(F32) for r in refs[n : 2 * n]).astype(BF16)
                outs[s][k, rows + n_tail :, : lanes // 2] = total[: rows // 2]
                outs[s][k, rows + n_tail :, lanes // 2 :] = total[rows // 2 :]

    return whole_call(
        body, [((sz.groups, full, lanes), BF16)] * sz.parts, 1, (place, *sel, *out, tail), "pack_sums"
    )


def add_halves(value):
    half = value.shape[-2] // 2
    value = value.astype(F32)
    return value[..., :half, :] + value[..., half:, :]


def split_halves(value, axis):
    high = value.astype(BF16)
    return jnp.concatenate([high, (value - high.astype(F32)).astype(BF16)], axis=axis)


def sum_packed(sz, pieces, rows, n_tail):
    end = rows + n_tail
    if not sz.packed:
        total = sum(p.astype(F32) for p in pieces).astype(BF16)
        tail = split_halves(sum(add_halves(p[:, rows:end]) for p in pieces), 1)
        total = jnp.concatenate([total[:, :rows], tail, total[:, end:]], axis=1)
        return [total[k] for k in range(sz.groups)]
    n = len(pieces)

    def body(*refs):
        for k in range(sz.groups):
            out = refs[n + k]
            for cut in (slice(0, rows), slice(end, None)):
                out[cut, :] = sum(r[k, cut, :].astype(F32) for r in refs[:n]).astype(BF16)
            out[rows:end, :] = split_halves(sum(add_halves(r[k, rows:end, :]) for r in refs[:n]), 0)

    return whole_call(body, [(pieces[0].shape[1:], BF16)] * sz.groups, 0, tuple(pieces), "sum_packed")


def unpack_sums(sz, place, blocks, rows, n_tail):
    full, lanes = blocks[0].shape
    end = rows + n_tail
    if not sz.packed:
        got = jnp.stack(blocks)
        total = got.astype(F32).sum(axis=0).astype(BF16)
        sel = got[:, :rows].astype(F32)
        sel = sel[: sz.half] + sel[sz.half :]
        sel = jnp.roll(sel[::-1], place[HG] + 1, axis=0).astype(BF16).reshape(-1, lanes)
        tail = split_halves(add_halves(got[:, rows:end]).sum(axis=0), 0)
        return jnp.concatenate([sel, tail, total[end:]], axis=0)

    def body(place_ref, *refs):
        blocks, out_ref = refs[: sz.groups], refs[sz.groups]
        for k in range(sz.half):
            at = pl.multiple_of(((place_ref[HG] - k) % sz.half) * rows, 16)
            total = blocks[k][:rows, :].astype(F32) + blocks[k + sz.half][:rows, :].astype(F32)
            out_ref[pl.ds(at, rows), :] = total.astype(BF16)
        at = sz.half * rows
        out_ref[at : at + n_tail, :] = split_halves(sum(add_halves(r[rows:end, :]) for r in blocks), 0)
        out_ref[at + n_tail :, :] = sum(r[end:, :].astype(F32) for r in blocks).astype(BF16)

    shape = (sz.half * rows + full - rows, lanes)
    return whole_call(body, [(shape, BF16)], 1, (place, *blocks), "unpack_sums")[0]


def small_cuts(sz):
    band, units = sz.width // sz.n_ctx, sz.hidden // sz.n_ctx
    one = [(0, i * band, band) for i in range(6)]
    return one[:2] + [(1, 0, 3 * band)] + one[2:5] + [(1, 3 * band, units)] + one[5:]


def pack_vectors(sz, place, ln1, qkv, middle, fc_sums):
    band, units = sz.width // sz.n_ctx, sz.hidden // sz.n_ctx
    share = units // sz.n_grp
    w3 = 3 * sz.lanes
    lanes = w3

    if not sz.packed:
        hg, mine = place[QUARTER], place[GX] * 2 + place[CORE]
        placed = jnp.zeros((sz.groups, 1, w3), F32)
        placed = lax.dynamic_update_slice(placed, qkv[None], (hg, 0, 0))
        fc_placed = jnp.zeros((sz.n_ctx, sz.n_grp, share), F32)
        fc_placed = lax.dynamic_update_slice(fc_placed, sum(fc_sums).reshape(sz.n_ctx, 1, share), (0, mine, 0))
        vectors = [ln1[0], ln1[1], join_slots(sz, placed)[0], middle[2], middle[0], middle[1]]
        vectors += [fc_placed.reshape(-1), middle[3]]
        out = jnp.zeros((sz.n_ctx, 8, lanes), F32)
        for v, (row, at, n) in zip(vectors, small_cuts(sz)):
            out = out.at[:, row, at : at + n].set(v.reshape(sz.n_ctx, n))
        return split_halves(out, 1)

    def body(place_ref, ln1_ref, qkv_ref, mid_ref, *refs):
        out_ref, held, fc_held, whole = refs[len(fc_sums) :]
        hg, mine = place_ref[QUARTER], place_ref[GX] * 2 + place_ref[CORE]
        held[...] = jnp.zeros_like(held)
        for g in range(sz.groups):

            @pl.when(hg == g)
            def _():
                for third in range(3):
                    at = third * sz.width + g * sz.used
                    held[0:1, at : at + sz.used] = qkv_ref[:, third * sz.lanes : third * sz.lanes + sz.used]

        for third in range(3):
            at, base = third * sz.width, third * sz.lanes + sz.used
            held[0:1, at : at + sz.head] += qkv_ref[:, base : base + sz.head]
        fc = sum(r[...] for r in refs[: len(fc_sums)])
        fc_held[...] = jnp.zeros_like(fc_held)
        for q in range(sz.n_grp):

            @pl.when(mine == q)
            def _():
                for j in range(sz.n_ctx):
                    fc_held[j : j + 1, q * share : (q + 1) * share] = fc[:, j * share : (j + 1) * share]

        whole[...] = jnp.zeros_like(whole)
        for j in range(sz.n_ctx):
            cut = slice(j * band, (j + 1) * band)
            singles = [ln1_ref[0:1, cut], ln1_ref[1:2, cut], mid_ref[2:3, cut], mid_ref[0:1, cut]]
            singles += [mid_ref[1:2, cut], mid_ref[3:4, cut]]
            whole[j, 0:1, : 6 * band] = jnp.concatenate(singles, axis=1)
            seconds = [held[0:1, 3 * j * band : 3 * (j + 1) * band], fc_held[j : j + 1, :]]
            whole[j, 1:2, : 3 * band + units] = jnp.concatenate(seconds, axis=1)
            out_ref[j] = split_halves(whole[j], 0)

    return whole_call(
        body,
        [((sz.n_ctx, 16, lanes), BF16)],
        1,
        (place, ln1, qkv, middle, *fc_sums),
        "pack_vectors",
        [
            pltpu.VMEM((8, 3 * sz.width), F32),
            pltpu.VMEM((sz.n_ctx, units), F32),
            pltpu.VMEM((sz.n_ctx, 8, lanes), F32),
        ],
    )[0]


def join_shares(sz, place, shares):
    band, width = sz.width // sz.n_ctx, sz.width
    share = sz.hidden // (sz.n_ctx * sz.n_grp)
    n = sz.n_grp
    n_fc = shares[0].shape[0] - share

    def body(place_ref, *refs):
        fc_ref, proj_ref, held = refs[n:]
        core, gx = place_ref[CORE], place_ref[GX]
        for c in range(2):
            for k in range(sz.gx):
                held[((gx - k) % sz.gx) * 2 + (core + c) % 2] = refs[c * sz.gx + k][...]
        for j in range(sz.n_ctx):
            cut = slice(j * share, (j + 1) * share)
            fc_ref[:, j * share * n : (j + 1) * share * n] = jnp.concatenate(
                [held[q, :n_fc, cut].astype(F32) for q in range(n)], axis=1
            )
        for q in range(n):
            proj_ref[q * share : (q + 1) * share, :] = held[q, n_fc:, :].astype(F32)

    if not sz.aligned:
        held = order_grp(sz, place, shares).reshape((n,) + shares[0].shape)
        fc = held[:, :n_fc].reshape(n, band, sz.n_ctx, share)
        fc = fc.transpose(1, 2, 0, 3).reshape(band, sz.hidden)
        return fc, held[:, n_fc:].reshape(n * share, width)
    return whole_call(
        body,
        [((band, sz.hidden), F32), ((n * share, width), F32)],
        1,
        (place, *shares),
        "join_shares",
        [pltpu.VMEM((n,) + shares[0].shape, BF16)],
    )


def order_grp(sz, place, values):
    held = jnp.stack(values).reshape((2, sz.gx) + values[0].shape)
    held = jnp.roll(held[:, ::-1], place[GX] + 1, axis=1)
    return jnp.roll(held, place[CORE], axis=0).swapaxes(0, 1).astype(F32)


def qkv_weights(sz, normed, dqkv):
    band = sz.width // sz.n_ctx
    w3 = 3 * sz.lanes

    def body(normed_ref, dqkv_ref, out_ref):
        grad = dot_tn(normed_ref[...], dqkv_ref[...]).astype(BF16)
        for i in range(sz.n_ctx):
            out_ref[i] = grad[i * band : (i + 1) * band, :]

    if not sz.packed:
        return dot_tn(normed, dqkv).astype(BF16).reshape(sz.n_ctx, band, w3)
    return whole_call(body, [((sz.n_ctx, band, w3), BF16)], 0, (normed, dqkv), "qkv_weights")[0]


def join_heads(sz, place, pieces, rows, n_tail):
    lanes = pieces[0].shape[1]
    start = sz.half * rows
    end = start + n_tail
    half = sz.width // 2
    if not sz.packed:
        held = order_grp(sz, place, pieces)
        sel = held[:, :, :start].reshape(sz.gx, 2, sz.half, rows, lanes)
        sel = sel.transpose(2, 1, 0, 3, 4).reshape(sz.groups, sz.gx * rows, lanes)
        out = held[:, :, end:].reshape(sz.gx, 2, rows // 2, 2, half)
        out = out.transpose(0, 3, 2, 1, 4).reshape(sz.gx * rows, sz.width)
        small = add_halves(held[:, :, start:end]).sum(axis=(0, 1))
        return join_slots(sz, sel), out, *(small[row, at : at + n] for row, at, n in small_cuts(sz))

    def body(place_ref, *refs):
        sel_ref, out_ref = refs[sz.n_grp : sz.n_grp + 2]
        small_refs, held = refs[sz.n_grp + 2 : -1], refs[-1]
        core, gx = place_ref[CORE], place_ref[GX]
        small = sum(add_halves(r[start:end, :]) for r in refs[: sz.n_grp])
        for ref, (row, at, n) in zip(small_refs, small_cuts(sz)):
            ref[...] = small[row, at : at + n]
        for c in range(2):
            for k in range(sz.gx):
                held[((gx - k) % sz.gx) * 2 + (core + c) % 2] = refs[c * sz.gx + k][...]
        for x in range(sz.gx):
            at_rows = slice(x * rows, (x + 1) * rows)
            both = [
                held[2 * x + g % 2, (g // 2) * rows : (g // 2 + 1) * rows, :].astype(F32) for g in range(sz.groups)
            ]
            for third in range(3):
                at = third * sz.lanes
                own = jnp.concatenate([b[:, at : at + sz.used] for b in both], axis=1)[:, : sz.width]
                first = sum(b[:, at + sz.used : at + sz.used + sz.head] for b in both)
                rest = jnp.zeros((rows, sz.width - sz.head), F32)
                sel_ref[at_rows, third * sz.width : (third + 1) * sz.width] = own + jnp.concatenate(
                    [first, rest], axis=1
                )
            for c in range(2):
                piece = held[2 * x + c, end:, :].astype(F32)
                columns = slice(c * half, (c + 1) * half)
                out_ref[x * rows : x * rows + rows // 2, columns] = piece[:, :half]
                out_ref[x * rows + rows // 2 : (x + 1) * rows, columns] = piece[:, half:]

    return whole_call(
        body,
        [((sz.gx * rows, 3 * sz.width), F32), ((sz.gx * rows, sz.width), F32)]
        + [((n,), F32) for _, _, n in small_cuts(sz)],
        1,
        (place, *pieces),
        "join_heads",
        [pltpu.VMEM((sz.n_grp,) + pieces[0].shape, BF16)],
    )


def join_slots(sz, sel):
    n = sel.shape[1]
    thirds = sel.reshape(sz.groups, n, 3, sz.lanes)
    own = thirds[..., : sz.used].transpose(2, 1, 0, 3).reshape(3, n, sz.groups * sz.used)
    own = own[..., : sz.width]
    first = thirds[..., sz.used : sz.used + sz.head].sum(axis=0).transpose(1, 0, 2)
    own = own.at[:, :, : sz.head].add(first)
    return own.transpose(1, 0, 2).reshape(n, 3 * sz.width)


def finish_tokens(sz, dnorm, tokens, grad_middle, gain):
    n = len(dnorm)

    def body(*refs):
        tok_ref, grad_ref, gain_ref = refs[n : n + 3]
        outs = refs[n + 3 :]
        e = refs[0][...].astype(F32)
        for ref in refs[1:n]:
            e += ref[...].astype(F32)
        hat, r = normalize(tok_ref[...].astype(F32))
        eg = e * gain_ref[...]
        inner = eg - jnp.mean(eg, axis=-1, keepdims=True)
        inner -= hat * jnp.mean(eg * hat, axis=-1, keepdims=True)
        total = (grad_ref[...] + r * inner).astype(BF16)
        for t in range(sz.parts):
            outs[t][...] = total[t * sz.block : (t + 1) * sz.block]

    return whole_call(
        body,
        [((sz.block, sz.width), BF16)] * sz.parts,
        0,
        (*dnorm, tokens, grad_middle, gain),
        "finish_tokens",
    )


def finish_middle(sz, mixed, middle, proj_bias):
    n = len(mixed)

    def body(*refs):
        middle_ref, bias_ref = refs[n : n + 2]
        outs = refs[n + 2 :]
        total = middle_ref[...] + bias_ref[...]
        for ref in refs[:n]:
            total += ref[...].astype(F32)
        total = total.astype(BF16)
        for t in range(sz.parts):
            outs[t][...] = total[t * sz.block : (t + 1) * sz.block]

    return whole_call(
        body,
        [((sz.block, sz.width), BF16)] * sz.parts,
        0,
        (*mixed, middle, proj_bias),
        "finish_middle",
    )


def unsort_rows(sz, place, docs, blocks):
    def body(place_ref, doc_ref, *refs):
        out_ref = refs[-1]
        for t in range(sz.parts):
            for a in range(4):
                src = source_grain(sz, doc_ref, 4 * ((place_ref[ROW] + t) % sz.parts) + a)
                out_ref[src] = refs[t][pl.ds(a * sz.grain, sz.grain), :].astype(F32)

    out = whole_call(
        body,
        [((sz.grains, sz.grain, sz.width), F32)],
        2,
        (place, docs, *blocks),
        "unsort_rows",
    )
    return out[0].reshape(sz.rows, sz.width)


def gather_near(sz, block):
    return [block, shift(block, "core", 2, 1)]


def gather_far(sz, block, before):
    far = []
    for k in range(1, sz.gx):
        along = after(before, shift(block, "gx", sz.gx, k))
        far += [along, shift(along, "core", 2, 1)]
    return far


def return_rows(sz, near, far, later):
    terms = [near[0], shift(near[1], "core", 2, 1)]
    for k in range(1, sz.gx):
        mine, other = far[2 * k - 2 : 2 * k]
        mine = (mine.astype(F32) + shift(other, "core", 2, 1).astype(F32)).astype(BF16)
        mine, later = lax.optimization_barrier((mine, later))
        terms.append(shift(mine, "gx", sz.gx, -k))
    return terms, later


def all_grp(sz, value):
    along = [value] + [shift(value, "gx", sz.gx, k) for k in range(1, sz.gx)]
    return along + [shift(v, "core", 2, 1) for v in along]


def after(gate, value):
    return lax.optimization_barrier((gate, value))[1]


def head_columns(sz, weight, hg):
    lead = weight.shape[:-1]
    pieces = []
    for third in range(3):
        full = weight[..., third * sz.width : (third + 1) * sz.width]
        spare = sz.groups * sz.used - sz.width
        if spare:
            full = jnp.pad(full, [(0, 0)] * len(lead) + [(0, spare)])
        own = lax.dynamic_slice_in_dim(full, hg * sz.used, sz.used, axis=len(lead))
        first = full[..., : sz.head] if third < 2 else jnp.zeros(lead + (sz.head,), weight.dtype)
        rest = sz.lanes - sz.used - sz.head
        pieces += [own, first]
        if rest:
            pieces.append(jnp.zeros(lead + (rest,), weight.dtype))
    return jnp.concatenate(pieces, axis=-1)


def weight_shares(sz, place, qkv_weight, fc_weight, proj_weight):
    share = sz.hidden // (sz.n_ctx * sz.n_grp)
    units = sz.n_ctx * share
    if not sz.aligned:
        mine = place[GX] * 2 + place[CORE]
        w_sel = head_columns(sz, qkv_weight, place[QUARTER])
        fc = fc_weight.reshape(sz.width, sz.n_ctx, sz.n_grp, share)
        fc = lax.dynamic_index_in_dim(fc, mine, 2, keepdims=False).reshape(sz.width, units)
        proj = proj_weight.reshape(sz.n_ctx, sz.n_grp, share, sz.width)
        proj = lax.dynamic_index_in_dim(proj, mine, 1, keepdims=False).reshape(units, sz.width)
        return w_sel, fc, proj

    def body(place_ref, qkv_ref, fc_in, proj_in, sel_ref, fc_ref, proj_ref):
        hg, mine = place_ref[QUARTER], place_ref[GX] * 2 + place_ref[CORE]
        for third in range(3):
            to, base = third * sz.lanes, third * sz.width
            end = jnp.zeros((sz.width, sz.lanes - sz.used), BF16)
            if third < 2:
                end = qkv_ref[:, base : base + 128][:, : sz.head]
                if sz.lanes - sz.used > sz.head:
                    end = jnp.concatenate(
                        [end, jnp.zeros((sz.width, sz.lanes - sz.used - sz.head), BF16)], axis=1
                    )
            for g in range(sz.groups):

                @pl.when(hg == g)
                def _():
                    own = qkv_ref[:, base : base + sz.width][:, g * sz.used : (g + 1) * sz.used]
                    sel_ref[:, to : to + sz.lanes] = jnp.concatenate([own, end], axis=1)

        wide = share * sz.n_grp
        for q in range(sz.n_grp):

            @pl.when(mine == q)
            def _():
                fc_ref[...] = jnp.concatenate(
                    [
                        fc_in[:, j * wide : (j + 1) * wide][:, q * share : (q + 1) * share]
                        for j in range(sz.n_ctx)
                    ],
                    axis=1,
                )

        for j in range(sz.n_ctx):
            at = pl.multiple_of(j * wide + mine * share, 16)
            proj_ref[j * share : (j + 1) * share, :] = proj_in[pl.ds(at, share), :]

    return whole_call(
        body,
        [((sz.width, 3 * sz.lanes), BF16), ((sz.width, units), BF16), ((units, sz.width), BF16)],
        1,
        (place, qkv_weight, fc_weight, proj_weight),
        "weight_shares",
    )


def body(
    tokens,
    ln1_gain,
    ln1_bias,
    qkv_weight,
    qkv_bias,
    out_weight,
    out_bias,
    ln2_gain,
    ln2_bias,
    fc_weight,
    fc_bias,
    proj_weight,
    proj_bias,
    doc_blocks,
    cotangent,
):
    rows, width = tokens.shape
    hidden = fc_weight.shape[1]
    n_ctx = lax.axis_size("hg") * lax.axis_size("part")
    n_grp = lax.axis_size("gx") * 2
    sz = Sizes(rows, width, hidden, doc_blocks.shape[1], n_ctx, n_grp)
    hg, part = lax.axis_index("hg"), lax.axis_index("part")
    gx, core = lax.axis_index("gx"), lax.axis_index("core")
    quarter = hg % sz.half * 2 + core
    my_part = part // 2 * 2 + hg // sz.half
    place = jnp.stack([quarter, my_part, core, gx, hg, part]).astype(jnp.int32)
    mine = gx * 2 + core

    def vector(v):
        return v.astype(F32)[None, :]

    gain1, bias1 = vector(ln1_gain), vector(ln1_bias)
    gain2, bias2 = vector(ln2_gain), vector(ln2_bias)
    share = hidden // (n_ctx * n_grp)
    b_sel = head_columns(sz, vector(qkv_bias), quarter)
    fc_b = lax.dynamic_index_in_dim(
        vector(fc_bias).reshape(1, n_ctx, n_grp, share), mine, 2, keepdims=False
    ).reshape(1, n_ctx * share)
    spare = sz.groups * sz.used - sz.width
    w_out = jnp.pad(out_weight, ((0, spare), (0, 0))) if spare else out_weight

    tok_parts, cot_parts = sort_rows(sz, place, doc_blocks, tokens, cotangent)
    tok_rows = jnp.concatenate(to_owner(sz, tok_parts), axis=0)
    docs = jnp.where(core == part % 2, doc_blocks, shift(doc_blocks, "core", 2, 1))

    chunks = []
    for k in range(sz.half):
        block = to_peer(sz, tok_rows, 2 * k)
        chunks += [block, to_peer(sz, block, 1)]

    qkv_weight, fc_weight, proj_weight, cot_parts = after(
        tok_rows, (qkv_weight, fc_weight, proj_weight, cot_parts)
    )
    w_sel, fc, proj = weight_shares(sz, place, qkv_weight, fc_weight, proj_weight)
    cot_rows = jnp.concatenate(to_owner(sz, cot_parts), axis=0)
    cot_near = gather_near(sz, cot_rows)
    cot_along = [shift(cot_rows, "gx", sz.gx, k) for k in range(1, sz.gx)]

    chunks = after(cot_rows, chunks)
    saved, att_out = attend_forward(sz, place, docs, chunks, gain1, bias1, w_sel, b_sel)
    cot_far = [b for along in cot_along for b in (along, shift(along, "core", 2, 1))]
    att_out = after((cot_along, cot_near), att_out)
    att = [to_peer(sz, att_out[k], k) for k in range(sz.groups)]
    middle, second = project_out(
        sz, place, att, tok_rows, w_out, vector(out_bias), gain2, bias2
    )

    sec_near = gather_near(sz, second)
    act_n, gh_n, back_n, fc_sum_n = feed_forward(sz, sec_near, cot_near, fc, fc_b, proj, "feed_forward_near")
    mixed_n = feed_forward_out(sz, act_n, proj)
    sec_far = gather_far(sz, second, (back_n, mixed_n))
    act_f, gh_f, back_f, fc_sum_f = feed_forward(sz, sec_far, cot_far, fc, fc_b, proj, "feed_forward_far")
    back, act_f = return_rows(sz, back_n, back_f, act_f)
    ff_sent = feed_forward_weights(
        sz, place, sec_near + sec_far, gh_n + gh_f, act_n + act_f, cot_near + cot_far
    )
    mixed_f = feed_forward_out(sz, after(ff_sent, act_f), proj)
    back = after(mixed_f, back)
    grad_middle, branch, mid_sums, datt_out = middle_backward(
        sz, place, back, middle, cot_rows, w_out, gain2
    )
    datt = [to_peer(sz, datt_out[k], k) for k in range(sz.groups)]

    band = width // n_ctx
    half = width // 2
    n_rows = band // sz.gx
    ff_got = [shift(ff_sent[s], "part", sz.parts, s) for s in range(1, sz.parts)]
    mixed, _ = return_rows(sz, mixed_n, mixed_f, place)

    def over_gx(value):
        value = value.reshape(n_ctx, sz.gx, n_rows, value.shape[2])
        pieces = []
        for k in range(sz.gx):
            piece = lax.dynamic_index_in_dim(value, (gx + k) % sz.gx, 1, keepdims=False)
            pieces.append(shift(piece, "gx", sz.gx, k) if k else piece)
        return pieces

    own, other = out_weights(sz, place, att, branch)
    own = own.astype(F32) + shift(other, "core", 2, 1).astype(F32)
    out_terms = over_gx(own.astype(BF16).reshape(n_ctx, band, half))

    dqkv, qkv_sum, ln1_sums, dnorm_out = attend_backward(sz, place, docs, saved, w_sel, datt)
    dnorm = [dnorm_out[0], to_peer(sz, dnorm_out[1], 1)]
    for k in range(1, sz.half):
        both = dnorm_out[2 * k].astype(F32) + to_peer(sz, dnorm_out[2 * k + 1], 1).astype(F32)
        both = both.astype(BF16)
        dnorm.append(to_peer(sz, both, 2 * k))
    grad_parts = finish_tokens(sz, dnorm, tok_rows, grad_middle, gain1)
    grad_tokens = unsort_rows(sz, place, doc_blocks, from_owner(sz, grad_parts))

    out_parts = finish_middle(sz, after(dqkv, mixed), middle, vector(proj_bias))
    output = unsort_rows(sz, place, doc_blocks, from_owner(sz, out_parts))

    d_sel = qkv_weights(sz, saved[1], after((both, ff_got, mixed, own), dqkv))
    sel_terms = after(grad_parts, over_gx(d_sel))
    tail = pack_vectors(sz, place, ln1_sums, qkv_sum, mid_sums, [fc_sum_n, fc_sum_f])
    n_tail = tail.shape[1]
    pieces = pack_sums(sz, place, sel_terms, out_terms, tail)
    pieces = [pieces[0]] + [shift(pieces[s], "part", sz.parts, s) for s in range(1, sz.parts)]
    blocks = sum_packed(sz, pieces, n_rows, n_tail)
    blocks = [blocks[0]] + [shift(blocks[k], "hg", sz.groups, k) for k in range(1, sz.groups)]
    sums = unpack_sums(sz, place, blocks, n_rows, n_tail)
    grad_qkv, grad_out, *cuts = join_heads(sz, place, all_grp(sz, sums), n_rows, n_tail)

    ff_near = sum_arrays(sz, [ff_sent[0]] + after((d_sel, dnorm), ff_got), "sum_parts")
    ff_share = sum_first(sz, lax.all_to_all(ff_near, "hg", 0, 0, tiled=True), "sum_groups")
    grad_fc, grad_proj = join_shares(sz, place, all_grp(sz, ff_share))

    g_ln1_gain, g_ln1_bias, g_qkv_bias, g_out_bias, g_ln2_gain, g_ln2_bias, g_fc_bias, g_proj_bias = cuts
    return (
        output,
        grad_tokens,
        g_ln1_gain,
        g_ln1_bias,
        grad_qkv,
        g_qkv_bias,
        grad_out,
        g_out_bias,
        g_ln2_gain,
        g_ln2_bias,
        grad_fc,
        g_fc_bias,
        grad_proj,
        g_proj_bias,
    )


def solution(mesh):
    n_grp, n_ctx = mesh.devices.shape
    split = P(GRP + CTX, None)

    def run(tokens, *rest):
        rows = tokens.shape[0] // (n_grp * n_ctx)
        parts = rows // min(rows // 2, SEQ_LEN // n_ctx)
        fine = Mesh(mesh.devices.reshape(n_grp // 2, 2, n_ctx // parts, parts), GRP + CTX)
        each = jax.shard_map(
            body,
            mesh=fine,
            in_specs=(split,) + (P(),) * 12 + (P(GRP, None), split),
            out_specs=(
                split,
                split,
                P(CTX),
                P(CTX),
                P(CTX, None),
                P(CTX),
                P(CTX, None),
                P(CTX),
                P(CTX),
                P(CTX),
                P(CTX, None),
                P(CTX),
                P(CTX, None),
                P(CTX),
            ),
            check_vma=False,
        )
        return each(tokens, *rest)

    return run
```

time: 280 us -> 250 us (0.89)
  waiting for transfers between devices: 71.3 us -> 49.7 us
  starting transfers between devices: 72 us -> 61.7 us
  Pallas kernels: 104 us -> 110 us
    ppermute x55 -> x27, starting transfers between devices: 63 us -> 14.4 us  [shift(): lax.ppermute(value, axis, [(i, (i + step) % size) for i in range(size)])]
    ppermute x55 -> x27, waiting for transfers between devices: 71.3 us -> 25.6 us  [shift(): lax.ppermute(value, axis, [(i, (i + step) % size) for i in range(size)])]
    ppermute x0 -> x20, starting transfers between devices: none -> 43.7 us  [the longest x4 16.6 us: from_owner(): lax.ppermute(b, ('core',) + CTX, [(b_, a_) for a_, b_ in owner_pairs(sz,...]
    ppermute x0 -> x20, waiting for transfers between devices: none -> 21.4 us  [the longest x12 11.5 us: to_peer(): return lax.ppermute(value, ('core', 'hg'), pairs)]
    pallas_call x24 -> x25, Pallas kernels: 104 us -> 110 us  [whole_call(): pl.pallas_call(body, out_shape=shapes, in_specs=specs, out_specs=[pl.Bloc...]
    all_to_all x1, starting transfers between devices: 8.94 us -> 3.66 us  [body(): lax.all_to_all(ff_near, 'hg', 0, 0, tiled=True)]
    unnamed x139 -> x124, local copies, waits for them, and re-layouts: 10.8 us -> 12.3 us
  transfers between devices with their start and end apart: 56 -> 48, of which waited for: 15 -> 17; matrix products, arithmetic and copies ran while one was open for 5% -> 4% of each run, Pallas kernels for 31% -> 38%
where the time goes in v1:
time: 250 us; the launch traced here: 245 us
  Pallas kernels  110 us (44%)
  starting transfers between devices  61.7 us (25%)
  waiting for transfers between devices  49.7 us (20%)
  local copies, waits for them, and re-layouts  20.4 us (8%)
    pallas_call x25, Pallas kernels, whole_call(): pl.pallas_call(body, out_shape=shapes, in_specs=specs, out_specs=[pl.Bloc...  110 us
    ppermute x27, waiting for transfers between devices, shift(): lax.ppermute(value, axis, [(i, (i + step) % size) for i in range(size)])  25.6 us
    ppermute x4, starting transfers between devices, from_owner(): lax.ppermute(b, ('core',) + CTX, [(b_, a_) for a_, b_ in owner_pairs(sz,...  16.6 us
    ppermute x12, starting transfers between devices, to_peer(): return lax.ppermute(value, ('core', 'hg'), pairs)  15 us
    ppermute x27, starting transfers between devices, shift(): lax.ppermute(value, axis, [(i, (i + step) % size) for i in range(size)])  14.4 us
    unnamed x124, local copies, waits for them, and re-layouts  12.3 us
    ppermute x4, starting transfers between devices, to_owner(): lax.ppermute(b, ('core',) + CTX, owner_pairs(sz, t))  12 us
    ppermute x12, waiting for transfers between devices, to_peer(): return lax.ppermute(value, ('core', 'hg'), pairs)  11.5 us
  transfers between devices with their start and end apart: 48, of which 17 were waited for; matrix products, arithmetic and copies ran while one was open for 4% of the time, Pallas kernels for 38%

profile of v1, /device:TPU:1, one launch (start us, length us, event | category | flops | bytes accessed | tf_op | source)
XLA Modules:
  0.0 244.8 jit_solution(16334459032180972198)
XLA Ops:
  1.4 2.2 sort_rows.1
  3.6 4.5 %collective-permute-start.1 = (bf16[128,768]{1,0:T(8,128)(2,1)}, bf16[128,768]{1,0:T(8,128)(2,1)S(1)}, u32[]{:S(2)}, u32[]{:S(2)}) collective-permute-start(bf16[128,768]{1,0:T(8,128)(2,1)} %get-tuple-element.121), channel_id=1, source_target_pairs={{0,0},{1,4},{2,8},{3,12},{4,2},{5,6},{6,10},{7,14},{8,1},{9,5},{10... | collective-permute-start | bytes 589832 | tf_op jit(solution)/shard_map/ppermute | solution.py:101
  8.2 3.6 %collective-permute-start.2 = (bf16[128,768]{1,0:T(8,128)(2,1)}, bf16[128,768]{1,0:T(8,128)(2,1)S(1)}, u32[]{:S(2)}, u32[]{:S(2)}) collective-permute-start(bf16[128,768]{1,0:T(8,128)(2,1)} %get-tuple-element.122), channel_id=1, source_target_pairs={{0,4},{1,0},{2,12},{3,8},{4,6},{5,2},{6,14},{7,10},{8,5},{9,1},{10... | collective-permute-start | bytes 589832 | tf_op jit(solution)/shard_map/ppermute | solution.py:101
  13.3 2.7 %collective-permute-done.2 = bf16[128,768]{1,0:T(8,128)(2,1)S(1)} collective-permute-done((bf16[128,768]{1,0:T(8,128)(2,1)}, bf16[128,768]{1,0:T(8,128)(2,1)S(1)}, u32[]{:S(2)}, u32[]{:S(2)}) %collective-permute-start.2) | collective-permute-done | bytes 196640 | tf_op jit(solution)/shard_map/ppermute | solution.py:101
  16.1 4.5 %collective-permute-start.6 = (bf16[256,768]{1,0:T(8,128)(2,1)S(1)}, bf16[256,768]{1,0:T(8,128)(2,1)S(1)}, u32[]{:S(2)}, u32[]{:S(2)}) collective-permute-start(bf16[256,768]{1,0:T(8,128)(2,1)S(1)} %constant_dynamic-update-slice_fusion.refs_0_.refs_4_.refs_3_), channel_id=1, source_target_pairs={{0,2},{2,0},{4,6},{6,4},{8,10},{10,8},{12,14},{14,12},{1,3},{3,1},... | collective-permute-start | bytes 1179656 | tf_op jit(solution)/shard_map/ppermute | solution.py:84
  22.6 2.3 collective-permute-start.5
  25.0 2.0 collective-permute-start.3
  28.8 2.4 collective-permute-start.7
  31.8 8.2 %weight_shares.1 = (bf16[768,768]{1,0:T(8,128)(2,1)}, bf16[768,768]{1,0:T(8,128)(2,1)}, bf16[768,768]{1,0:T(8,128)(2,1)}) custom-call(s32[6]{0:T(128)} %stack.27.place_ref, bf16[768,2304]{1,0:T(8,128)(2,1)} %qkv_ref, bf16[768,3072]{1,0:T(8,128)(2,1)} %fc_in, bf16[3072,768]{1,0:T(8,128)(2,1)} %proj_in), custom_call_target="tpu_custom_call" | custom-call | bytes 16515096 | tf_op jit(solution)/shard_map/weight_shares/pallas_call | solution.py:120
  42.2 11.0 %attend_forward.1 = (bf16[1024,768]{1,0:T(8,128)(2,1)}, bf16[1024,768]{1,0:T(8,128)(2,1)}, bf16[1024,768]{1,0:T(8,128)(2,1)}, f32[1024,128]{1,0:T(8,128)}, f32[1...) custom-call(s32[6]{0:T(128)} %stack.27.place_ref, ...), custom_call_target="tpu_custom_call" | custom-call | flops 8999999488 | bytes 9462828 | tf_op jit(solution)/shard_map/attend_forward/pallas_call | solution.py:120
  58.6 3.2 %collective-permute-done.12.refs_3_ = bf16[256,192]{1,0:T(8,128)(2,1)S(1)} collective-permute-done((bf16[256,192]{1,0:T(8,128)(2,1)}, bf16[256,192]{1,0:T(8,128)(2,1)S(1)}, u32[]{:S(2)}, u32[]{:S(2)}) %collective-permute-start.12) | collective-permute-done | bytes 98336 | tf_op jit(solution)/shard_map/ppermute | solution.py:84
  62.5 3.2 %project_out.1 = (f32[256,768]{1,0:T(8,128)}, bf16[256,768]{1,0:T(8,128)(2,1)}) custom-call(s32[6]{0:T(128)} %stack.27.place_ref, bf16[256,192]{1,0:T(8,128)(2,1)} %get-tuple-element.144.refs_0_, bf16[256,192]{1,0:T(8,128)(2,1)} %copy-done.15, bf16[256,192]{1,0:T(8,128)(2,1)} %copy-done.16, bf16[256,192]{1,0:T(8,128)(2,1)} %copy-done.17, ...), custom_call_target="tpu_custom_call" | custom-call | bytes 3154968 | tf_op jit(solution)/shard_map/project_out/pallas_call | solution.py:120
  68.6 5.7 %feed_forward_near.1 = (bf16[256,768]{1,0:T(8,128)(2,1)}, bf16[256,768]{1,0:T(8,128)(2,1)}, bf16[256,768]{1,0:T(8,128)(2,1)}, bf16[256,768]{1,0:T(8,128)(2,1)}, ...) custom-call(bf16[256,768]{1,0:T(8,128)(2,1)} %get-tuple-element.148.refs_0_, ...), custom_call_target="tpu_custom_call" | custom-call | bytes 6297600 | tf_op jit(solution)/shard_map/feed_forward_near/pallas_call | solution.py:120
  74.3 3.3 %feed_forward_out.2 = (bf16[256,768]{1,0:T(8,128)(2,1)}, bf16[256,768]{1,0:T(8,128)(2,1)}) custom-call(bf16[256,768]{1,0:T(8,128)(2,1)} %get-tuple-element.153.refs_0_.refs_8_, bf16[256,768]{1,0:T(8,128)(2,1)} %get-tuple-element.154.refs_1_.refs_9_, bf16[768,768]{1,0:T(8,128)(2,1)} %get-tuple-element.150.refs_6_.refs_2_), custom_call_target="tpu_custom_call" | custom-call | bytes 2752512 | tf_op jit(solution)/shard_map/feed_forward_out/pallas_call | solution.py:120
  80.1 5.8 %feed_forward_far.1 = (bf16[256,768]{1,0:T(8,128)(2,1)}, bf16[256,768]{1,0:T(8,128)(2,1)}, bf16[256,768]{1,0:T(8,128)(2,1)}, bf16[256,768]{1,0:T(8,128)(2,1)}, b...) custom-call(bf16[256,768]{1,0:T(8,128)(2,1)} %copy-done.7, bf16[256,768]{1,0:T(8,128)(2,1)} %copy-done.9, ...), custom_call_target="tpu_custom_call" | custom-call | bytes 6297600 | tf_op jit(solution)/shard_map/feed_forward_far/pallas_call | solution.py:120
  89.9 7.3 %feed_forward_weights.1 = (bf16[4,192,768]{2,1,0:T(8,128)(2,1)}, bf16[4,192,768]{2,1,0:T(8,128)(2,1)}) custom-call(s32[6]{0:T(128)} %stack.27.place_ref, bf16[256,768]{1,0:T(8,128)(2,1)} %get-tuple-element.148.refs_0_, bf16[256,768]{1,0:T(8,128)(2,1)} %copy-done.6, bf16[256,768]{1,0:T(8,128)(2,1)} %copy-done.7, bf16[256,768]{1,0:T(8,128)(2,1)} %copy-done.9, ...), custom_call_target="tpu_custom_call" | custom-call | bytes 8650776 | tf_op jit(solution)/shard_map/feed_forward_weights/pallas_call | solution.py:120
  97.2 3.1 %feed_forward_out.3 = (bf16[256,768]{1,0:T(8,128)(2,1)}, bf16[256,768]{1,0:T(8,128)(2,1)}) custom-call(bf16[256,768]{1,0:T(8,128)(2,1)} %get-tuple-element.170.refs_10_.refs_0_, bf16[256,768]{1,0:T(8,128)(2,1)} %get-tuple-element.171.refs_11_.refs_1_, bf16[768,768]{1,0:T(8,128)(2,1)} %get-tuple-element.150.refs_6_.refs_2_), custom_call_target="tpu_custom_call" | custom-call | bytes 2752512 | tf_op jit(solution)/shard_map/feed_forward_out/pallas_call | solution.py:120
  101.2 4.1 %middle_backward.1 = (f32[256,768]{1,0:T(8,128)}, bf16[256,768]{1,0:T(8,128)(2,1)}, f32[4,768]{1,0:T(4,128)}, bf16[256,192]{1,0:T(8,128)(2,1)}, bf16[256,192]{1,...) custom-call(s32[6]{0:T(128)} %stack.27.place_ref, bf16[256,768]{1,0:T(8,128)(2,1)} %get-tuple-element.175.refs_0_, ...), custom_call_target="tpu_custom_call" | custom-call | bytes 5127192 | tf_op jit(solution)/shard_map/middle_backward/pallas_call | solution.py:120
  107.6 3.4 %collective-permute-done.21.refs_2_ = bf16[256,192]{1,0:T(8,128)(2,1)S(1)} collective-permute-done((bf16[256,192]{1,0:T(8,128)(2,1)}, bf16[256,192]{1,0:T(8,128)(2,1)S(1)}, u32[]{:S(2)}, u32[]{:S(2)}) %collective-permute-start.21) | collective-permute-done | bytes 98336 | tf_op jit(solution)/shard_map/ppermute | solution.py:84
  111.0 3.3 %collective-permute-done.22.refs_3_ = bf16[256,192]{1,0:T(8,128)(2,1)S(1)} collective-permute-done((bf16[256,192]{1,0:T(8,128)(2,1)}, bf16[256,192]{1,0:T(8,128)(2,1)S(1)}, u32[]{:S(2)}, u32[]{:S(2)}) %collective-permute-start.22) | collective-permute-done | bytes 98336 | tf_op jit(solution)/shard_map/ppermute | solution.py:84
  114.9 18.6 %attend_backward.1 = (bf16[1024,768]{1,0:T(8,128)(2,1)}, f32[1,768]{1,0:T(1,128)}, f32[2,768]{1,0:T(2,128)}, bf16[256,768]{1,0:T(8,128)(2,1)}, bf16[256,768]{1,0...) custom-call(s32[6]{0:T(128)} %stack.27.place_ref, s32[1,5]{1,0:T(1,128)} %broadcast_select_fusion.doc_ref, ...), custom_call_target="tpu_custom_call" | custom-call | flops 16999999488 | bytes 9462828 | tf_op jit(solution)/shard_map/attend_backward/pallas_call | solution.py:120
  136.6 3.5 %out_weights.1 = (bf16[768,384]{1,0:T(8,128)(2,1)}, bf16[768,384]{1,0:T(8,128)(2,1)}) custom-call(s32[6]{0:T(128)} %stack.27.place_ref, bf16[256,192]{1,0:T(8,128)(2,1)} %get-tuple-element.144.refs_0_, bf16[256,192]{1,0:T(8,128)(2,1)} %copy-done.15, bf16[256,192]{1,0:T(8,128)(2,1)} %copy-done.16, bf16[256,192]{1,0:T(8,128)(2,1)} %copy-done.17, ...), custom_call_target="tpu_custom_call" | custom-call | bytes 1966104 | tf_op jit(solution)/shard_map/out_weights/pallas_call | solution.py:120
  140.6 4.4 %collective-permute-done.25.refs_2_ = bf16[256,768]{1,0:T(8,128)(2,1)S(1)} collective-permute-done((bf16[256,768]{1,0:T(8,128)(2,1)S(1)}, bf16[256,768]{1,0:T(8,128)(2,1)S(1)}, u32[]{:S(2)}, u32[]{:S(2)}) %collective-permute-start.25) | collective-permute-done | bytes 393248 | tf_op jit(solution)/shard_map/ppermute | solution.py:73
  145.0 4.9 %qkv_weights.1 = bf16[8,96,768]{2,1,0:T(8,128)(2,1)} custom-call(bf16[1024,768]{1,0:T(8,128)(2,1)} %get-tuple-element.197.normed_ref, bf16[1024,768]{1,0:T(8,128)(2,1)} %get-tuple-element.201.dqkv_ref), custom_call_target="tpu_custom_call" | custom-call | bytes 4325376 | tf_op jit(solution)/shard_map/qkv_weights/pallas_call | solution.py:120
  150.7 2.9 %sum_parts.1 = bf16[4,192,768]{2,1,0:T(8,128)(2,1)} custom-call(bf16[4,192,768]{2,1,0:T(8,128)(2,1)} %get-tuple-element.168.refs_0_, bf16[4,192,768]{2,1,0:T(8,128)(2,1)} %copy-done.10), custom_call_target="tpu_custom_call" | custom-call | bytes 3538944 | tf_op jit(solution)/shard_map/sum_parts/pallas_call | solution.py:120
  153.6 3.7 %all-to-all-start = ((bf16[4,192,768]{2,1,0:T(8,128)(2,1)}), bf16[4,192,768]{2,1,0:T(8,128)(2,1)S(1)}, u32[]{:S(2)}, u32[]{:S(2)}) async-start(bf16[4,192,768]{2,1,0:T(8,128)(2,1)} %sum_parts.1), calls=%async_computation | async-start | bytes 2359296 | tf_op jit(solution)/shard_map/all_to_all | solution.py:1099
  160.6 2.1 pack_vectors.1.refs_4_
  162.7 2.9 %finish_tokens.1 = (bf16[128,768]{1,0:T(8,128)(2,1)}, bf16[128,768]{1,0:T(8,128)(2,1)}) custom-call(bf16[256,768]{1,0:T(8,128)(2,1)} %get-tuple-element.190.refs_0_, bf16[256,768]{1,0:T(8,128)(2,1)} %copy-done.18, bf16[256,768]{1,0:T(8,128)(2,1)} %copy-done.19, bf16[256,768]{1,0:T(8,128)(2,1)} %copy-done.3, f32[256,768]{1,0:T(8,128)} %get-tuple-element.194.refs_4_, ...), custom_call_target="tpu_custom_call" | custom-call | bytes 2755584 | tf_op jit(solution)/shard_map/finish_tokens/pallas_call | solution.py:120
  165.6 6.6 %collective-permute-done.35.refs_1_ = bf16[8,48,768]{2,1,0:T(8,128)(2,1)S(1)} collective-permute-done((bf16[8,48,768]{2,1,0:T(8,128)(2,1)S(1)}, bf16[8,48,768]{2,1,0:T(8,128)(2,1)S(1)}, u32[]{:S(2)}, u32[]{:S(2)}) %collective-permute-start.35) | collective-permute-done | bytes 589856 | tf_op jit(solution)/shard_map/ppermute | solution.py:73
  172.2 6.3 %collective-permute-done.36.refs_3_ = bf16[8,48,384]{2,1,0:T(8,128)(2,1)S(1)} collective-permute-done((bf16[8,48,384]{2,1,0:T(8,128)(2,1)S(1)}, bf16[8,48,384]{2,1,0:T(8,128)(2,1)S(1)}, u32[]{:S(2)}, u32[]{:S(2)}) %collective-permute-start.36) | collective-permute-done | bytes 294944 | tf_op jit(solution)/shard_map/ppermute | solution.py:73
  179.3 2.7 %pack_sums.1 = (bf16[4,88,768]{2,1,0:T(8,128)(2,1)}, bf16[4,88,768]{2,1,0:T(8,128)(2,1)}) custom-call(s32[6]{0:T(128)} %stack.27.place_ref, bf16[8,48,768]{2,1,0:T(8,128)(2,1)} %get-tuple-element.202.refs_0_, bf16[8,48,768]{2,1,0:T(8,128)(2,1)} %copy-done.13, bf16[8,48,384]{2,1,0:T(8,128)(2,1)} %get-tuple-element.231.refs_2_, ...), custom_call_target="tpu_custom_call" | custom-call | bytes 3047448 | tf_op jit(solution)/shard_map/pack_sums/pallas_call | solution.py:120
  182.5 2.8 %all-to-all-done.ref = bf16[4,192,768]{2,1,0:T(8,128)(2,1)S(1)} async-done(((bf16[4,192,768]{2,1,0:T(8,128)(2,1)}), bf16[4,192,768]{2,1,0:T(8,128)(2,1)S(1)}, u32[]{:S(2)}, u32[]{:S(2)}) %all-to-all-start) | async-done | bytes 1179680 | tf_op jit(solution)/shard_map/all_to_all | solution.py:1099
  186.3 2.2 sum_groups.1.refs_0_
  189.0 5.1 %collective-permute-done.37.refs_1_ = bf16[4,88,768]{2,1,0:T(8,128)(2,1)S(1)} collective-permute-done((bf16[4,88,768]{2,1,0:T(8,128)(2,1)}, bf16[4,88,768]{2,1,0:T(8,128)(2,1)S(1)}, u32[]{:S(2)}, u32[]{:S(2)}) %collective-permute-start.37) | collective-permute-done | bytes 540704 | tf_op jit(solution)/shard_map/ppermute | solution.py:73
  194.9 2.0 sum_packed.1
  197.7 2.1 collective-permute-start.39
  201.6 2.4 finish_middle.1
  204.0 5.9 %collective-permute-start.26 = (bf16[128,768]{1,0:T(8,128)(2,1)}, bf16[128,768]{1,0:T(8,128)(2,1)S(1)}, u32[]{:S(2)}, u32[]{:S(2)}) collective-permute-start(bf16[128,768]{1,0:T(8,128)(2,1)} %get-tuple-element.188), channel_id=1, source_target_pairs={{0,0},{4,1},{8,2},{12,3},{2,4},{6,5},{10,6},{14,7},{1,8},{5,9},{9,... | collective-permute-start | bytes 589832 | tf_op jit(solution)/shard_map/ppermute | solution.py:106
  213.1 5.0 %collective-permute-start.27 = (bf16[128,768]{1,0:T(8,128)(2,1)}, bf16[128,768]{1,0:T(8,128)(2,1)S(1)}, u32[]{:S(2)}, u32[]{:S(2)}) collective-permute-start(bf16[128,768]{1,0:T(8,128)(2,1)} %get-tuple-element.189), channel_id=1, source_target_pairs={{4,0},{0,1},{12,2},{8,3},{6,4},{2,5},{14,6},{10,7},{5,8},{1,9},{13... | collective-permute-start | bytes 589832 | tf_op jit(solution)/shard_map/ppermute | solution.py:106
  218.1 1.9 collective-permute-start.31
  220.6 1.9 collective-permute-done.27.refs_1_
  223.0 2.0 collective-permute-done.31.refs_0_
  225.1 3.8 %collective-permute-start.32 = (bf16[128,768]{1,0:T(8,128)(2,1)S(1)}, bf16[128,768]{1,0:T(8,128)(2,1)S(1)}, u32[]{:S(2)}, u32[]{:S(2)}) collective-permute-start(bf16[128,768]{1,0:T(8,128)(2,1)S(1)} %copy-done.56), channel_id=1, source_target_pairs={{4,0},{0,1},{12,2},{8,3},{6,4},{2,5},{14,6},{10,7},{5,8},{1,9},{13... | collective-permute-start | bytes 589832 | tf_op jit(solution)/shard_map/ppermute | solution.py:106
  228.9 2.1 unsort_rows.2
  231.0 2.4 collective-permute-done.32.refs_1_
  234.1 2.1 unsort_rows.3
  237.6 2.5 %join_heads.1 = (f32[96,2304]{1,0:T(8,128)}, f32[96,768]{1,0:T(8,128)}, f32[96]{0:T(128)}, f32[96]{0:T(128)}, f32[288]{0:T(512)}, /*index=5*/f32[96]{0:T(128)}, ...) custom-call(s32[6]{0:T(128)} %stack.27.place_ref, bf16[136,768]{1,0:T(8,128)(2,1)} %unpack_sums.1.refs_0_, ...), custom_call_target="tpu_custom_call" | custom-call | bytes 2020248 | tf_op jit(solution)/shard_map/join_heads/pallas_call | solution.py:120
  241.5 3.1 %join_shares.1 = (f32[96,3072]{1,0:T(8,128)}, f32[384,768]{1,0:T(8,128)}) custom-call(s32[6]{0:T(128)} %stack.27.place_ref, bf16[192,768]{1,0:T(8,128)(2,1)} %sum_groups.1.refs_0_, bf16[192,768]{1,0:T(8,128)(2,1)} %copy-done.26, bf16[192,768]{1,0:T(8,128)(2,1)} %copy-done.27, bf16[192,768]{1,0:T(8,128)(2,1)} %copy-done.28), custom_call_target="tpu_custom_call" | custom-call | bytes 3538968 | tf_op jit(solution)/shard_map/join_shares/pallas_call | solution.py:120
  (223 shorter events, 49.8 us)
Async XLA Ops:
  0.7 30.6 %collective-permute-start = (s32[1,5]{1,0:T(1,128)}, s32[1,5]{1,0:T(1,128)S(1)}, u32[]{:S(2)}, u32[]{:S(2)}) collective-permute-start(s32[1,5]{1,0:T(1,128)} %doc_ref.5), channel_id=1, source_target_pairs={{0,8},{8,0},{1,9},{9,1},{2,10},{10,2},{3,11},{11,3},{4,12},{12,4},... | collective-permute-start | bytes 68 | tf_op jit(solution)/shard_map/ppermute | solution.py:73
  3.6 9.7 %collective-permute-start.1 = (bf16[128,768]{1,0:T(8,128)(2,1)}, bf16[128,768]{1,0:T(8,128)(2,1)S(1)}, u32[]{:S(2)}, u32[]{:S(2)}) collective-permute-start(bf16[128,768]{1,0:T(8,128)(2,1)} %get-tuple-element.121), channel_id=1, source_target_pairs={{0,0},{1,4},{2,8},{3,12},{4,2},{5,6},{6,10},{7,14},{8,1},{9,5},{10... | collective-permute-start | bytes 589832 | tf_op jit(solution)/shard_map/ppermute | solution.py:101
  8.2 7.9 %collective-permute-start.2 = (bf16[128,768]{1,0:T(8,128)(2,1)}, bf16[128,768]{1,0:T(8,128)(2,1)S(1)}, u32[]{:S(2)}, u32[]{:S(2)}) collective-permute-start(bf16[128,768]{1,0:T(8,128)(2,1)} %get-tuple-element.122), channel_id=1, source_target_pairs={{0,4},{1,0},{2,12},{3,8},{4,6},{5,2},{6,14},{7,10},{8,5},{9,1},{10... | collective-permute-start | bytes 589832 | tf_op jit(solution)/shard_map/ppermute | solution.py:101
  16.1 12.8 %collective-permute-start.6 = (bf16[256,768]{1,0:T(8,128)(2,1)S(1)}, bf16[256,768]{1,0:T(8,128)(2,1)S(1)}, u32[]{:S(2)}, u32[]{:S(2)}) collective-permute-start(bf16[256,768]{1,0:T(8,128)(2,1)S(1)} %constant_dynamic-update-slice_fusion.refs_0_.refs_4_.refs_3_), channel_id=1, source_target_pairs={{0,2},{2,0},{4,6},{6,4},{8,10},{10,8},{12,14},{14,12},{1,3},{3,1},... | collective-permute-start | bytes 1179656 | tf_op jit(solution)/shard_map/ppermute | solution.py:84
  22.6 18.7 %collective-permute-start.5 = (bf16[256,768]{1,0:T(8,128)(2,1)S(1)}, bf16[256,768]{1,0:T(8,128)(2,1)S(1)}, u32[]{:S(2)}, u32[]{:S(2)}) collective-permute-start(bf16[256,768]{1,0:T(8,128)(2,1)S(1)} %constant_dynamic-update-slice_fusion.refs_0_.refs_4_.refs_3_), channel_id=1, source_target_pairs={{0,8},{2,10},{4,12},{6,14},{8,0},{10,2},{12,4},{14,6},{1,9},{3,11}... | collective-permute-start | bytes 1179656 | tf_op jit(solution)/shard_map/ppermute | solution.py:84
  25.0 15.0 %collective-permute-start.3 = (bf16[128,768]{1,0:T(8,128)(2,1)}, bf16[128,768]{1,0:T(8,128)(2,1)S(1)}, u32[]{:S(2)}, u32[]{:S(2)}) collective-permute-start(bf16[128,768]{1,0:T(8,128)(2,1)} %get-tuple-element.125), channel_id=1, source_target_pairs={{0,0},{1,4},{2,8},{3,12},{4,2},{5,6},{6,10},{7,14},{8,1},{9,5},{10... | collective-permute-start | bytes 589832 | tf_op jit(solution)/shard_map/ppermute | solution.py:101
  27.0 13.0 %collective-permute-start.4 = (bf16[128,768]{1,0:T(8,128)(2,1)}, bf16[128,768]{1,0:T(8,128)(2,1)S(1)}, u32[]{:S(2)}, u32[]{:S(2)}) collective-permute-start(bf16[128,768]{1,0:T(8,128)(2,1)} %get-tuple-element.126), channel_id=1, source_target_pairs={{0,4},{1,0},{2,12},{3,8},{4,6},{5,2},{6,14},{7,10},{8,5},{9,1},{10... | collective-permute-start | bytes 589832 | tf_op jit(solution)/shard_map/ppermute | solution.py:101
  28.8 12.5 %collective-permute-start.7 = (bf16[256,768]{1,0:T(8,128)(2,1)S(1)}, bf16[256,768]{1,0:T(8,128)(2,1)S(1)}, u32[]{:S(2)}, u32[]{:S(2)}) collective-permute-start(bf16[256,768]{1,0:T(8,128)(2,1)S(1)} %collective-permute-done.6.refs_2_), channel_id=1, source_target_pairs={{0,8},{2,10},{4,12},{6,14},{8,0},{10,2},{12,4},{14,6},{1,9},{3,11}... | collective-permute-start | bytes 1179656 | tf_op jit(solution)/shard_map/ppermute | solution.py:84
  40.0 13.2 %collective-permute-start.8 = (bf16[256,768]{1,0:T(8,128)(2,1)S(1)}, bf16[256,768]{1,0:T(8,128)(2,1)S(1)}, u32[]{:S(2)}, u32[]{:S(2)}) collective-permute-start(bf16[256,768]{1,0:T(8,128)(2,1)S(1)} %constant_dynamic-update-slice_fusion.2.refs_2_.refs_12_.refs_3_), channel_id=1, source_target_pairs={{0,16},{16,0},{1,17},{17,1},{2,18},{18,2},{3,19},{19,3},{4,20},{20... | collective-permute-start | bytes 1179656 | tf_op jit(solution)/shard_map/ppermute | solution.py:73
  41.0 12.2 %collective-permute-start.9 = (bf16[256,768]{1,0:T(8,128)(2,1)S(1)}, bf16[256,768]{1,0:T(8,128)(2,1)S(1)}, u32[]{:S(2)}, u32[]{:S(2)}) collective-permute-start(bf16[256,768]{1,0:T(8,128)(2,1)S(1)} %constant_dynamic-update-slice_fusion.2.refs_2_.refs_12_.refs_3_), channel_id=1, source_target_pairs={{0,8},{8,0},{1,9},{9,1},{2,10},{10,2},{3,11},{11,3},{4,12},{12,4},... | collective-permute-start | bytes 1179656 | tf_op jit(solution)/shard_map/ppermute | solution.py:73
  53.3 4.0 %collective-permute-start.10 = (bf16[256,192]{1,0:T(8,128)(2,1)}, bf16[256,192]{1,0:T(8,128)(2,1)S(1)}, u32[]{:S(2)}, u32[]{:S(2)}) collective-permute-start(bf16[256,192]{1,0:T(8,128)(2,1)} %get-tuple-element.145), channel_id=1, source_target_pairs={{0,8},{2,10},{4,12},{6,14},{8,0},{10,2},{12,4},{14,6},{1,9},{3,11}... | collective-permute-start | bytes 294920 | tf_op jit(solution)/shard_map/ppermute | solution.py:84
  53.6 5.0 %collective-permute-start.11 = (bf16[256,192]{1,0:T(8,128)(2,1)}, bf16[256,192]{1,0:T(8,128)(2,1)S(1)}, u32[]{:S(2)}, u32[]{:S(2)}) collective-permute-start(bf16[256,192]{1,0:T(8,128)(2,1)} %get-tuple-element.146), channel_id=1, source_target_pairs={{0,2},{2,0},{4,6},{6,4},{8,10},{10,8},{12,14},{14,12},{1,3},{3,1},... | collective-permute-start | bytes 294920 | tf_op jit(solution)/shard_map/ppermute | solution.py:84
  54.5 7.3 %collective-permute-start.12 = (bf16[256,192]{1,0:T(8,128)(2,1)}, bf16[256,192]{1,0:T(8,128)(2,1)S(1)}, u32[]{:S(2)}, u32[]{:S(2)}) collective-permute-start(bf16[256,192]{1,0:T(8,128)(2,1)} %get-tuple-element.147), channel_id=1, source_target_pairs={{0,10},{2,8},{4,14},{6,12},{8,2},{10,0},{12,6},{14,4},{1,11},{3,9}... | collective-permute-start | bytes 294920 | tf_op jit(solution)/shard_map/ppermute | solution.py:84
  65.6 2.1 collective-permute-start.13
  65.6 11.9 %collective-permute-start.14 = (bf16[256,768]{1,0:T(8,128)(2,1)}, bf16[256,768]{1,0:T(8,128)(2,1)S(1)}, u32[]{:S(2)}, u32[]{:S(2)}) collective-permute-start(bf16[256,768]{1,0:T(8,128)(2,1)} %get-tuple-element.148.refs_0_), channel_id=1, source_target_pairs={{0,16},{16,0},{1,17},{17,1},{2,18},{18,2},{3,19},{19,3},{4,20},{20... | collective-permute-start | bytes 1179656 | tf_op jit(solution)/shard_map/ppermute | solution.py:73
  67.2 10.4 %collective-permute-start.16 = (bf16[256,768]{1,0:T(8,128)(2,1)S(1)}, bf16[256,768]{1,0:T(8,128)(2,1)S(1)}, u32[]{:S(2)}, u32[]{:S(2)}) collective-permute-start(bf16[256,768]{1,0:T(8,128)(2,1)S(1)} %collective-permute-done.8.refs_2_.refs_14_), channel_id=1, source_target_pairs={{0,8},{8,0},{1,9},{9,1},{2,10},{10,2},{3,11},{11,3},{4,12},{12,4},... | collective-permute-start | bytes 1179656 | tf_op jit(solution)/shard_map/ppermute | solution.py:73
  77.6 1.8 collective-permute-start.15
  85.9 1.9 collective-permute-start.17
  86.0 14.2 %collective-permute-start.18 = (bf16[256,768]{1,0:T(8,128)(2,1)S(1)}, bf16[256,768]{1,0:T(8,128)(2,1)S(1)}, u32[]{:S(2)}, u32[]{:S(2)}) collective-permute-start(bf16[256,768]{1,0:T(8,128)(2,1)S(1)} %copy-done.53), channel_id=1, source_target_pairs={{0,8},{8,0},{1,9},{9,1},{2,10},{10,2},{3,11},{11,3},{4,12},{12,4},... | collective-permute-start | bytes 1179656 | tf_op jit(solution)/shard_map/ppermute | solution.py:73
  88.9 11.4 %collective-permute-start.19 = (bf16[256,768]{1,0:T(8,128)(2,1)S(1)}, bf16[256,768]{1,0:T(8,128)(2,1)S(1)}, u32[]{:S(2)}, u32[]{:S(2)}) collective-permute-start(bf16[256,768]{1,0:T(8,128)(2,1)S(1)} %add_convert_fusion.2), channel_id=1, source_target_pairs={{0,16},{16,0},{1,17},{17,1},{2,18},{18,2},{3,19},{19,3},{4,20},{20... | collective-permute-start | bytes 1179656 | tf_op jit(solution)/shard_map/ppermute | solution.py:73
  105.2 2.3 collective-permute-start.20
  105.7 5.3 %collective-permute-start.21 = (bf16[256,192]{1,0:T(8,128)(2,1)}, bf16[256,192]{1,0:T(8,128)(2,1)S(1)}, u32[]{:S(2)}, u32[]{:S(2)}) collective-permute-start(bf16[256,192]{1,0:T(8,128)(2,1)} %get-tuple-element.181), channel_id=1, source_target_pairs={{0,2},{2,0},{4,6},{6,4},{8,10},{10,8},{12,14},{14,12},{1,3},{3,1},... | collective-permute-start | bytes 294920 | tf_op jit(solution)/shard_map/ppermute | solution.py:84
  106.6 7.6 %collective-permute-start.22 = (bf16[256,192]{1,0:T(8,128)(2,1)}, bf16[256,192]{1,0:T(8,128)(2,1)S(1)}, u32[]{:S(2)}, u32[]{:S(2)}) collective-permute-start(bf16[256,192]{1,0:T(8,128)(2,1)} %get-tuple-element.182), channel_id=1, source_target_pairs={{0,10},{2,8},{4,14},{6,12},{8,2},{10,0},{12,6},{14,4},{1,11},{3,9}... | collective-permute-start | bytes 294920 | tf_op jit(solution)/shard_map/ppermute | solution.py:84
  107.4 26.7 %collective-permute-start.24 = (bf16[256,768]{1,0:T(8,128)(2,1)S(1)}, bf16[256,768]{1,0:T(8,128)(2,1)S(1)}, u32[]{:S(2)}, u32[]{:S(2)}) collective-permute-start(bf16[256,768]{1,0:T(8,128)(2,1)S(1)} %copy-done.51), channel_id=1, source_target_pairs={{0,8},{8,0},{1,9},{9,1},{2,10},{10,2},{3,11},{11,3},{4,12},{12,4},... | collective-permute-start | bytes 1179656 | tf_op jit(solution)/shard_map/ppermute | solution.py:73
  107.6 37.4 %collective-permute-start.33 = (bf16[4,192,768]{2,1,0:T(8,128)(2,1)S(1)}, bf16[4,192,768]{2,1,0:T(8,128)(2,1)S(1)}, u32[]{:S(2)}, u32[]{:S(2)}) collective-permute-start(bf16[4,192,768]{2,1,0:T(8,128)(2,1)S(1)} %copy-done.48), channel_id=1, source_target_pairs={{0,1},{1,0},{2,3},{3,2},{4,5},{5,4},{6,7},{7,6},{8,9},{9,8},{10,11... | collective-permute-start | bytes 3538952 | tf_op jit(solution)/shard_map/ppermute | solution.py:73
  133.5 2.0 collective-permute-start.29
  133.6 6.5 %collective-permute-start.23 = (bf16[256,768]{1,0:T(8,128)(2,1)S(1)}, bf16[256,768]{1,0:T(8,128)(2,1)S(1)}, u32[]{:S(2)}, u32[]{:S(2)}) collective-permute-start(bf16[256,768]{1,0:T(8,128)(2,1)S(1)} %copy-done.49), channel_id=1, source_target_pairs={{0,8},{8,0},{1,9},{9,1},{2,10},{10,2},{3,11},{11,3},{4,12},{12,4},... | collective-permute-start | bytes 1179656 | tf_op jit(solution)/shard_map/ppermute | solution.py:73
  134.2 10.7 %collective-permute-start.25 = (bf16[256,768]{1,0:T(8,128)(2,1)S(1)}, bf16[256,768]{1,0:T(8,128)(2,1)S(1)}, u32[]{:S(2)}, u32[]{:S(2)}) collective-permute-start(bf16[256,768]{1,0:T(8,128)(2,1)S(1)} %add_convert_fusion.1), channel_id=1, source_target_pairs={{0,16},{16,0},{1,17},{17,1},{2,18},{18,2},{3,19},{19,3},{4,20},{20... | collective-permute-start | bytes 1179656 | tf_op jit(solution)/shard_map/ppermute | solution.py:73
  134.9 15.0 %collective-permute-start.28 = (bf16[256,768]{1,0:T(8,128)(2,1)S(1)}, bf16[256,768]{1,0:T(8,128)(2,1)S(1)}, u32[]{:S(2)}, u32[]{:S(2)}) collective-permute-start(bf16[256,768]{1,0:T(8,128)(2,1)S(1)} %copy-done.52), channel_id=1, source_target_pairs={{0,8},{2,10},{4,12},{6,14},{8,0},{10,2},{12,4},{14,6},{1,9},{3,11}... | collective-permute-start | bytes 1179656 | tf_op jit(solution)/shard_map/ppermute | solution.py:84
  135.6 14.3 %collective-permute-start.30 = (bf16[256,768]{1,0:T(8,128)(2,1)S(1)}, bf16[256,768]{1,0:T(8,128)(2,1)S(1)}, u32[]{:S(2)}, u32[]{:S(2)}) collective-permute-start(bf16[256,768]{1,0:T(8,128)(2,1)S(1)} %add_convert_fusion), channel_id=1, source_target_pairs={{0,2},{2,0},{4,6},{6,4},{8,10},{10,8},{12,14},{14,12},{1,3},{3,1},... | collective-permute-start | bytes 1179656 | tf_op jit(solution)/shard_map/ppermute | solution.py:84
  140.1 18.7 %collective-permute-start.34 = (bf16[768,384]{1,0:T(8,128)(2,1)}, bf16[768,384]{1,0:T(8,128)(2,1)S(1)}, u32[]{:S(2)}, u32[]{:S(2)}) collective-permute-start(bf16[768,384]{1,0:T(8,128)(2,1)} %get-tuple-element.200), channel_id=1, source_target_pairs={{0,8},{8,0},{1,9},{9,1},{2,10},{10,2},{3,11},{11,3},{4,12},{12,4},... | collective-permute-start | bytes 1769480 | tf_op jit(solution)/shard_map/ppermute | solution.py:73
  153.6 31.7 %all-to-all-start = ((bf16[4,192,768]{2,1,0:T(8,128)(2,1)}), bf16[4,192,768]{2,1,0:T(8,128)(2,1)S(1)}, u32[]{:S(2)}, u32[]{:S(2)}) async-start(bf16[4,192,768]{2,1,0:T(8,128)(2,1)} %sum_parts.1), calls=%async_computation | async-start | bytes 2359296 | tf_op jit(solution)/shard_map/all_to_all | solution.py:1099
  158.2 14.0 %collective-permute-start.35 = (bf16[8,48,768]{2,1,0:T(8,128)(2,1)S(1)}, bf16[8,48,768]{2,1,0:T(8,128)(2,1)S(1)}, u32[]{:S(2)}, u32[]{:S(2)}) collective-permute-start(bf16[8,48,768]{2,1,0:T(8,128)(2,1)S(1)} %get-tuple-element.228), channel_id=1, source_target_pairs={{0,16},{16,0},{1,17},{17,1},{2,18},{18,2},{3,19},{19,3},{4,20},{20... | collective-permute-start | bytes 1769480 | tf_op jit(solution)/shard_map/ppermute | solution.py:73
  159.7 18.8 %collective-permute-start.36 = (bf16[8,48,384]{2,1,0:T(8,128)(2,1)S(1)}, bf16[8,48,384]{2,1,0:T(8,128)(2,1)S(1)}, u32[]{:S(2)}, u32[]{:S(2)}) collective-permute-start(bf16[8,48,384]{2,1,0:T(8,128)(2,1)S(1)} %get-tuple-element.230), channel_id=1, source_target_pairs={{0,16},{16,0},{1,17},{17,1},{2,18},{18,2},{3,19},{19,3},{4,20},{20... | collective-permute-start | bytes 884744 | tf_op jit(solution)/shard_map/ppermute | solution.py:73
  181.9 12.2 %collective-permute-start.37 = (bf16[4,88,768]{2,1,0:T(8,128)(2,1)}, bf16[4,88,768]{2,1,0:T(8,128)(2,1)S(1)}, u32[]{:S(2)}, u32[]{:S(2)}) collective-permute-start(bf16[4,88,768]{2,1,0:T(8,128)(2,1)} %get-tuple-element.210), channel_id=1, source_target_pairs={{0,1},{1,0},{2,3},{3,2},{4,5},{5,4},{6,7},{7,6},{8,9},{9,8},{10,11... | collective-permute-start | bytes 1622024 | tf_op jit(solution)/shard_map/ppermute | solution.py:73
  188.5 31.7 %collective-permute-start.44 = (bf16[192,768]{1,0:T(8,128)(2,1)}, bf16[192,768]{1,0:T(8,128)(2,1)S(1)}, u32[]{:S(2)}, u32[]{:S(2)}) collective-permute-start(bf16[192,768]{1,0:T(8,128)(2,1)} %sum_groups.1.refs_0_), channel_id=1, source_target_pairs={{0,16},{16,0},{1,17},{17,1},{2,18},{18,2},{3,19},{19,3},{4,20},{20... | collective-permute-start | bytes 884744 | tf_op jit(solution)/shard_map/ppermute | solution.py:73
  197.0 12.9 %collective-permute-start.38 = (bf16[88,768]{1,0:T(8,128)(2,1)}, bf16[88,768]{1,0:T(8,128)(2,1)S(1)}, u32[]{:S(2)}, u32[]{:S(2)}) collective-permute-start(bf16[88,768]{1,0:T(8,128)(2,1)} %get-tuple-element.212), channel_id=1, source_target_pairs={{0,2},{2,4},{4,6},{6,0},{1,3},{3,5},{5,7},{7,1},{8,10},{10,12},{12... | collective-permute-start | bytes 405512 | tf_op jit(solution)/shard_map/ppermute | solution.py:73
  197.7 12.2 %collective-permute-start.39 = (bf16[88,768]{1,0:T(8,128)(2,1)}, bf16[88,768]{1,0:T(8,128)(2,1)S(1)}, u32[]{:S(2)}, u32[]{:S(2)}) collective-permute-start(bf16[88,768]{1,0:T(8,128)(2,1)} %get-tuple-element.213), channel_id=1, source_target_pairs={{0,4},{2,6},{4,0},{6,2},{1,5},{3,7},{5,1},{7,3},{8,12},{10,14},{12... | collective-permute-start | bytes 405512 | tf_op jit(solution)/shard_map/ppermute | solution.py:73
  199.8 10.1 %collective-permute-start.40 = (bf16[88,768]{1,0:T(8,128)(2,1)}, bf16[88,768]{1,0:T(8,128)(2,1)S(1)}, u32[]{:S(2)}, u32[]{:S(2)}) collective-permute-start(bf16[88,768]{1,0:T(8,128)(2,1)} %get-tuple-element.214), channel_id=1, source_target_pairs={{0,6},{2,0},{4,2},{6,4},{1,7},{3,1},{5,3},{7,5},{8,14},{10,8},{12,... | collective-permute-start | bytes 405512 | tf_op jit(solution)/shard_map/ppermute | solution.py:73
  204.0 16.0 %collective-permute-start.26 = (bf16[128,768]{1,0:T(8,128)(2,1)}, bf16[128,768]{1,0:T(8,128)(2,1)S(1)}, u32[]{:S(2)}, u32[]{:S(2)}) collective-permute-start(bf16[128,768]{1,0:T(8,128)(2,1)} %get-tuple-element.188), channel_id=1, source_target_pairs={{0,0},{4,1},{8,2},{12,3},{2,4},{6,5},{10,6},{14,7},{1,8},{5,9},{9,... | collective-permute-start | bytes 589832 | tf_op jit(solution)/shard_map/ppermute | solution.py:106
  212.5 10.3 %collective-permute-start.41 = (bf16[136,768]{1,0:T(8,128)(2,1)}, bf16[136,768]{1,0:T(8,128)(2,1)S(1)}, u32[]{:S(2)}, u32[]{:S(2)}) collective-permute-start(bf16[136,768]{1,0:T(8,128)(2,1)} %unpack_sums.1.refs_0_), channel_id=1, source_target_pairs={{0,16},{16,0},{1,17},{17,1},{2,18},{18,2},{3,19},{19,3},{4,20},{20... | collective-permute-start | bytes 626696 | tf_op jit(solution)/shard_map/ppermute | solution.py:73
  213.1 9.4 %collective-permute-start.27 = (bf16[128,768]{1,0:T(8,128)(2,1)}, bf16[128,768]{1,0:T(8,128)(2,1)S(1)}, u32[]{:S(2)}, u32[]{:S(2)}) collective-permute-start(bf16[128,768]{1,0:T(8,128)(2,1)} %get-tuple-element.189), channel_id=1, source_target_pairs={{4,0},{0,1},{12,2},{8,3},{6,4},{2,5},{14,6},{10,7},{5,8},{1,9},{13... | collective-permute-start | bytes 589832 | tf_op jit(solution)/shard_map/ppermute | solution.py:106
  218.1 7.0 %collective-permute-start.31 = (bf16[128,768]{1,0:T(8,128)(2,1)S(1)}, bf16[128,768]{1,0:T(8,128)(2,1)S(1)}, u32[]{:S(2)}, u32[]{:S(2)}) collective-permute-start(bf16[128,768]{1,0:T(8,128)(2,1)S(1)} %copy-done.57), channel_id=1, source_target_pairs={{0,0},{4,1},{8,2},{12,3},{2,4},{6,5},{10,6},{14,7},{1,8},{5,9},{9,... | collective-permute-start | bytes 589832 | tf_op jit(solution)/shard_map/ppermute | solution.py:106
  220.0 20.1 %collective-permute-start.45 = (bf16[192,768]{1,0:T(8,128)(2,1)S(1)}, bf16[192,768]{1,0:T(8,128)(2,1)S(1)}, u32[]{:S(2)}, u32[]{:S(2)}) collective-permute-start(bf16[192,768]{1,0:T(8,128)(2,1)S(1)} %copy-done.11), channel_id=1, source_target_pairs={{0,8},{8,0},{1,9},{9,1},{2,10},{10,2},{3,11},{11,3},{4,12},{12,4},... | collective-permute-start | bytes 884744 | tf_op jit(solution)/shard_map/ppermute | solution.py:73
  220.1 20.0 %collective-permute-start.46 = (bf16[192,768]{1,0:T(8,128)(2,1)S(1)}, bf16[192,768]{1,0:T(8,128)(2,1)S(1)}, u32[]{:S(2)}, u32[]{:S(2)}) collective-permute-start(bf16[192,768]{1,0:T(8,128)(2,1)S(1)} %collective-permute-done.44.refs_1_), channel_id=1, source_target_pairs={{0,8},{8,0},{1,9},{9,1},{2,10},{10,2},{3,11},{11,3},{4,12},{12,4},... | collective-permute-start | bytes 884744 | tf_op jit(solution)/shard_map/ppermute | solution.py:73
  222.5 13.7 %collective-permute-start.42 = (bf16[136,768]{1,0:T(8,128)(2,1)}, bf16[136,768]{1,0:T(8,128)(2,1)S(1)}, u32[]{:S(2)}, u32[]{:S(2)}) collective-permute-start(bf16[136,768]{1,0:T(8,128)(2,1)} %unpack_sums.1.refs_0_), channel_id=1, source_target_pairs={{0,8},{8,0},{1,9},{9,1},{2,10},{10,2},{3,11},{11,3},{4,12},{12,4},... | collective-permute-start | bytes 626696 | tf_op jit(solution)/shard_map/ppermute | solution.py:73
  222.8 13.4 %collective-permute-start.43 = (bf16[136,768]{1,0:T(8,128)(2,1)S(1)}, bf16[136,768]{1,0:T(8,128)(2,1)S(1)}, u32[]{:S(2)}, u32[]{:S(2)}) collective-permute-start(bf16[136,768]{1,0:T(8,128)(2,1)S(1)} %collective-permute-done.41.refs_1_), channel_id=1, source_target_pairs={{0,8},{8,0},{1,9},{9,1},{2,10},{10,2},{3,11},{11,3},{4,12},{12,4},... | collective-permute-start | bytes 626696 | tf_op jit(solution)/shard_map/ppermute | solution.py:73
  225.1 8.3 %collective-permute-start.32 = (bf16[128,768]{1,0:T(8,128)(2,1)S(1)}, bf16[128,768]{1,0:T(8,128)(2,1)S(1)}, u32[]{:S(2)}, u32[]{:S(2)}) collective-permute-start(bf16[128,768]{1,0:T(8,128)(2,1)S(1)} %copy-done.56), channel_id=1, source_target_pairs={{4,0},{0,1},{12,2},{8,3},{6,4},{2,5},{14,6},{10,7},{5,8},{1,9},{13... | collective-permute-start | bytes 589832 | tf_op jit(solution)/shard_map/ppermute | solution.py:106
  (61 other events, 473.9 us)

commit v2 on v1

--- a/solution.py
+++ b/solution.py
@@ -413,13 +413,16 @@
     return out[:n], out[n : 2 * n], out[2 * n : 3 * n], out[3 * n]
 
 
-def middle_backward(sz, place, back, middle, cot, out_weight, gain):
+def middle_backward(sz, place, back, middle, cot, out_weight, gain, att):
     n_back = len(back)
+    half = sz.width // 2
 
     def body(place_ref, *refs):
         back_refs = refs[:n_back]
-        cot_ref, middle_ref, w_ref, gain_ref, grad_ref, branch_ref, sums_ref = refs[n_back : n_back + 7]
-        datt_refs = refs[n_back + 7 :]
+        att_refs = refs[n_back : n_back + sz.groups]
+        rest = refs[n_back + sz.groups :]
+        cot_ref, middle_ref, w_ref, gain_ref, grad_ref, own_ref, other_ref, sums_ref = rest[:8]
+        datt_refs = rest[8:]
         cot = cot_ref[...].astype(F32)
         e = back_refs[0][...].astype(F32)
         for ref in back_refs[1:]:
@@ -431,7 +434,17 @@
         grad = cot + r * inner
         grad_ref[...] = grad
         branch = grad.astype(BF16)
-        branch_ref[...] = branch
+        core = place_ref[CORE]
+        for k in range(sz.groups):
+            at = pl.multiple_of(peer(sz, place_ref[QUARTER], k, -1) * sz.used, 16)
+
+            @pl.when(at < sz.width)
+            def _():
+                grad_w = dot_tn(att_refs[k][...], branch).astype(BF16)
+                left, right = grad_w[:, :half], grad_w[:, half:]
+                own_ref[pl.ds(at, sz.used), :] = jnp.where(core == 0, left, right)
+                other_ref[pl.ds(at, sz.used), :] = jnp.where(core == 0, right, left)
+
         for k in range(sz.groups):
             at = pl.multiple_of(peer(sz, place_ref[QUARTER], k, 1) * sz.used, 16)
             datt_refs[k][...] = dot_nt(branch, w_ref[pl.ds(at, sz.used), :]).astype(BF16)
@@ -440,13 +453,13 @@
         sums_ref[2:3, :] = jnp.sum(branch.astype(F32), axis=0, keepdims=True)
         sums_ref[3:4, :] = jnp.sum(cot, axis=0, keepdims=True)
 
-    outs = [((sz.rows, sz.width), F32), ((sz.rows, sz.width), BF16), ((4, sz.width), F32)]
+    outs = [((sz.rows, sz.width), F32)] + [((sz.width, half), BF16)] * 2 + [((4, sz.width), F32)]
     outs += [((sz.rows, sz.used), BF16)] * sz.groups
-    out = whole_call(body, outs, 1, (place, *back, cot, middle, out_weight, gain), "middle_backward")
-    return out[0], out[1], out[2], out[3:]
-
-
-def feed_forward_weights(sz, place, second, grad_hidden, act, cot):
+    out = whole_call(body, outs, 1, (place, *back, *att, cot, middle, out_weight, gain), "middle_backward")
+    return out[0], out[1:3], out[3], out[4:]
+
+
+def feed_forward_weights(sz, second, grad_hidden, act, cot):
     n = len(second)
     width, units = sz.width, act[0].shape[1]
     band, share = width // sz.n_ctx, units // sz.n_ctx
@@ -456,28 +469,25 @@
         second, grad_hidden, act, cot = (jnp.concatenate(v, axis=0) for v in (second, grad_hidden, act, cot))
         d_fc = dot_tn(second, grad_hidden).astype(BF16).reshape(sz.groups, sz.parts, -1, width)
         d_proj = dot_tn(act, cot).astype(BF16).reshape(sz.groups, sz.parts, -1, width)
-        total = jnp.roll(jnp.concatenate([d_fc, d_proj], axis=2), -place[ROW], axis=1)
-        return [total[:, s] for s in range(sz.parts)]
-
-    def body(place_ref, *refs):
+        return jnp.concatenate([d_fc, d_proj], axis=2)
+
+    def body(*refs):
         second_refs, grad_refs, act_refs, cot_refs = (refs[i * n : (i + 1) * n] for i in range(4))
-        outs, held = refs[4 * n : -1], refs[-1]
-        held[:width, :] = sum(dot_tn(x[...], g[...]) for x, g in zip(second_refs, grad_refs)).astype(BF16)
-        held[width:, :] = sum(dot_tn(a[...], c[...]) for a, c in zip(act_refs, cot_refs)).astype(BF16)
-        for s in range(sz.parts):
-            for g in range(sz.groups):
-                to = g * sz.parts + (place_ref[ROW] + s) % sz.parts
-                outs[s][g, :band, :] = held[pl.ds(pl.multiple_of(to * band, 16), band), :]
-                outs[s][g, band:, :] = held[pl.ds(pl.multiple_of(width + to * share, 16), share), :]
+        out_ref = refs[-1]
+        d_fc = sum(dot_tn(x[...], g[...]) for x, g in zip(second_refs, grad_refs)).astype(BF16)
+        for i in range(sz.n_ctx):
+            out_ref[i // sz.parts, i % sz.parts, :band, :] = d_fc[i * band : (i + 1) * band, :]
+        d_proj = sum(dot_tn(a[...], c[...]) for a, c in zip(act_refs, cot_refs)).astype(BF16)
+        for i in range(sz.n_ctx):
+            out_ref[i // sz.parts, i % sz.parts, band:, :] = d_proj[i * share : (i + 1) * share, :]
 
     return whole_call(
         body,
-        [((sz.groups, both, width), BF16)] * sz.parts,
-        1,
-        (place, *second, *grad_hidden, *act, *cot),
+        [((sz.groups, sz.parts, both, width), BF16)],
+        0,
+        (*second, *grad_hidden, *act, *cot),
         "feed_forward_weights",
-        [pltpu.VMEM((width + units, width), BF16)],
-    )
+    )[0]
 
 
 def feed_forward_out(sz, act, proj):
@@ -490,25 +500,6 @@
     return whole_call(body, [((sz.rows, sz.width), BF16)] * n, 0, (*act, proj), "feed_forward_out")
 
 
-def out_weights(sz, place, att, branch):
-    half = sz.width // 2
-
-    def body(place_ref, *refs):
-        branch_ref, own_ref, other_ref = refs[sz.groups :]
-        core = place_ref[CORE]
-        for k in range(sz.groups):
-            at = pl.multiple_of(peer(sz, place_ref[QUARTER], k, -1) * sz.used, 16)
-
-            @pl.when(at < sz.width)
-            def _():
-                grad_w = dot_tn(refs[k][...], branch_ref[...]).astype(BF16)
-                left, right = grad_w[:, :half], grad_w[:, half:]
-                own_ref[pl.ds(at, sz.used), :] = jnp.where(core == 0, left, right)
-                other_ref[pl.ds(at, sz.used), :] = jnp.where(core == 0, right, left)
-
-    return whole_call(body, [((sz.width, half), BF16)] * 2, 1, (place, *att, branch), "out_weights")
-
-
 def sum_arrays(sz, pieces, name):
     def body(*refs):
         refs[-1][...] = sum(r[...].astype(F32) for r in refs[:-1]).astype(BF16)
@@ -516,36 +507,43 @@
     return whole_call(body, [(pieces[0].shape, BF16)], 0, tuple(pieces), name)[0]
 
 
-def sum_first(sz, value, name):
-    def body(ref, out_ref):
-        out_ref[...] = sum(ref[k].astype(F32) for k in range(value.shape[0])).astype(BF16)
-
-    return whole_call(body, [(value.shape[1:], BF16)], 0, (value,), name)[0]
+def sum_groups(sz, place, got):
+    shape = got.shape[2:]
+    if not sz.aligned:
+        total = jnp.roll(got.astype(F32).sum(axis=0), -place[ROW], axis=0).astype(BF16)
+        return [total[s] for s in range(sz.parts)]
+
+    def body(place_ref, got_ref, *outs):
+        for s in range(sz.parts):
+            at = (place_ref[ROW] + s) % sz.parts
+            outs[s][...] = sum(got_ref[k, at].astype(F32) for k in range(sz.groups)).astype(BF16)
+
+    return whole_call(body, [(shape, BF16)] * sz.parts, 1, (place, got), "sum_groups")
 
 
 def pack_sums(sz, place, sel, out, tail):
     rows, lanes = sel[0].shape[1:]
-    n_tail = tail.shape[1]
-    full = rows + n_tail + rows // 2
+    n_tail, n_out = tail.shape[1], out[0].shape[1] // 2
+    full = rows + n_tail + n_out
     if not sz.packed:
         sel = sum(t.astype(F32) for t in sel).astype(BF16)
         out = sum(t.astype(F32) for t in out).astype(BF16)
-        out = jnp.concatenate([out[:, : rows // 2], out[:, rows // 2 :]], axis=2)
+        out = jnp.concatenate([out[:, :n_out], out[:, n_out:]], axis=2)
         both = jnp.concatenate([sel, tail, out], axis=1).reshape((sz.groups, sz.parts, full, lanes))
         both = jnp.roll(both, (-place[HG], -place[ROW]), axis=(0, 1))
         return [both[:, s] for s in range(sz.parts)]
     n = len(sel)
 
     def body(place_ref, *refs):
-        tail_ref, outs = refs[2 * n], refs[2 * n + 1 :]
+        tail_ref, outs = refs[n + 2], refs[n + 3 :]
         for k in range(sz.groups):
             for s in range(sz.parts):
                 to = ((place_ref[HG] + k) % sz.groups) * sz.parts + (place_ref[ROW] + s) % sz.parts
                 outs[s][k, :rows, :] = sum(r[to].astype(F32) for r in refs[:n]).astype(BF16)
                 outs[s][k, rows : rows + n_tail, :] = tail_ref[to]
-                total = sum(r[to].astype(F32) for r in refs[n : 2 * n]).astype(BF16)
-                outs[s][k, rows + n_tail :, : lanes // 2] = total[: rows // 2]
-                outs[s][k, rows + n_tail :, lanes // 2 :] = total[rows // 2 :]
+                total = (refs[n][to].astype(F32) + refs[n + 1][to].astype(F32)).astype(BF16)
+                outs[s][k, rows + n_tail :, : lanes // 2] = total[:n_out]
+                outs[s][k, rows + n_tail :, lanes // 2 :] = total[n_out:]
 
     return whole_call(
         body, [((sz.groups, full, lanes), BF16)] * sz.parts, 1, (place, *sel, *out, tail), "pack_sums"
@@ -722,18 +720,33 @@
     return jnp.roll(held, place[CORE], axis=0).swapaxes(0, 1).astype(F32)
 
 
-def qkv_weights(sz, normed, dqkv):
+def qkv_weights(sz, place, normed, dqkv):
     band = sz.width // sz.n_ctx
+    rows = band // sz.gx
     w3 = 3 * sz.lanes
 
-    def body(normed_ref, dqkv_ref, out_ref):
-        grad = dot_tn(normed_ref[...], dqkv_ref[...]).astype(BF16)
-        for i in range(sz.n_ctx):
-            out_ref[i] = grad[i * band : (i + 1) * band, :]
-
     if not sz.packed:
-        return dot_tn(normed, dqkv).astype(BF16).reshape(sz.n_ctx, band, w3)
-    return whole_call(body, [((sz.n_ctx, band, w3), BF16)], 0, (normed, dqkv), "qkv_weights")[0]
+        grad = dot_tn(normed, dqkv).astype(BF16).reshape(sz.n_ctx, sz.gx, rows, w3)
+        grad = jnp.roll(grad, -place[GX], axis=1)
+        return [grad[:, k] for k in range(sz.gx)]
+
+    def body(place_ref, normed_ref, dqkv_ref, *refs):
+        held = refs[-1]
+        held[...] = dot_tn(normed_ref[...], dqkv_ref[...]).astype(BF16)
+        for k in range(sz.gx):
+            to = (place_ref[GX] + k) % sz.gx
+            for i in range(sz.n_ctx):
+                at = pl.multiple_of(i * band + to * rows, 16)
+                refs[k][i] = held[pl.ds(at, rows), :]
+
+    return whole_call(
+        body,
+        [((sz.n_ctx, rows, w3), BF16)] * sz.gx,
+        1,
+        (place, normed, dqkv),
+        "qkv_weights",
+        [pltpu.VMEM((sz.width, w3), BF16)],
+    )
 
 
 def join_heads(sz, place, pieces, rows, n_tail):
@@ -745,8 +758,8 @@
         held = order_grp(sz, place, pieces)
         sel = held[:, :, :start].reshape(sz.gx, 2, sz.half, rows, lanes)
         sel = sel.transpose(2, 1, 0, 3, 4).reshape(sz.groups, sz.gx * rows, lanes)
-        out = held[:, :, end:].reshape(sz.gx, 2, rows // 2, 2, half)
-        out = out.transpose(0, 3, 2, 1, 4).reshape(sz.gx * rows, sz.width)
+        out = held[:, :, end:].sum(axis=0).reshape(2, sz.gx * rows // 2, 2, half)
+        out = out.transpose(2, 1, 0, 3).reshape(sz.gx * rows, sz.width)
         small = add_halves(held[:, :, start:end]).sum(axis=(0, 1))
         return join_slots(sz, sel), out, *(small[row, at : at + n] for row, at, n in small_cuts(sz))
 
@@ -773,11 +786,11 @@
                 sel_ref[at_rows, third * sz.width : (third + 1) * sz.width] = own + jnp.concatenate(
                     [first, rest], axis=1
                 )
-            for c in range(2):
-                piece = held[2 * x + c, end:, :].astype(F32)
-                columns = slice(c * half, (c + 1) * half)
-                out_ref[x * rows : x * rows + rows // 2, columns] = piece[:, :half]
-                out_ref[x * rows + rows // 2 : (x + 1) * rows, columns] = piece[:, half:]
+        mid = sz.gx * rows // 2
+        for c in range(2):
+            piece = sum(held[2 * x + c, end:, :].astype(F32) for x in range(sz.gx))
+            out_ref[:mid, c * half : (c + 1) * half] = piece[:, :half]
+            out_ref[mid:, c * half : (c + 1) * half] = piece[:, half:]
 
     return whole_call(
         body,
@@ -848,22 +861,26 @@
     )
 
 
-def unsort_rows(sz, place, docs, blocks):
+def unsort_rows(sz, place, docs, *arrays):
+    n = len(arrays)
+
     def body(place_ref, doc_ref, *refs):
-        out_ref = refs[-1]
+        outs = refs[n * sz.parts :]
         for t in range(sz.parts):
             for a in range(4):
                 src = source_grain(sz, doc_ref, 4 * ((place_ref[ROW] + t) % sz.parts) + a)
-                out_ref[src] = refs[t][pl.ds(a * sz.grain, sz.grain), :].astype(F32)
+                at = pl.ds(a * sz.grain, sz.grain)
+                for i in range(n):
+                    outs[i][src] = refs[i * sz.parts + t][at, :].astype(F32)
 
     out = whole_call(
         body,
-        [((sz.grains, sz.grain, sz.width), F32)],
+        [((sz.grains, sz.grain, sz.width), F32)] * n,
         2,
-        (place, docs, *blocks),
+        (place, docs, *(b for blocks in arrays for b in blocks)),
         "unsort_rows",
     )
-    return out[0].reshape(sz.rows, sz.width)
+    return [o.reshape(sz.rows, sz.width) for o in out]
 
 
 def gather_near(sz, block):
@@ -888,8 +905,21 @@
     return terms, later
 
 
-def all_grp(sz, value):
+def return_direct(sz, near, far):
+    terms = [near[0], shift(near[1], "core", 2, 1)]
+    for k in range(1, sz.gx):
+        for c in range(2):
+            pairs = [
+                (2 * x + core, 2 * ((x - k) % sz.gx) + (core + c) % 2) for x in range(sz.gx) for core in range(2)
+            ]
+            terms.append(lax.ppermute(far[2 * k - 2 + c], GRP, pairs))
+    return terms
+
+
+def all_grp(sz, value, before=None):
     along = [value] + [shift(value, "gx", sz.gx, k) for k in range(1, sz.gx)]
+    if before is not None:
+        along = after(before, along)
     return along + [shift(v, "core", 2, 1) for v in along]
 
 
@@ -1016,23 +1046,18 @@
     tok_rows = jnp.concatenate(to_owner(sz, tok_parts), axis=0)
     docs = jnp.where(core == part % 2, doc_blocks, shift(doc_blocks, "core", 2, 1))
 
+    w_sel, fc, proj = weight_shares(sz, place, *after(tok_rows, (qkv_weight, fc_weight, proj_weight)))
     chunks = []
     for k in range(sz.half):
-        block = to_peer(sz, tok_rows, 2 * k)
+        block = after(w_sel, to_peer(sz, tok_rows, 2 * k)) if k else tok_rows
         chunks += [block, to_peer(sz, block, 1)]
 
-    qkv_weight, fc_weight, proj_weight, cot_parts = after(
-        tok_rows, (qkv_weight, fc_weight, proj_weight, cot_parts)
-    )
-    w_sel, fc, proj = weight_shares(sz, place, qkv_weight, fc_weight, proj_weight)
-    cot_rows = jnp.concatenate(to_owner(sz, cot_parts), axis=0)
+    cot_rows = jnp.concatenate(to_owner(sz, after(tok_rows, cot_parts)), axis=0)
     cot_near = gather_near(sz, cot_rows)
-    cot_along = [shift(cot_rows, "gx", sz.gx, k) for k in range(1, sz.gx)]
-
-    chunks = after(cot_rows, chunks)
+    cot_far = gather_far(sz, cot_rows, place)
+
     saved, att_out = attend_forward(sz, place, docs, chunks, gain1, bias1, w_sel, b_sel)
-    cot_far = [b for along in cot_along for b in (along, shift(along, "core", 2, 1))]
-    att_out = after((cot_along, cot_near), att_out)
+    att_out = after(cot_rows, att_out)
     att = [to_peer(sz, att_out[k], k) for k in range(sz.groups)]
     middle, second = project_out(
         sz, place, att, tok_rows, w_out, vector(out_bias), gain2, bias2
@@ -1044,60 +1069,51 @@
     sec_far = gather_far(sz, second, (back_n, mixed_n))
     act_f, gh_f, back_f, fc_sum_f = feed_forward(sz, sec_far, cot_far, fc, fc_b, proj, "feed_forward_far")
     back, act_f = return_rows(sz, back_n, back_f, act_f)
-    ff_sent = feed_forward_weights(
-        sz, place, sec_near + sec_far, gh_n + gh_f, act_n + act_f, cot_near + cot_far
-    )
+    ff_sent = feed_forward_weights(sz, sec_near + sec_far, gh_n + gh_f, act_n + act_f, cot_near + cot_far)
     mixed_f = feed_forward_out(sz, after(ff_sent, act_f), proj)
     back = after(mixed_f, back)
-    grad_middle, branch, mid_sums, datt_out = middle_backward(
-        sz, place, back, middle, cot_rows, w_out, gain2
+    grad_middle, d_out, mid_sums, datt_out = middle_backward(
+        sz, place, back, middle, cot_rows, w_out, gain2, att
     )
     datt = [to_peer(sz, datt_out[k], k) for k in range(sz.groups)]
 
     band = width // n_ctx
     half = width // 2
     n_rows = band // sz.gx
-    ff_got = [shift(ff_sent[s], "part", sz.parts, s) for s in range(1, sz.parts)]
-    mixed, _ = return_rows(sz, mixed_n, mixed_f, place)
-
-    def over_gx(value):
-        value = value.reshape(n_ctx, sz.gx, n_rows, value.shape[2])
-        pieces = []
-        for k in range(sz.gx):
-            piece = lax.dynamic_index_in_dim(value, (gx + k) % sz.gx, 1, keepdims=False)
-            pieces.append(shift(piece, "gx", sz.gx, k) if k else piece)
-        return pieces
-
-    own, other = out_weights(sz, place, att, branch)
-    own = own.astype(F32) + shift(other, "core", 2, 1).astype(F32)
-    out_terms = over_gx(own.astype(BF16).reshape(n_ctx, band, half))
+    datt[1:], ff_sent = lax.optimization_barrier((datt[1:], ff_sent))
+    ff_far = lax.all_to_all(ff_sent, "hg", 0, 0, tiled=True)
+    mixed = return_direct(sz, mixed_n, mixed_f)
+
+    out_terms = [d.reshape(n_ctx, band, half) for d in (d_out[0], shift(d_out[1], "core", 2, 1))]
 
     dqkv, qkv_sum, ln1_sums, dnorm_out = attend_backward(sz, place, docs, saved, w_sel, datt)
+    dnorm_out, dqkv = after((mixed, out_terms), (dnorm_out, dqkv))
     dnorm = [dnorm_out[0], to_peer(sz, dnorm_out[1], 1)]
     for k in range(1, sz.half):
         both = dnorm_out[2 * k].astype(F32) + to_peer(sz, dnorm_out[2 * k + 1], 1).astype(F32)
         both = both.astype(BF16)
         dnorm.append(to_peer(sz, both, 2 * k))
     grad_parts = finish_tokens(sz, dnorm, tok_rows, grad_middle, gain1)
-    grad_tokens = unsort_rows(sz, place, doc_blocks, from_owner(sz, grad_parts))
-
+    grad_back = from_owner(sz, grad_parts)
     out_parts = finish_middle(sz, after(dqkv, mixed), middle, vector(proj_bias))
-    output = unsort_rows(sz, place, doc_blocks, from_owner(sz, out_parts))
-
-    d_sel = qkv_weights(sz, saved[1], after((both, ff_got, mixed, own), dqkv))
-    sel_terms = after(grad_parts, over_gx(d_sel))
+
+    sel_terms = qkv_weights(sz, place, saved[1], dqkv)
+    sel_terms = [sel_terms[0]] + [shift(sel_terms[k], "gx", sz.gx, k) for k in range(1, sz.gx)]
     tail = pack_vectors(sz, place, ln1_sums, qkv_sum, mid_sums, [fc_sum_n, fc_sum_f])
     n_tail = tail.shape[1]
-    pieces = pack_sums(sz, place, sel_terms, out_terms, tail)
-    pieces = [pieces[0]] + [shift(pieces[s], "part", sz.parts, s) for s in range(1, sz.parts)]
-    blocks = sum_packed(sz, pieces, n_rows, n_tail)
-    blocks = [blocks[0]] + [shift(blocks[k], "hg", sz.groups, k) for k in range(1, sz.groups)]
-    sums = unpack_sums(sz, place, blocks, n_rows, n_tail)
+    pieces = pack_sums(sz, place, sel_terms, out_terms, after(out_parts, tail))
+    got = [pieces[0]] + [shift(pieces[s], "part", sz.parts, s) for s in range(1, sz.parts)]
+    out_back = from_owner(sz, out_parts)
+    blocks = sum_packed(sz, after((grad_parts, out_back), got), n_rows, n_tail)
+    got = [blocks[0]] + [shift(blocks[k], "hg", sz.groups, k) for k in range(1, sz.groups)]
+    sums = unpack_sums(sz, place, after(grad_back, got), n_rows, n_tail)
     grad_qkv, grad_out, *cuts = join_heads(sz, place, all_grp(sz, sums), n_rows, n_tail)
-
-    ff_near = sum_arrays(sz, [ff_sent[0]] + after((d_sel, dnorm), ff_got), "sum_parts")
-    ff_share = sum_first(sz, lax.all_to_all(ff_near, "hg", 0, 0, tiled=True), "sum_groups")
-    grad_fc, grad_proj = join_shares(sz, place, all_grp(sz, ff_share))
+    output, grad_tokens = unsort_rows(sz, place, doc_blocks, out_back, grad_back)
+
+    ff_parts = sum_groups(sz, place, after(pieces, ff_far))
+    ff_parts = [ff_parts[0]] + [shift(ff_parts[s], "part", sz.parts, s) for s in range(1, sz.parts)]
+    ff_share = sum_arrays(sz, after(blocks, ff_parts), "sum_parts")
+    grad_fc, grad_proj = join_shares(sz, place, all_grp(sz, ff_share, sums))
 
     g_ln1_gain, g_ln1_bias, g_qkv_bias, g_out_bias, g_ln2_gain, g_ln2_bias, g_fc_bias, g_proj_bias = cuts
     return (

time: 250 us -> 240 us (0.960)
  the two profiles are of different devices: /device:TPU:1 before, /device:TPU:9 now
where the time goes in v2:
time: 240 us; the launch traced here: 235 us
  Pallas kernels  106 us (44%)
  starting transfers between devices  57.2 us (24%)
  waiting for transfers between devices  51.2 us (21%)
  local copies, waits for them, and re-layouts  17.1 us (7%)
  other arithmetic  2.46 us (1%)
    pallas_call x23, Pallas kernels, whole_call(): pl.pallas_call(body, out_shape=shapes, in_specs=specs, out_specs=[pl.Bloc...  106 us
    ppermute x24, waiting for transfers between devices, shift(): lax.ppermute(value, axis, [(i, (i + step) % size) for i in range(size)])  28.4 us
    ppermute x4, starting transfers between devices, from_owner(): lax.ppermute(b, ('core',) + CTX, [(b_, a_) for a_, b_ in owner_pairs(sz,...  17.9 us
    ppermute x24, starting transfers between devices, shift(): lax.ppermute(value, axis, [(i, (i + step) % size) for i in range(size)])  15.7 us
    unnamed x110, local copies, waits for them, and re-layouts  10.7 us
    ppermute x12, waiting for transfers between devices, to_peer(): return lax.ppermute(value, ('core', 'hg'), pairs)  10.1 us
    ppermute x4, starting transfers between devices, to_owner(): lax.ppermute(b, ('core',) + CTX, owner_pairs(sz, t))  10 us
    ppermute x4, waiting for transfers between devices, to_owner(): lax.ppermute(b, ('core',) + CTX, owner_pairs(sz, t))  8.13 us
  transfers between devices with their start and end apart: 47, of which 16 were waited for; matrix products, arithmetic and copies ran while one was open for 4% of the time, Pallas kernels for 34%

profile of v2, /device:TPU:9, one launch (start us, length us, event | category | flops | bytes accessed | tf_op | source)
XLA Modules:
  0.0 234.8 jit_solution(3408702088021357730)
XLA Ops:
  2.0 2.2 sort_rows.1
  4.2 3.0 %collective-permute-start = (bf16[128,768]{1,0:T(8,128)(2,1)}, bf16[128,768]{1,0:T(8,128)(2,1)S(1)}, u32[]{:S(2)}, u32[]{:S(2)}) collective-permute-start(bf16[128,768]{1,0:T(8,128)(2,1)} %get-tuple-element.139), channel_id=1, source_target_pairs={{0,0},{1,4},{2,8},{3,12},{4,2},{5,6},{6,10},{7,14},{8,1},{9,5},{10... | collective-permute-start | bytes 589832 | tf_op jit(solution)/shard_map/ppermute | solution.py:101
  7.3 2.4 %collective-permute-start.1 = (bf16[128,768]{1,0:T(8,128)(2,1)}, bf16[128,768]{1,0:T(8,128)(2,1)S(1)}, u32[]{:S(2)}, u32[]{:S(2)}) collective-permute-start(bf16[128,768]{1,0:T(8,128)(2,1)} %get-tuple-element.140), channel_id=1, source_target_pairs={{0,4},{1,0},{2,12},{3,8},{4,6},{5,2},{6,14},{7,10},{8,5},{9,1},{10... | collective-permute-start | bytes 589832 | tf_op jit(solution)/shard_map/ppermute | solution.py:101
  10.4 4.1 %collective-permute-done = bf16[128,768]{1,0:T(8,128)(2,1)S(1)} collective-permute-done((bf16[128,768]{1,0:T(8,128)(2,1)}, bf16[128,768]{1,0:T(8,128)(2,1)S(1)}, u32[]{:S(2)}, u32[]{:S(2)}) %collective-permute-start) | collective-permute-done | bytes 196640 | tf_op jit(solution)/shard_map/ppermute | solution.py:101
  14.5 3.9 %collective-permute-done.1 = bf16[128,768]{1,0:T(8,128)(2,1)S(1)} collective-permute-done((bf16[128,768]{1,0:T(8,128)(2,1)}, bf16[128,768]{1,0:T(8,128)(2,1)S(1)}, u32[]{:S(2)}, u32[]{:S(2)}) %collective-permute-start.1) | collective-permute-done | bytes 196640 | tf_op jit(solution)/shard_map/ppermute | solution.py:101
  20.5 2.0 collective-permute-start.5
  22.5 3.7 %collective-permute-start.2 = (bf16[128,768]{1,0:T(8,128)(2,1)}, bf16[128,768]{1,0:T(8,128)(2,1)S(1)}, u32[]{:S(2)}, u32[]{:S(2)}) collective-permute-start(bf16[128,768]{1,0:T(8,128)(2,1)} %get-tuple-element.143), channel_id=1, source_target_pairs={{0,0},{1,4},{2,8},{3,12},{4,2},{5,6},{6,10},{7,14},{8,1},{9,5},{10... | collective-permute-start | bytes 589832 | tf_op jit(solution)/shard_map/ppermute | solution.py:101
  27.1 8.2 %weight_shares.1 = (bf16[768,768]{1,0:T(8,128)(2,1)}, bf16[768,768]{1,0:T(8,128)(2,1)}, bf16[768,768]{1,0:T(8,128)(2,1)}) custom-call(s32[6]{0:T(128)} %stack.27.place_ref, bf16[768,2304]{1,0:T(8,128)(2,1)} %qkv_ref, bf16[768,3072]{1,0:T(8,128)(2,1)} %fc_in, bf16[3072,768]{1,0:T(8,128)(2,1)} %proj_in), custom_call_target="tpu_custom_call" | custom-call | bytes 16515096 | tf_op jit(solution)/shard_map/weight_shares/pallas_call | solution.py:120
  37.9 11.0 %attend_forward.1 = (bf16[1024,768]{1,0:T(8,128)(2,1)}, bf16[1024,768]{1,0:T(8,128)(2,1)}, bf16[1024,768]{1,0:T(8,128)(2,1)}, f32[1024,128]{1,0:T(8,128)}, f32[1...) custom-call(s32[6]{0:T(128)} %stack.27.place_ref, ...), custom_call_target="tpu_custom_call" | custom-call | flops 8999999488 | bytes 9462828 | tf_op jit(solution)/shard_map/attend_forward/pallas_call | solution.py:120
  55.5 2.6 %collective-permute-done.9.refs_2_.refs_5_ = bf16[256,192]{1,0:T(8,128)(2,1)S(1)} collective-permute-done((bf16[256,192]{1,0:T(8,128)(2,1)}, bf16[256,192]{1,0:T(8,128)(2,1)S(1)}, u32[]{:S(2)}, u32[]{:S(2)}) %collective-permute-start.9) | collective-permute-done | bytes 98336 | tf_op jit(solution)/shard_map/ppermute | solution.py:84
  58.7 3.2 %project_out.1 = (f32[256,768]{1,0:T(8,128)}, bf16[256,768]{1,0:T(8,128)(2,1)}) custom-call(s32[6]{0:T(128)} %stack.27.place_ref, bf16[256,192]{1,0:T(8,128)(2,1)} %get-tuple-element.154.refs_0_.refs_3_, bf16[256,192]{1,0:T(8,128)(2,1)} %copy-done.13, bf16[256,192]{1,0:T(8,128)(2,1)} %copy-done.14, bf16[256,192]{1,0:T(8,128)(2,1)} %copy-done.12, ...), custom_call_target="tpu_custom_call" | custom-call | bytes 3154968 | tf_op jit(solution)/shard_map/project_out/pallas_call | solution.py:120
  63.7 1.3 collective-permute-done.16.refs_2_.refs_14_
  67.0 5.8 %feed_forward_near.1 = (bf16[256,768]{1,0:T(8,128)(2,1)}, bf16[256,768]{1,0:T(8,128)(2,1)}, bf16[256,768]{1,0:T(8,128)(2,1)}, bf16[256,768]{1,0:T(8,128)(2,1)}, ...) custom-call(bf16[256,768]{1,0:T(8,128)(2,1)} %get-tuple-element.158.refs_0_, ...), custom_call_target="tpu_custom_call" | custom-call | bytes 6297600 | tf_op jit(solution)/shard_map/feed_forward_near/pallas_call | solution.py:120
  72.9 3.3 %feed_forward_out.2 = (bf16[256,768]{1,0:T(8,128)(2,1)}, bf16[256,768]{1,0:T(8,128)(2,1)}) custom-call(bf16[256,768]{1,0:T(8,128)(2,1)} %get-tuple-element.161.refs_0_.refs_8_, bf16[256,768]{1,0:T(8,128)(2,1)} %get-tuple-element.162.refs_1_.refs_9_, bf16[768,768]{1,0:T(8,128)(2,1)} %get-tuple-element.160.refs_6_.refs_2_), custom_call_target="tpu_custom_call" | custom-call | bytes 2752512 | tf_op jit(solution)/shard_map/feed_forward_out/pallas_call | solution.py:120
  76.3 1.7 collective-permute-done.15.refs_1_.refs_3_
  78.7 5.8 %feed_forward_far.1 = (bf16[256,768]{1,0:T(8,128)(2,1)}, bf16[256,768]{1,0:T(8,128)(2,1)}, bf16[256,768]{1,0:T(8,128)(2,1)}, bf16[256,768]{1,0:T(8,128)(2,1)}, b...) custom-call(bf16[256,768]{1,0:T(8,128)(2,1)} %copy-done.6, bf16[256,768]{1,0:T(8,128)(2,1)} %copy-done.8, ...), custom_call_target="tpu_custom_call" | custom-call | bytes 6297600 | tf_op jit(solution)/shard_map/feed_forward_far/pallas_call | solution.py:120
  85.0 1.4 collective-permute-done.18
  88.8 6.8 %feed_forward_weights.1 = bf16[4,2,192,768]{3,2,1,0:T(8,128)(2,1)} custom-call(bf16[256,768]{1,0:T(8,128)(2,1)} %get-tuple-element.158.refs_0_, bf16[256,768]{1,0:T(8,128)(2,1)} %copy-done.5, bf16[256,768]{1,0:T(8,128)(2,1)} %copy-done.6, bf16[256,768]{1,0:T(8,128)(2,1)} %copy-done.8, bf16[256,768]{1,0:T(8,128)(2,1)} %get-tuple-element.168.refs_4_, ...), custom_call_target="tpu_custom_call" | custom-call | bytes 8650752 | tf_op jit(solution)/shard_map/feed_forward_weights/pallas_call | solution.py:120
  95.6 3.0 %feed_forward_out.3 = (bf16[256,768]{1,0:T(8,128)(2,1)}, bf16[256,768]{1,0:T(8,128)(2,1)}) custom-call(bf16[256,768]{1,0:T(8,128)(2,1)} %get-tuple-element.179.refs_10_.refs_0_, bf16[256,768]{1,0:T(8,128)(2,1)} %get-tuple-element.180.refs_11_.refs_1_, bf16[768,768]{1,0:T(8,128)(2,1)} %get-tuple-element.160.refs_6_.refs_2_), custom_call_target="tpu_custom_call" | custom-call | bytes 2752512 | tf_op jit(solution)/shard_map/feed_forward_out/pallas_call | solution.py:120
  99.6 5.5 %middle_backward.1 = (f32[256,768]{1,0:T(8,128)}, bf16[768,384]{1,0:T(8,128)(2,1)}, bf16[768,384]{1,0:T(8,128)(2,1)}, f32[4,768]{1,0:T(4,128)}, bf16[256,192]{1,...) custom-call(s32[6]{0:T(128)} %stack.27.place_ref, ...), custom_call_target="tpu_custom_call" | custom-call | bytes 6306840 | tf_op jit(solution)/shard_map/middle_backward/pallas_call | solution.py:120
  105.6 1.7 collective-permute-start.26
  107.3 3.7 %collective-permute-done.25.refs_2_ = bf16[256,192]{1,0:T(8,128)(2,1)} collective-permute-done((bf16[256,192]{1,0:T(8,128)(2,1)}, bf16[256,192]{1,0:T(8,128)(2,1)}, u32[]{:S(2)}, u32[]{:S(2)}) %collective-permute-start.25) | collective-permute-done | bytes 98336 | tf_op jit(solution)/shard_map/ppermute | solution.py:84
  111.0 3.0 %collective-permute-done.26.refs_3_ = bf16[256,192]{1,0:T(8,128)(2,1)} collective-permute-done((bf16[256,192]{1,0:T(8,128)(2,1)}, bf16[256,192]{1,0:T(8,128)(2,1)}, u32[]{:S(2)}, u32[]{:S(2)}) %collective-permute-start.26) | collective-permute-done | bytes 98336 | tf_op jit(solution)/shard_map/ppermute | solution.py:84
  114.0 4.0 %all-to-all-start = ((bf16[4,2,192,768]{3,2,1,0:T(8,128)(2,1)}), bf16[4,2,192,768]{3,2,1,0:T(8,128)(2,1)S(1)}, u32[]{:S(2)}, u32[]{:S(2)}) async-start(bf16[4,2,192,768]{3,2,1,0:T(8,128)(2,1)} %feed_forward_weights.1), calls=%async_computation | async-start | bytes 4718592 | tf_op jit(solution)/shard_map/all_to_all | solution.py:1084
  120.6 18.3 %attend_backward.1 = (bf16[1024,768]{1,0:T(8,128)(2,1)}, f32[1,768]{1,0:T(1,128)}, f32[2,768]{1,0:T(2,128)}, bf16[256,768]{1,0:T(8,128)(2,1)}, bf16[256,768]{1,0...) custom-call(s32[6]{0:T(128)} %stack.27.place_ref, s32[1,5]{1,0:T(1,128)} %broadcast_select_fusion.doc_ref, ...), custom_call_target="tpu_custom_call" | custom-call | flops 16999999488 | bytes 9462828 | tf_op jit(solution)/shard_map/attend_backward/pallas_call | solution.py:120
  139.0 5.0 %qkv_weights.1 = (bf16[8,48,768]{2,1,0:T(8,128)(2,1)}, bf16[8,48,768]{2,1,0:T(8,128)(2,1)}) custom-call(s32[6]{0:T(128)} %stack.27.place_ref, bf16[1024,768]{1,0:T(8,128)(2,1)} %get-tuple-element.223.normed_ref, bf16[1024,768]{1,0:T(8,128)(2,1)} %get-tuple-element.207.dqkv_ref), custom_call_target="tpu_custom_call" | custom-call | bytes 4325400 | tf_op jit(solution)/shard_map/qkv_weights/pallas_call | solution.py:120
  146.4 1.9 pack_vectors.1.refs_4_
  148.4 2.5 %finish_middle.1 = (bf16[128,768]{1,0:T(8,128)(2,1)}, bf16[128,768]{1,0:T(8,128)(2,1)}) custom-call(bf16[256,768]{1,0:T(8,128)(2,1)} %get-tuple-element.208.refs_0_, bf16[256,768]{1,0:T(8,128)(2,1)} %copy-done.15, bf16[256,768]{1,0:T(8,128)(2,1)} %copy-done.16, bf16[256,768]{1,0:T(8,128)(2,1)} %copy-done.17, f32[256,768]{1,0:T(8,128)} %get-tuple-element.187.refs_8_.refs_4_, ...), custom_call_target="tpu_custom_call" | custom-call | bytes 2755584 | tf_op jit(solution)/shard_map/finish_middle/pallas_call | solution.py:120
  150.9 8.0 %collective-permute-done.34.refs_1_ = bf16[8,48,768]{2,1,0:T(8,128)(2,1)S(1)} collective-permute-done((bf16[8,48,768]{2,1,0:T(8,128)(2,1)}, bf16[8,48,768]{2,1,0:T(8,128)(2,1)S(1)}, u32[]{:S(2)}, u32[]{:S(2)}) %collective-permute-start.34) | collective-permute-done | bytes 589856 | tf_op jit(solution)/shard_map/ppermute | solution.py:73
  159.8 3.0 %pack_sums.1 = (bf16[4,112,768]{2,1,0:T(8,128)(2,1)}, bf16[4,112,768]{2,1,0:T(8,128)(2,1)}) custom-call(s32[6]{0:T(128)} %stack.27.place_ref, bf16[8,48,768]{2,1,0:T(8,128)(2,1)} %get-tuple-element.224.refs_0_, bf16[8,48,768]{2,1,0:T(8,128)(2,1)} %copy-done.11, bf16[8,96,384]{2,1,0:T(8,128)(2,1)} %bitcast.12, bf16[8,96,384]{2,1,0:T(8,128)(2,1)} %bitcast.13, ...), custom_call_target="tpu_custom_call" | custom-call | bytes 3932184 | tf_op jit(solution)/shard_map/pack_sums/pallas_call | solution.py:120
  163.7 4.5 %all-to-all-done.got_ref = bf16[4,2,192,768]{3,2,1,0:T(8,128)(2,1)S(1)} async-done(((bf16[4,2,192,768]{3,2,1,0:T(8,128)(2,1)}), bf16[4,2,192,768]{3,2,1,0:T(8,128)(2,1)S(1)}, u32[]{:S(2)}, u32[]{:S(2)}) %all-to-all-start) | async-done | bytes 2359328 | tf_op jit(solution)/shard_map/all_to_all | solution.py:1084
  168.2 1.4 copy-done
  169.6 2.7 %sum_groups.1 = (bf16[192,768]{1,0:T(8,128)(2,1)}, bf16[192,768]{1,0:T(8,128)(2,1)}) custom-call(s32[6]{0:T(128)} %stack.27.place_ref, bf16[4,2,192,768]{3,2,1,0:T(8,128)(2,1)} %copy-done), custom_call_target="tpu_custom_call" | custom-call | bytes 2949144 | tf_op jit(solution)/shard_map/sum_groups/pallas_call | solution.py:120
  172.3 6.3 %collective-permute-start.27 = (bf16[128,768]{1,0:T(8,128)(2,1)S(1)}, bf16[128,768]{1,0:T(8,128)(2,1)S(1)}, u32[]{:S(2)}, u32[]{:S(2)}) collective-permute-start(bf16[128,768]{1,0:T(8,128)(2,1)S(1)} %copy-done.52), channel_id=1, source_target_pairs={{0,0},{4,1},{8,2},{12,3},{2,4},{6,5},{10,6},{14,7},{1,8},{5,9},{9,... | collective-permute-start | bytes 589832 | tf_op jit(solution)/shard_map/ppermute | solution.py:106
  179.9 2.9 %finish_tokens.1 = (bf16[128,768]{1,0:T(8,128)(2,1)}, bf16[128,768]{1,0:T(8,128)(2,1)}) custom-call(bf16[256,768]{1,0:T(8,128)(2,1)} %get-tuple-element.214.refs_0_, bf16[256,768]{1,0:T(8,128)(2,1)} %copy-done.18, bf16[256,768]{1,0:T(8,128)(2,1)} %collective-permute-done.31.refs_2_, bf16[256,768]{1,0:T(8,128)(2,1)} %copy-done.2, ...), custom_call_target="tpu_custom_call" | custom-call | bytes 2755584 | tf_op jit(solution)/shard_map/finish_tokens/pallas_call | solution.py:120
  182.8 4.8 %collective-permute-start.32 = (bf16[128,768]{1,0:T(8,128)(2,1)}, bf16[128,768]{1,0:T(8,128)(2,1)S(1)}, u32[]{:S(2)}, u32[]{:S(2)}) collective-permute-start(bf16[128,768]{1,0:T(8,128)(2,1)} %get-tuple-element.219), channel_id=1, source_target_pairs={{0,0},{4,1},{8,2},{12,3},{2,4},{6,5},{10,6},{14,7},{1,8},{5,9},{9,... | collective-permute-start | bytes 589832 | tf_op jit(solution)/shard_map/ppermute | solution.py:106
  187.7 5.5 %collective-permute-start.33 = (bf16[128,768]{1,0:T(8,128)(2,1)}, bf16[128,768]{1,0:T(8,128)(2,1)S(1)}, u32[]{:S(2)}, u32[]{:S(2)}) collective-permute-start(bf16[128,768]{1,0:T(8,128)(2,1)} %get-tuple-element.220), channel_id=1, source_target_pairs={{4,0},{0,1},{12,2},{8,3},{6,4},{2,5},{14,6},{10,7},{5,8},{1,9},{13... | collective-permute-start | bytes 589832 | tf_op jit(solution)/shard_map/ppermute | solution.py:106
  194.0 2.2 sum_packed.1
  196.2 2.0 collective-permute-start.37
  198.2 1.5 collective-permute-start.38
  199.7 1.8 sum_parts.1.refs_0_
  202.6 6.7 %collective-permute-done.36.refs_1_ = bf16[112,768]{1,0:T(8,128)(2,1)S(1)} collective-permute-done((bf16[112,768]{1,0:T(8,128)(2,1)}, bf16[112,768]{1,0:T(8,128)(2,1)S(1)}, u32[]{:S(2)}, u32[]{:S(2)}) %collective-permute-start.36) | collective-permute-done | bytes 172064 | tf_op jit(solution)/shard_map/ppermute | solution.py:73
  209.3 2.1 collective-permute-done.37.refs_2_
  212.9 2.0 unpack_sums.1.refs_0_
  216.6 6.4 %collective-permute-done.39.refs_1_ = bf16[160,768]{1,0:T(8,128)(2,1)S(1)} collective-permute-done((bf16[160,768]{1,0:T(8,128)(2,1)}, bf16[160,768]{1,0:T(8,128)(2,1)S(1)}, u32[]{:S(2)}, u32[]{:S(2)}) %collective-permute-start.39) | collective-permute-done | bytes 245792 | tf_op jit(solution)/shard_map/ppermute | solution.py:73
  223.5 2.6 %unsort_rows.1 = (f32[8,32,768]{2,1,0:T(8,128)}, f32[8,32,768]{2,1,0:T(8,128)}) custom-call(s32[6]{0:T(128)} %stack.27.place_ref, s32[1,5]{1,0:T(1,128)} %doc_ref.3, bf16[128,768]{1,0:T(8,128)(2,1)} %copy-done.29, bf16[128,768]{1,0:T(8,128)(2,1)} %copy-done.30, bf16[128,768]{1,0:T(8,128)(2,1)} %copy-done.31, bf16[128,768]{1,0:T(8,128)(2,1)} %copy-done.32), custom_call_target="tpu_custom_call" | custom-call | bytes 2359340 | tf_op jit(solution)/shard_map/unsort_rows/pallas_call | solution.py:120
  227.5 2.6 %join_heads.1 = (f32[96,2304]{1,0:T(8,128)}, f32[96,768]{1,0:T(8,128)}, f32[96]{0:T(128)}, f32[96]{0:T(128)}, f32[288]{0:T(512)}, /*index=5*/f32[96]{0:T(128)}, ...) custom-call(s32[6]{0:T(128)} %stack.27.place_ref, bf16[160,768]{1,0:T(8,128)(2,1)} %unpack_sums.1.refs_0_, ...), custom_call_target="tpu_custom_call" | custom-call | bytes 2167704 | tf_op jit(solution)/shard_map/join_heads/pallas_call | solution.py:120
  231.6 3.1 %join_shares.1 = (f32[96,3072]{1,0:T(8,128)}, f32[384,768]{1,0:T(8,128)}) custom-call(s32[6]{0:T(128)} %stack.27.place_ref, bf16[192,768]{1,0:T(8,128)(2,1)} %sum_parts.1.refs_0_, bf16[192,768]{1,0:T(8,128)(2,1)} %copy-done.23, bf16[192,768]{1,0:T(8,128)(2,1)} %copy-done.24, bf16[192,768]{1,0:T(8,128)(2,1)} %copy-done.25), custom_call_target="tpu_custom_call" | custom-call | bytes 3538968 | tf_op jit(solution)/shard_map/join_shares/pallas_call | solution.py:120
  (201 shorter events, 40.4 us)
Async XLA Ops:
  0.7 34.8 %collective-permute-start.4 = (s32[1,5]{1,0:T(1,128)}, s32[1,5]{1,0:T(1,128)S(1)}, u32[]{:S(2)}, u32[]{:S(2)}) collective-permute-start(s32[1,5]{1,0:T(1,128)} %doc_ref.3), channel_id=1, source_target_pairs={{0,8},{8,0},{1,9},{9,1},{2,10},{10,2},{3,11},{11,3},{4,12},{12,4},... | collective-permute-start | bytes 68 | tf_op jit(solution)/shard_map/ppermute | solution.py:73
  4.2 10.2 %collective-permute-start = (bf16[128,768]{1,0:T(8,128)(2,1)}, bf16[128,768]{1,0:T(8,128)(2,1)S(1)}, u32[]{:S(2)}, u32[]{:S(2)}) collective-permute-start(bf16[128,768]{1,0:T(8,128)(2,1)} %get-tuple-element.139), channel_id=1, source_target_pairs={{0,0},{1,4},{2,8},{3,12},{4,2},{5,6},{6,10},{7,14},{8,1},{9,5},{10... | collective-permute-start | bytes 589832 | tf_op jit(solution)/shard_map/ppermute | solution.py:101
  7.3 11.1 %collective-permute-start.1 = (bf16[128,768]{1,0:T(8,128)(2,1)}, bf16[128,768]{1,0:T(8,128)(2,1)S(1)}, u32[]{:S(2)}, u32[]{:S(2)}) collective-permute-start(bf16[128,768]{1,0:T(8,128)(2,1)} %get-tuple-element.140), channel_id=1, source_target_pairs={{0,4},{1,0},{2,12},{3,8},{4,6},{5,2},{6,14},{7,10},{8,5},{9,1},{10... | collective-permute-start | bytes 589832 | tf_op jit(solution)/shard_map/ppermute | solution.py:101
  18.4 17.0 %collective-permute-start.6 = (bf16[256,768]{1,0:T(8,128)(2,1)S(1)}, bf16[256,768]{1,0:T(8,128)(2,1)S(1)}, u32[]{:S(2)}, u32[]{:S(2)}) collective-permute-start(bf16[256,768]{1,0:T(8,128)(2,1)S(1)} %constant_dynamic-update-slice_fusion.refs_0_.refs_4_.refs_3_), channel_id=1, source_target_pairs={{0,2},{2,0},{4,6},{6,4},{8,10},{10,8},{12,14},{14,12},{1,3},{3,1},... | collective-permute-start | bytes 1179656 | tf_op jit(solution)/shard_map/ppermute | solution.py:84
  20.5 15.8 %collective-permute-start.5 = (bf16[256,768]{1,0:T(8,128)(2,1)S(1)}, bf16[256,768]{1,0:T(8,128)(2,1)S(1)}, u32[]{:S(2)}, u32[]{:S(2)}) collective-permute-start(bf16[256,768]{1,0:T(8,128)(2,1)S(1)} %constant_dynamic-update-slice_fusion.refs_0_.refs_4_.refs_3_), channel_id=1, source_target_pairs={{0,8},{2,10},{4,12},{6,14},{8,0},{10,2},{12,4},{14,6},{1,9},{3,11}... | collective-permute-start | bytes 1179656 | tf_op jit(solution)/shard_map/ppermute | solution.py:84
  22.5 13.5 %collective-permute-start.2 = (bf16[128,768]{1,0:T(8,128)(2,1)}, bf16[128,768]{1,0:T(8,128)(2,1)S(1)}, u32[]{:S(2)}, u32[]{:S(2)}) collective-permute-start(bf16[128,768]{1,0:T(8,128)(2,1)} %get-tuple-element.143), channel_id=1, source_target_pairs={{0,0},{1,4},{2,8},{3,12},{4,2},{5,6},{6,10},{7,14},{8,1},{9,5},{10... | collective-permute-start | bytes 589832 | tf_op jit(solution)/shard_map/ppermute | solution.py:101
  26.2 10.0 %collective-permute-start.3 = (bf16[128,768]{1,0:T(8,128)(2,1)}, bf16[128,768]{1,0:T(8,128)(2,1)S(1)}, u32[]{:S(2)}, u32[]{:S(2)}) collective-permute-start(bf16[128,768]{1,0:T(8,128)(2,1)} %get-tuple-element.144), channel_id=1, source_target_pairs={{0,4},{1,0},{2,12},{3,8},{4,6},{5,2},{6,14},{7,10},{8,5},{9,1},{10... | collective-permute-start | bytes 589832 | tf_op jit(solution)/shard_map/ppermute | solution.py:101
  35.4 1.8 collective-permute-start.7
  48.9 6.6 %collective-permute-start.10 = (bf16[256,192]{1,0:T(8,128)(2,1)}, bf16[256,192]{1,0:T(8,128)(2,1)S(1)}, u32[]{:S(2)}, u32[]{:S(2)}) collective-permute-start(bf16[256,192]{1,0:T(8,128)(2,1)} %get-tuple-element.157), channel_id=1, source_target_pairs={{0,10},{2,8},{4,14},{6,12},{8,2},{10,0},{12,6},{14,4},{1,11},{3,9}... | collective-permute-start | bytes 294920 | tf_op jit(solution)/shard_map/ppermute | solution.py:84
  50.1 5.4 %collective-permute-start.8 = (bf16[256,192]{1,0:T(8,128)(2,1)}, bf16[256,192]{1,0:T(8,128)(2,1)S(1)}, u32[]{:S(2)}, u32[]{:S(2)}) collective-permute-start(bf16[256,192]{1,0:T(8,128)(2,1)} %get-tuple-element.155), channel_id=1, source_target_pairs={{0,8},{2,10},{4,12},{6,14},{8,0},{10,2},{12,4},{14,6},{1,9},{3,11}... | collective-permute-start | bytes 294920 | tf_op jit(solution)/shard_map/ppermute | solution.py:84
  50.5 7.6 %collective-permute-start.9 = (bf16[256,192]{1,0:T(8,128)(2,1)}, bf16[256,192]{1,0:T(8,128)(2,1)S(1)}, u32[]{:S(2)}, u32[]{:S(2)}) collective-permute-start(bf16[256,192]{1,0:T(8,128)(2,1)} %get-tuple-element.156), channel_id=1, source_target_pairs={{0,2},{2,0},{4,6},{6,4},{8,10},{10,8},{12,14},{14,12},{1,3},{3,1},... | collective-permute-start | bytes 294920 | tf_op jit(solution)/shard_map/ppermute | solution.py:84
  53.5 12.7 %collective-permute-start.12 = (bf16[256,768]{1,0:T(8,128)(2,1)S(1)}, bf16[256,768]{1,0:T(8,128)(2,1)S(1)}, u32[]{:S(2)}, u32[]{:S(2)}) collective-permute-start(bf16[256,768]{1,0:T(8,128)(2,1)S(1)} %constant_dynamic-update-slice_fusion.2.refs_2_.refs_12_.refs_7_), channel_id=1, source_target_pairs={{0,8},{8,0},{1,9},{9,1},{2,10},{10,2},{3,11},{11,3},{4,12},{12,4},... | collective-permute-start | bytes 1179656 | tf_op jit(solution)/shard_map/ppermute | solution.py:73
  54.2 10.7 %collective-permute-start.16 = (bf16[256,768]{1,0:T(8,128)(2,1)S(1)}, bf16[256,768]{1,0:T(8,128)(2,1)S(1)}, u32[]{:S(2)}, u32[]{:S(2)}) collective-permute-start(bf16[256,768]{1,0:T(8,128)(2,1)S(1)} %constant_dynamic-update-slice_fusion.2.refs_2_.refs_12_.refs_7_), channel_id=1, source_target_pairs={{0,16},{16,0},{1,17},{17,1},{2,18},{18,2},{3,19},{19,3},{4,20},{20... | collective-permute-start | bytes 1179656 | tf_op jit(solution)/shard_map/ppermute | solution.py:73
  61.9 4.3 %collective-permute-start.11 = (bf16[256,768]{1,0:T(8,128)(2,1)}, bf16[256,768]{1,0:T(8,128)(2,1)S(1)}, u32[]{:S(2)}, u32[]{:S(2)}) collective-permute-start(bf16[256,768]{1,0:T(8,128)(2,1)} %get-tuple-element.158.refs_0_), channel_id=1, source_target_pairs={{0,8},{8,0},{1,9},{9,1},{2,10},{10,2},{3,11},{11,3},{4,12},{12,4},... | collective-permute-start | bytes 1179656 | tf_op jit(solution)/shard_map/ppermute | solution.py:73
  61.9 14.3 %collective-permute-start.14 = (bf16[256,768]{1,0:T(8,128)(2,1)}, bf16[256,768]{1,0:T(8,128)(2,1)S(1)}, u32[]{:S(2)}, u32[]{:S(2)}) collective-permute-start(bf16[256,768]{1,0:T(8,128)(2,1)} %get-tuple-element.158.refs_0_), channel_id=1, source_target_pairs={{0,16},{16,0},{1,17},{17,1},{2,18},{18,2},{3,19},{19,3},{4,20},{20... | collective-permute-start | bytes 1179656 | tf_op jit(solution)/shard_map/ppermute | solution.py:73
  65.0 11.3 %collective-permute-start.17 = (bf16[256,768]{1,0:T(8,128)(2,1)S(1)}, bf16[256,768]{1,0:T(8,128)(2,1)S(1)}, u32[]{:S(2)}, u32[]{:S(2)}) collective-permute-start(bf16[256,768]{1,0:T(8,128)(2,1)S(1)} %collective-permute-done.16.refs_2_.refs_14_), channel_id=1, source_target_pairs={{0,8},{8,0},{1,9},{9,1},{2,10},{10,2},{3,11},{11,3},{4,12},{12,4},... | collective-permute-start | bytes 1179656 | tf_op jit(solution)/shard_map/ppermute | solution.py:73
  76.2 1.8 collective-permute-start.15
  84.5 1.9 collective-permute-start.18
  84.6 14.0 %collective-permute-start.21 = (bf16[256,768]{1,0:T(8,128)(2,1)S(1)}, bf16[256,768]{1,0:T(8,128)(2,1)S(1)}, u32[]{:S(2)}, u32[]{:S(2)}) collective-permute-start(bf16[256,768]{1,0:T(8,128)(2,1)S(1)} %copy-done.48), channel_id=1, source_target_pairs={{0,8},{8,0},{1,9},{9,1},{2,10},{10,2},{3,11},{11,3},{4,12},{12,4},... | collective-permute-start | bytes 1179656 | tf_op jit(solution)/shard_map/ppermute | solution.py:73
  87.5 11.1 %collective-permute-start.22 = (bf16[256,768]{1,0:T(8,128)(2,1)S(1)}, bf16[256,768]{1,0:T(8,128)(2,1)S(1)}, u32[]{:S(2)}, u32[]{:S(2)}) collective-permute-start(bf16[256,768]{1,0:T(8,128)(2,1)S(1)} %add_convert_fusion.1), channel_id=1, source_target_pairs={{0,16},{16,0},{1,17},{17,1},{2,18},{18,2},{3,19},{19,3},{4,20},{20... | collective-permute-start | bytes 1179656 | tf_op jit(solution)/shard_map/ppermute | solution.py:73
  105.1 2.2 collective-permute-start.24
  105.6 5.4 %collective-permute-start.25 = (bf16[256,192]{1,0:T(8,128)(2,1)}, bf16[256,192]{1,0:T(8,128)(2,1)}, u32[]{:S(2)}, u32[]{:S(2)}) collective-permute-start(bf16[256,192]{1,0:T(8,128)(2,1)} %get-tuple-element.197), channel_id=1, source_target_pairs={{0,2},{2,0},{4,6},{6,4},{8,10},{10,8},{12,14},{14,12},{1,3},{3,1},... | collective-permute-start | bytes 294920 | tf_op jit(solution)/shard_map/ppermute | solution.py:84
  105.6 8.4 %collective-permute-start.26 = (bf16[256,192]{1,0:T(8,128)(2,1)}, bf16[256,192]{1,0:T(8,128)(2,1)}, u32[]{:S(2)}, u32[]{:S(2)}) collective-permute-start(bf16[256,192]{1,0:T(8,128)(2,1)} %get-tuple-element.198), channel_id=1, source_target_pairs={{0,10},{2,8},{4,14},{6,12},{8,2},{10,0},{12,6},{14,4},{1,11},{3,9}... | collective-permute-start | bytes 294920 | tf_op jit(solution)/shard_map/ppermute | solution.py:84
  114.0 54.2 %all-to-all-start = ((bf16[4,2,192,768]{3,2,1,0:T(8,128)(2,1)}), bf16[4,2,192,768]{3,2,1,0:T(8,128)(2,1)S(1)}, u32[]{:S(2)}, u32[]{:S(2)}) async-start(bf16[4,2,192,768]{3,2,1,0:T(8,128)(2,1)} %feed_forward_weights.1), calls=%async_computation | async-start | bytes 4718592 | tf_op jit(solution)/shard_map/all_to_all | solution.py:1084
  118.0 20.9 %collective-permute-start.13 = (bf16[256,768]{1,0:T(8,128)(2,1)S(1)}, bf16[256,768]{1,0:T(8,128)(2,1)S(1)}, u32[]{:S(2)}, u32[]{:S(2)}) collective-permute-start(bf16[256,768]{1,0:T(8,128)(2,1)S(1)} %copy-done.45), channel_id=1, source_target_pairs={{0,8},{8,0},{1,9},{9,1},{2,10},{10,2},{3,11},{11,3},{4,12},{12,4},... | collective-permute-start | bytes 1179656 | tf_op jit(solution)/shard_map/ppermute | solution.py:73
  118.7 20.2 %collective-permute-start.19 = (bf16[256,768]{1,0:T(8,128)(2,1)}, bf16[256,768]{1,0:T(8,128)(2,1)S(1)}, u32[]{:S(2)}, u32[]{:S(2)}) collective-permute-start(bf16[256,768]{1,0:T(8,128)(2,1)} %get-tuple-element.181), channel_id=1, source_target_pairs={{0,16},{8,24},{16,0},{24,8},{1,17},{9,25},{17,1},{25,9},{2,18},{10... | collective-permute-start | bytes 1179656 | tf_op jit(solution)/shard_map/ppermute | solution.py:915
  119.8 19.2 %collective-permute-start.20 = (bf16[256,768]{1,0:T(8,128)(2,1)}, bf16[256,768]{1,0:T(8,128)(2,1)S(1)}, u32[]{:S(2)}, u32[]{:S(2)}) collective-permute-start(bf16[256,768]{1,0:T(8,128)(2,1)} %get-tuple-element.182), channel_id=1, source_target_pairs={{0,24},{8,16},{16,8},{24,0},{1,25},{9,17},{17,9},{25,1},{2,26},{10... | collective-permute-start | bytes 1179656 | tf_op jit(solution)/shard_map/ppermute | solution.py:915
  120.4 18.6 %collective-permute-start.23 = (bf16[768,384]{1,0:T(8,128)(2,1)S(1)}, bf16[768,384]{1,0:T(8,128)(2,1)S(1)}, u32[]{:S(2)}, u32[]{:S(2)}) collective-permute-start(bf16[768,384]{1,0:T(8,128)(2,1)S(1)} %copy-done.44), channel_id=1, source_target_pairs={{0,8},{8,0},{1,9},{9,1},{2,10},{10,2},{3,11},{11,3},{4,12},{12,4},... | collective-permute-start | bytes 1769480 | tf_op jit(solution)/shard_map/ppermute | solution.py:73
  144.1 14.8 %collective-permute-start.34 = (bf16[8,48,768]{2,1,0:T(8,128)(2,1)}, bf16[8,48,768]{2,1,0:T(8,128)(2,1)S(1)}, u32[]{:S(2)}, u32[]{:S(2)}) collective-permute-start(bf16[8,48,768]{2,1,0:T(8,128)(2,1)} %get-tuple-element.225), channel_id=1, source_target_pairs={{0,16},{16,0},{1,17},{17,1},{2,18},{18,2},{3,19},{19,3},{4,20},{20... | collective-permute-start | bytes 1769480 | tf_op jit(solution)/shard_map/ppermute | solution.py:73
  145.2 17.6 %collective-permute-start.30 = (bf16[256,768]{1,0:T(8,128)(2,1)S(1)}, bf16[256,768]{1,0:T(8,128)(2,1)S(1)}, u32[]{:S(2)}, u32[]{:S(2)}) collective-permute-start(bf16[256,768]{1,0:T(8,128)(2,1)S(1)} %copy-done.47), channel_id=1, source_target_pairs={{0,8},{2,10},{4,12},{6,14},{8,0},{10,2},{12,4},{14,6},{1,9},{3,11}... | collective-permute-start | bytes 1179656 | tf_op jit(solution)/shard_map/ppermute | solution.py:84
  150.9 27.7 %collective-permute-start.29 = (bf16[256,768]{1,0:T(8,128)(2,1)}, bf16[256,768]{1,0:T(8,128)(2,1)S(1)}, u32[]{:S(2)}, u32[]{:S(2)}) collective-permute-start(bf16[256,768]{1,0:T(8,128)(2,1)} %get-tuple-element.215), channel_id=1, source_target_pairs={{0,8},{2,10},{4,12},{6,14},{8,0},{10,2},{12,4},{14,6},{1,9},{3,11}... | collective-permute-start | bytes 1179656 | tf_op jit(solution)/shard_map/ppermute | solution.py:84
  162.7 30.4 %collective-permute-start.35 = (bf16[4,112,768]{2,1,0:T(8,128)(2,1)}, bf16[4,112,768]{2,1,0:T(8,128)(2,1)S(1)}, u32[]{:S(2)}, u32[]{:S(2)}) collective-permute-start(bf16[4,112,768]{2,1,0:T(8,128)(2,1)} %get-tuple-element.233), channel_id=1, source_target_pairs={{0,1},{1,0},{2,3},{3,2},{4,5},{5,4},{6,7},{7,6},{8,9},{9,8},{10,11... | collective-permute-start | bytes 2064392 | tf_op jit(solution)/shard_map/ppermute | solution.py:73
  163.7 16.2 %collective-permute-start.31 = (bf16[256,768]{1,0:T(8,128)(2,1)}, bf16[256,768]{1,0:T(8,128)(2,1)}, u32[]{:S(2)}, u32[]{:S(2)}) collective-permute-start(bf16[256,768]{1,0:T(8,128)(2,1)} %add_convert_fusion), channel_id=1, source_target_pairs={{0,2},{2,0},{4,6},{6,4},{8,10},{10,8},{12,14},{14,12},{1,3},{3,1},... | collective-permute-start | bytes 1179656 | tf_op jit(solution)/shard_map/ppermute | solution.py:84
  172.3 25.9 %collective-permute-start.42 = (bf16[192,768]{1,0:T(8,128)(2,1)}, bf16[192,768]{1,0:T(8,128)(2,1)S(1)}, u32[]{:S(2)}, u32[]{:S(2)}) collective-permute-start(bf16[192,768]{1,0:T(8,128)(2,1)} %get-tuple-element.255), channel_id=1, source_target_pairs={{0,1},{1,0},{2,3},{3,2},{4,5},{5,4},{6,7},{7,6},{8,9},{9,8},{10,11... | collective-permute-start | bytes 884744 | tf_op jit(solution)/shard_map/ppermute | solution.py:73
  172.3 15.4 %collective-permute-start.27 = (bf16[128,768]{1,0:T(8,128)(2,1)S(1)}, bf16[128,768]{1,0:T(8,128)(2,1)S(1)}, u32[]{:S(2)}, u32[]{:S(2)}) collective-permute-start(bf16[128,768]{1,0:T(8,128)(2,1)S(1)} %copy-done.52), channel_id=1, source_target_pairs={{0,0},{4,1},{8,2},{12,3},{2,4},{6,5},{10,6},{14,7},{1,8},{5,9},{9,... | collective-permute-start | bytes 589832 | tf_op jit(solution)/shard_map/ppermute | solution.py:106
  178.7 14.5 %collective-permute-start.28 = (bf16[128,768]{1,0:T(8,128)(2,1)S(1)}, bf16[128,768]{1,0:T(8,128)(2,1)S(1)}, u32[]{:S(2)}, u32[]{:S(2)}) collective-permute-start(bf16[128,768]{1,0:T(8,128)(2,1)S(1)} %copy-done.51), channel_id=1, source_target_pairs={{4,0},{0,1},{12,2},{8,3},{6,4},{2,5},{14,6},{10,7},{5,8},{1,9},{13... | collective-permute-start | bytes 589832 | tf_op jit(solution)/shard_map/ppermute | solution.py:106
  182.8 18.7 %collective-permute-start.32 = (bf16[128,768]{1,0:T(8,128)(2,1)}, bf16[128,768]{1,0:T(8,128)(2,1)S(1)}, u32[]{:S(2)}, u32[]{:S(2)}) collective-permute-start(bf16[128,768]{1,0:T(8,128)(2,1)} %get-tuple-element.219), channel_id=1, source_target_pairs={{0,0},{4,1},{8,2},{12,3},{2,4},{6,5},{10,6},{14,7},{1,8},{5,9},{9,... | collective-permute-start | bytes 589832 | tf_op jit(solution)/shard_map/ppermute | solution.py:106
  187.6 35.8 %copy-start.29 = (bf16[128,768]{1,0:T(8,128)(2,1)}, bf16[128,768]{1,0:T(8,128)(2,1)S(1)}, u32[]{:S(2)}) copy-start(bf16[128,768]{1,0:T(8,128)(2,1)S(1)} %collective-permute-done.27.refs_0_) | copy-start | bytes 589828
  187.7 14.9 %collective-permute-start.33 = (bf16[128,768]{1,0:T(8,128)(2,1)}, bf16[128,768]{1,0:T(8,128)(2,1)S(1)}, u32[]{:S(2)}, u32[]{:S(2)}) collective-permute-start(bf16[128,768]{1,0:T(8,128)(2,1)} %get-tuple-element.220), channel_id=1, source_target_pairs={{4,0},{0,1},{12,2},{8,3},{6,4},{2,5},{14,6},{10,7},{5,8},{1,9},{13... | collective-permute-start | bytes 589832 | tf_op jit(solution)/shard_map/ppermute | solution.py:106
  196.2 13.1 %collective-permute-start.36 = (bf16[112,768]{1,0:T(8,128)(2,1)}, bf16[112,768]{1,0:T(8,128)(2,1)S(1)}, u32[]{:S(2)}, u32[]{:S(2)}) collective-permute-start(bf16[112,768]{1,0:T(8,128)(2,1)} %get-tuple-element.237), channel_id=1, source_target_pairs={{0,2},{2,4},{4,6},{6,0},{1,3},{3,5},{5,7},{7,1},{8,10},{10,12},{12... | collective-permute-start | bytes 516104 | tf_op jit(solution)/shard_map/ppermute | solution.py:73
  196.2 15.2 %collective-permute-start.37 = (bf16[112,768]{1,0:T(8,128)(2,1)}, bf16[112,768]{1,0:T(8,128)(2,1)S(1)}, u32[]{:S(2)}, u32[]{:S(2)}) collective-permute-start(bf16[112,768]{1,0:T(8,128)(2,1)} %get-tuple-element.238), channel_id=1, source_target_pairs={{0,4},{2,6},{4,0},{6,2},{1,5},{3,7},{5,1},{7,3},{8,12},{10,14},{12... | collective-permute-start | bytes 516104 | tf_op jit(solution)/shard_map/ppermute | solution.py:73
  198.2 14.1 %collective-permute-start.38 = (bf16[112,768]{1,0:T(8,128)(2,1)}, bf16[112,768]{1,0:T(8,128)(2,1)S(1)}, u32[]{:S(2)}, u32[]{:S(2)}) collective-permute-start(bf16[112,768]{1,0:T(8,128)(2,1)} %get-tuple-element.239), channel_id=1, source_target_pairs={{0,6},{2,0},{4,2},{6,4},{1,7},{3,1},{5,3},{7,5},{8,14},{10,8},{12,... | collective-permute-start | bytes 516104 | tf_op jit(solution)/shard_map/ppermute | solution.py:73
  201.5 14.5 %collective-permute-start.43 = (bf16[192,768]{1,0:T(8,128)(2,1)}, bf16[192,768]{1,0:T(8,128)(2,1)S(1)}, u32[]{:S(2)}, u32[]{:S(2)}) collective-permute-start(bf16[192,768]{1,0:T(8,128)(2,1)} %sum_parts.1.refs_0_), channel_id=1, source_target_pairs={{0,16},{16,0},{1,17},{17,1},{2,18},{18,2},{3,19},{19,3},{4,20},{20... | collective-permute-start | bytes 884744 | tf_op jit(solution)/shard_map/ppermute | solution.py:73
  214.9 8.1 %collective-permute-start.39 = (bf16[160,768]{1,0:T(8,128)(2,1)}, bf16[160,768]{1,0:T(8,128)(2,1)S(1)}, u32[]{:S(2)}, u32[]{:S(2)}) collective-permute-start(bf16[160,768]{1,0:T(8,128)(2,1)} %unpack_sums.1.refs_0_), channel_id=1, source_target_pairs={{0,16},{16,0},{1,17},{17,1},{2,18},{18,2},{3,19},{19,3},{4,20},{20... | collective-permute-start | bytes 737288 | tf_op jit(solution)/shard_map/ppermute | solution.py:73
  216.0 14.1 %collective-permute-start.44 = (bf16[192,768]{1,0:T(8,128)(2,1)}, bf16[192,768]{1,0:T(8,128)(2,1)S(1)}, u32[]{:S(2)}, u32[]{:S(2)}) collective-permute-start(bf16[192,768]{1,0:T(8,128)(2,1)} %sum_parts.1.refs_0_), channel_id=1, source_target_pairs={{0,8},{8,0},{1,9},{9,1},{2,10},{10,2},{3,11},{11,3},{4,12},{12,4},... | collective-permute-start | bytes 884744 | tf_op jit(solution)/shard_map/ppermute | solution.py:73
  216.0 14.1 %collective-permute-start.45 = (bf16[192,768]{1,0:T(8,128)(2,1)S(1)}, bf16[192,768]{1,0:T(8,128)(2,1)S(1)}, u32[]{:S(2)}, u32[]{:S(2)}) collective-permute-start(bf16[192,768]{1,0:T(8,128)(2,1)S(1)} %collective-permute-done.43.refs_1_), channel_id=1, source_target_pairs={{0,8},{8,0},{1,9},{9,1},{2,10},{10,2},{3,11},{11,3},{4,12},{12,4},... | collective-permute-start | bytes 884744 | tf_op jit(solution)/shard_map/ppermute | solution.py:73
  216.5 9.6 %collective-permute-start.40 = (bf16[160,768]{1,0:T(8,128)(2,1)}, bf16[160,768]{1,0:T(8,128)(2,1)S(1)}, u32[]{:S(2)}, u32[]{:S(2)}) collective-permute-start(bf16[160,768]{1,0:T(8,128)(2,1)} %unpack_sums.1.refs_0_), channel_id=1, source_target_pairs={{0,8},{8,0},{1,9},{9,1},{2,10},{10,2},{3,11},{11,3},{4,12},{12,4},... | collective-permute-start | bytes 737288 | tf_op jit(solution)/shard_map/ppermute | solution.py:73
  223.0 3.1 %collective-permute-start.41 = (bf16[160,768]{1,0:T(8,128)(2,1)S(1)}, bf16[160,768]{1,0:T(8,128)(2,1)S(1)}, u32[]{:S(2)}, u32[]{:S(2)}) collective-permute-start(bf16[160,768]{1,0:T(8,128)(2,1)S(1)} %collective-permute-done.39.refs_1_), channel_id=1, source_target_pairs={{0,8},{8,0},{1,9},{9,1},{2,10},{10,2},{3,11},{11,3},{4,12},{12,4},... | collective-permute-start | bytes 737288 | tf_op jit(solution)/shard_map/ppermute | solution.py:73
  (53 other events, 382.4 us)

commit v3 on v2

--- a/solution.py
+++ b/solution.py
@@ -42,8 +42,9 @@
         self.gx = n_grp // 2
         self.scale = self.head ** (-0.5)
         band, share = width // n_ctx, hidden // (n_ctx * n_grp)
-        self.aligned = band % 32 == 0 and share % 32 == 0 and share * n_ctx == width
-        self.packed = band % (32 * self.gx // 2) == 0 and 3 * self.lanes == width
+        whole = self.groups * self.used == width
+        self.aligned = whole and band % 32 == 0 and share % 32 == 0 and share * n_ctx == width
+        self.packed = whole and band % (32 * self.gx // 2) == 0 and 3 * self.lanes == width
 
 
 def peer(sz, quarter, at, sign):
@@ -285,14 +286,20 @@
 
 def attend_backward(sz, place, docs, saved, w_sel, grads):
     lw = sz.lanes
-    qkv, _, hat, lse, att, carry = saved
-
-    def body(place_ref, doc_ref, qkv_ref, hat_ref, lse_ref, att_ref, carry_ref, w_ref, *refs):
+    qkv, normed, hat, lse, att, carry = saved
+    band = sz.width // sz.n_ctx
+    share = band // sz.gx
+    n_sel = sz.gx if sz.packed else 1
+
+    def body(place_ref, doc_ref, qkv_ref, normed_ref, hat_ref, lse_ref, att_ref, carry_ref, w_ref, *refs):
         grad_refs = refs[: sz.groups]
         outs = refs[sz.groups :]
-        dqkv_ref, sums_ref, lnsum_ref = outs[:3]
-        dnorm_refs = outs[3 : 3 + sz.groups]
-        dout, dk_sum, dv_sum, behind = outs[3 + sz.groups :]
+        sums_ref, lnsum_ref = outs[:2]
+        dnorm_refs = outs[2 : 2 + sz.groups]
+        sel_refs = outs[2 + sz.groups : 2 + sz.groups + n_sel]
+        rest = outs[2 + sz.groups + n_sel :]
+        dout, dk_sum, dv_sum, behind = rest[:4]
+        dqkv_ref = rest[4] if sz.packed else sel_refs[0]
         quarter = place_ref[QUARTER]
         long_part = part_is_long(sz, doc_ref, place_ref[PART])
         dout[...] = jnp.zeros_like(dout)
@@ -351,19 +358,37 @@
                 gain_sum += jnp.sum(dnorm * hat_ref[at, :].astype(F32), axis=0, keepdims=True)
         lnsum_ref[0:1, :] = gain_sum
         lnsum_ref[1:2, :] = bias_sum
-
-    outs = [((sz.span, 3 * lw), BF16), ((1, 3 * lw), F32), ((2, sz.width), F32)]
+        if sz.packed:
+            held = rest[5]
+            held[...] = dot_tn(normed_ref[...], dqkv_ref[...]).astype(BF16)
+            for k in range(sz.gx):
+                to = (place_ref[GX] + k) % sz.gx
+                for i in range(sz.n_ctx):
+                    at = pl.multiple_of(i * band + to * share, 16)
+                    sel_refs[k][i] = held[pl.ds(at, share), :]
+
+    outs = [((1, 3 * lw), F32), ((2, sz.width), F32)]
     outs += [((sz.rows, sz.width), BF16)] * sz.groups
+    if sz.packed:
+        outs += [((sz.n_ctx, share, 3 * lw), BF16)] * sz.gx
+    else:
+        outs += [((sz.span, 3 * lw), BF16)]
     scratch = [
         pltpu.VMEM((sz.span, lw), BF16),
         pltpu.VMEM((sz.span, lw), F32),
         pltpu.VMEM((sz.span, lw), F32),
         pltpu.VMEM((8, sz.span), F32),
     ]
-    out = whole_call(
-        body, outs, 2, (place, docs, qkv, hat, lse, att, carry, w_sel, *grads), "attend_backward", scratch, 17e9
-    )
-    return out[0], out[1], out[2], out[3:]
+    if sz.packed:
+        scratch += [pltpu.VMEM((sz.span, 3 * lw), BF16), pltpu.VMEM((sz.width, 3 * lw), BF16)]
+    args = (place, docs, qkv, normed, hat, lse, att, carry, w_sel, *grads)
+    out = whole_call(body, outs, 2, args, "attend_backward", scratch)
+    sel = out[2 + sz.groups :]
+    if not sz.packed:
+        grad = dot_tn(normed, sel[0]).astype(BF16).reshape(sz.n_ctx, sz.gx, share, 3 * lw)
+        grad = jnp.roll(grad, -place[GX], axis=1)
+        sel = [grad[:, k] for k in range(sz.gx)]
+    return out[0], out[1], out[2 : 2 + sz.groups], sel
 
 
 def project_out(sz, place, att, tokens, out_weight, out_bias, gain, bias):
@@ -718,35 +743,6 @@
     held = jnp.stack(values).reshape((2, sz.gx) + values[0].shape)
     held = jnp.roll(held[:, ::-1], place[GX] + 1, axis=1)
     return jnp.roll(held, place[CORE], axis=0).swapaxes(0, 1).astype(F32)
-
-
-def qkv_weights(sz, place, normed, dqkv):
-    band = sz.width // sz.n_ctx
-    rows = band // sz.gx
-    w3 = 3 * sz.lanes
-
-    if not sz.packed:
-        grad = dot_tn(normed, dqkv).astype(BF16).reshape(sz.n_ctx, sz.gx, rows, w3)
-        grad = jnp.roll(grad, -place[GX], axis=1)
-        return [grad[:, k] for k in range(sz.gx)]
-
-    def body(place_ref, normed_ref, dqkv_ref, *refs):
-        held = refs[-1]
-        held[...] = dot_tn(normed_ref[...], dqkv_ref[...]).astype(BF16)
-        for k in range(sz.gx):
-            to = (place_ref[GX] + k) % sz.gx
-            for i in range(sz.n_ctx):
-                at = pl.multiple_of(i * band + to * rows, 16)
-                refs[k][i] = held[pl.ds(at, rows), :]
-
-    return whole_call(
-        body,
-        [((sz.n_ctx, rows, w3), BF16)] * sz.gx,
-        1,
-        (place, normed, dqkv),
-        "qkv_weights",
-        [pltpu.VMEM((sz.width, w3), BF16)],
-    )
 
 
 def join_heads(sz, place, pieces, rows, n_tail):
@@ -1086,8 +1082,8 @@
 
     out_terms = [d.reshape(n_ctx, band, half) for d in (d_out[0], shift(d_out[1], "core", 2, 1))]
 
-    dqkv, qkv_sum, ln1_sums, dnorm_out = attend_backward(sz, place, docs, saved, w_sel, datt)
-    dnorm_out, dqkv = after((mixed, out_terms), (dnorm_out, dqkv))
+    qkv_sum, ln1_sums, dnorm_out, sel_sent = attend_backward(sz, place, docs, saved, w_sel, datt)
+    dnorm_out, sel_sent = after((mixed, out_terms), (dnorm_out, sel_sent))
     dnorm = [dnorm_out[0], to_peer(sz, dnorm_out[1], 1)]
     for k in range(1, sz.half):
         both = dnorm_out[2 * k].astype(F32) + to_peer(sz, dnorm_out[2 * k + 1], 1).astype(F32)
@@ -1095,10 +1091,9 @@
         dnorm.append(to_peer(sz, both, 2 * k))
     grad_parts = finish_tokens(sz, dnorm, tok_rows, grad_middle, gain1)
     grad_back = from_owner(sz, grad_parts)
-    out_parts = finish_middle(sz, after(dqkv, mixed), middle, vector(proj_bias))
-
-    sel_terms = qkv_weights(sz, place, saved[1], dqkv)
-    sel_terms = [sel_terms[0]] + [shift(sel_terms[k], "gx", sz.gx, k) for k in range(1, sz.gx)]
+    out_parts = finish_middle(sz, after(sel_sent, mixed), middle, vector(proj_bias))
+
+    sel_terms = [sel_sent[0]] + [shift(sel_sent[k], "gx", sz.gx, k) for k in range(1, sz.gx)]
     tail = pack_vectors(sz, place, ln1_sums, qkv_sum, mid_sums, [fc_sum_n, fc_sum_f])
     n_tail = tail.shape[1]
     pieces = pack_sums(sz, place, sel_terms, out_terms, after(out_parts, tail))
@@ -1107,8 +1102,8 @@
     blocks = sum_packed(sz, after((grad_parts, out_back), got), n_rows, n_tail)
     got = [blocks[0]] + [shift(blocks[k], "hg", sz.groups, k) for k in range(1, sz.groups)]
     sums = unpack_sums(sz, place, after(grad_back, got), n_rows, n_tail)
-    grad_qkv, grad_out, *cuts = join_heads(sz, place, all_grp(sz, sums), n_rows, n_tail)
     output, grad_tokens = unsort_rows(sz, place, doc_blocks, out_back, grad_back)
+    grad_qkv, grad_out, *cuts = join_heads(sz, place, all_grp(sz, sums, output), n_rows, n_tail)
 
     ff_parts = sum_groups(sz, place, after(pieces, ff_far))
     ff_parts = [ff_parts[0]] + [shift(ff_parts[s], "part", sz.parts, s) for s in range(1, sz.parts)]

time: 240 us -> 240 us (level)
  the two profiles are of different devices: /device:TPU:9 before, /device:TPU:25 now
where the time goes in v3:
time: 240 us; the launch traced here: 235 us
  Pallas kernels  104 us (43%)
  waiting for transfers between devices  58.7 us (24%)
  starting transfers between devices  49.9 us (21%)
  local copies, waits for them, and re-layouts  18.9 us (8%)
  other arithmetic  2.46 us (1%)
    pallas_call x22, Pallas kernels, whole_call(): pl.pallas_call(body, out_shape=shapes, in_specs=specs, out_specs=[pl.Bloc...  104 us
    ppermute x24, waiting for transfers between devices, shift(): lax.ppermute(value, axis, [(i, (i + step) % size) for i in range(size)])  30.2 us
    ppermute x24, starting transfers between devices, shift(): lax.ppermute(value, axis, [(i, (i + step) % size) for i in range(size)])  16.3 us
    unnamed x110, local copies, waits for them, and re-layouts  12.4 us
    ppermute x12, starting transfers between devices, to_peer(): return lax.ppermute(value, ('core', 'hg'), pairs)  11.8 us
    ppermute x12, waiting for transfers between devices, to_peer(): return lax.ppermute(value, ('core', 'hg'), pairs)  10.1 us
    all_to_all x1, waiting for transfers between devices, body(): ff_far = lax.all_to_all(ff_sent, 'hg', 0, 0, tiled=True)  7 us
    ppermute x4, starting transfers between devices, from_owner(): lax.ppermute(b, ('core',) + CTX, [(b_, a_) for a_, b_ in owner_pairs(sz,...  6.88 us
  transfers between devices with their start and end apart: 47, of which 16 were waited for; matrix products, arithmetic and copies ran while one was open for 4% of the time, Pallas kernels for 33%

profile of v3, /device:TPU:25, one launch (start us, length us, event | category | flops | bytes accessed | tf_op | source)
XLA Modules:
  0.0 235.1 jit_solution(13472157257717927735)
XLA Ops:
  2.1 2.2 sort_rows.1
  4.3 2.9 %collective-permute-start = (bf16[128,768]{1,0:T(8,128)(2,1)}, bf16[128,768]{1,0:T(8,128)(2,1)S(1)}, u32[]{:S(2)}, u32[]{:S(2)}) collective-permute-start(bf16[128,768]{1,0:T(8,128)(2,1)} %get-tuple-element.141), channel_id=1, source_target_pairs={{0,0},{1,4},{2,8},{3,12},{4,2},{5,6},{6,10},{7,14},{8,1},{9,5},{10... | collective-permute-start | bytes 589832 | tf_op jit(solution)/shard_map/ppermute | solution.py:102
  8.0 5.1 %collective-permute-done = bf16[128,768]{1,0:T(8,128)(2,1)S(1)} collective-permute-done((bf16[128,768]{1,0:T(8,128)(2,1)}, bf16[128,768]{1,0:T(8,128)(2,1)S(1)}, u32[]{:S(2)}, u32[]{:S(2)}) %collective-permute-start) | collective-permute-done | bytes 196640 | tf_op jit(solution)/shard_map/ppermute | solution.py:102
  13.2 5.7 %collective-permute-start.6 = (bf16[256,768]{1,0:T(8,128)(2,1)S(1)}, bf16[256,768]{1,0:T(8,128)(2,1)S(1)}, u32[]{:S(2)}, u32[]{:S(2)}) collective-permute-start(bf16[256,768]{1,0:T(8,128)(2,1)S(1)} %constant_dynamic-update-slice_fusion.refs_0_.refs_4_.refs_3_), channel_id=1, source_target_pairs={{0,2},{2,0},{4,6},{6,4},{8,10},{10,8},{12,14},{14,12},{1,3},{3,1},... | collective-permute-start | bytes 1179656 | tf_op jit(solution)/shard_map/ppermute | solution.py:85
  20.9 3.7 %collective-permute-start.2 = (bf16[128,768]{1,0:T(8,128)(2,1)}, bf16[128,768]{1,0:T(8,128)(2,1)S(1)}, u32[]{:S(2)}, u32[]{:S(2)}) collective-permute-start(bf16[128,768]{1,0:T(8,128)(2,1)} %get-tuple-element.145), channel_id=1, source_target_pairs={{0,0},{1,4},{2,8},{3,12},{4,2},{5,6},{6,10},{7,14},{8,1},{9,5},{10... | collective-permute-start | bytes 589832 | tf_op jit(solution)/shard_map/ppermute | solution.py:102
  24.7 8.3 %weight_shares.1 = (bf16[768,768]{1,0:T(8,128)(2,1)}, bf16[768,768]{1,0:T(8,128)(2,1)}, bf16[768,768]{1,0:T(8,128)(2,1)}) custom-call(s32[6]{0:T(128)} %stack.27.place_ref, bf16[768,2304]{1,0:T(8,128)(2,1)} %qkv_ref, bf16[768,3072]{1,0:T(8,128)(2,1)} %fc_in, bf16[3072,768]{1,0:T(8,128)(2,1)} %proj_in), custom_call_target="tpu_custom_call" | custom-call | bytes 16515096 | tf_op jit(solution)/shard_map/weight_shares/pallas_call | solution.py:121
  35.6 11.0 %attend_forward.1 = (bf16[1024,768]{1,0:T(8,128)(2,1)}, bf16[1024,768]{1,0:T(8,128)(2,1)}, bf16[1024,768]{1,0:T(8,128)(2,1)}, f32[1024,128]{1,0:T(8,128)}, f32[1...) custom-call(s32[6]{0:T(128)} %stack.27.place_ref, ...), custom_call_target="tpu_custom_call" | custom-call | flops 8999999488 | bytes 9462828 | tf_op jit(solution)/shard_map/attend_forward/pallas_call | solution.py:121
  46.6 1.6 collective-permute-start.10
  48.1 1.6 collective-permute-start.8
  53.2 2.3 collective-permute-done.9.refs_2_.refs_5_
  56.2 3.2 %project_out.1 = (f32[256,768]{1,0:T(8,128)}, bf16[256,768]{1,0:T(8,128)(2,1)}) custom-call(s32[6]{0:T(128)} %stack.27.place_ref, bf16[256,192]{1,0:T(8,128)(2,1)} %get-tuple-element.156.refs_0_.refs_3_, bf16[256,192]{1,0:T(8,128)(2,1)} %copy-done.13, bf16[256,192]{1,0:T(8,128)(2,1)} %copy-done.14, bf16[256,192]{1,0:T(8,128)(2,1)} %copy-done.12, ...), custom_call_target="tpu_custom_call" | custom-call | bytes 3154968 | tf_op jit(solution)/shard_map/project_out/pallas_call | solution.py:121
  64.5 5.8 %feed_forward_near.1 = (bf16[256,768]{1,0:T(8,128)(2,1)}, bf16[256,768]{1,0:T(8,128)(2,1)}, bf16[256,768]{1,0:T(8,128)(2,1)}, bf16[256,768]{1,0:T(8,128)(2,1)}, ...) custom-call(bf16[256,768]{1,0:T(8,128)(2,1)} %get-tuple-element.160.refs_0_, ...), custom_call_target="tpu_custom_call" | custom-call | bytes 6297600 | tf_op jit(solution)/shard_map/feed_forward_near/pallas_call | solution.py:121
  70.3 3.6 %feed_forward_out.2 = (bf16[256,768]{1,0:T(8,128)(2,1)}, bf16[256,768]{1,0:T(8,128)(2,1)}) custom-call(bf16[256,768]{1,0:T(8,128)(2,1)} %get-tuple-element.163.refs_0_.refs_8_, bf16[256,768]{1,0:T(8,128)(2,1)} %get-tuple-element.164.refs_1_.refs_9_, bf16[768,768]{1,0:T(8,128)(2,1)} %get-tuple-element.162.refs_6_.refs_2_), custom_call_target="tpu_custom_call" | custom-call | bytes 2752512 | tf_op jit(solution)/shard_map/feed_forward_out/pallas_call | solution.py:121
  74.1 1.7 collective-permute-done.15.refs_1_.refs_3_
  76.5 5.8 %feed_forward_far.1 = (bf16[256,768]{1,0:T(8,128)(2,1)}, bf16[256,768]{1,0:T(8,128)(2,1)}, bf16[256,768]{1,0:T(8,128)(2,1)}, bf16[256,768]{1,0:T(8,128)(2,1)}, b...) custom-call(bf16[256,768]{1,0:T(8,128)(2,1)} %copy-done.6, bf16[256,768]{1,0:T(8,128)(2,1)} %copy-done.8, ...), custom_call_target="tpu_custom_call" | custom-call | bytes 6297600 | tf_op jit(solution)/shard_map/feed_forward_far/pallas_call | solution.py:121
  82.8 1.4 collective-permute-done.18
  85.3 1.3 collective-permute-start.22
  86.6 6.8 %feed_forward_weights.1 = bf16[4,2,192,768]{3,2,1,0:T(8,128)(2,1)} custom-call(bf16[256,768]{1,0:T(8,128)(2,1)} %get-tuple-element.160.refs_0_, bf16[256,768]{1,0:T(8,128)(2,1)} %copy-done.5, bf16[256,768]{1,0:T(8,128)(2,1)} %copy-done.6, bf16[256,768]{1,0:T(8,128)(2,1)} %copy-done.8, bf16[256,768]{1,0:T(8,128)(2,1)} %get-tuple-element.170.refs_4_, ...), custom_call_target="tpu_custom_call" | custom-call | bytes 8650752 | tf_op jit(solution)/shard_map/feed_forward_weights/pallas_call | solution.py:121
  93.4 3.0 %feed_forward_out.3 = (bf16[256,768]{1,0:T(8,128)(2,1)}, bf16[256,768]{1,0:T(8,128)(2,1)}) custom-call(bf16[256,768]{1,0:T(8,128)(2,1)} %get-tuple-element.181.refs_10_.refs_0_, bf16[256,768]{1,0:T(8,128)(2,1)} %get-tuple-element.182.refs_11_.refs_1_, bf16[768,768]{1,0:T(8,128)(2,1)} %get-tuple-element.162.refs_6_.refs_2_), custom_call_target="tpu_custom_call" | custom-call | bytes 2752512 | tf_op jit(solution)/shard_map/feed_forward_out/pallas_call | solution.py:121
  97.4 5.5 %middle_backward.1 = (f32[256,768]{1,0:T(8,128)}, bf16[768,384]{1,0:T(8,128)(2,1)}, bf16[768,384]{1,0:T(8,128)(2,1)}, f32[4,768]{1,0:T(4,128)}, bf16[256,192]{1,...) custom-call(s32[6]{0:T(128)} %stack.27.place_ref, ...), custom_call_target="tpu_custom_call" | custom-call | bytes 6306840 | tf_op jit(solution)/shard_map/middle_backward/pallas_call | solution.py:121
  103.4 1.4 collective-permute-start.25
  105.1 3.6 %collective-permute-done.25.refs_2_ = bf16[256,192]{1,0:T(8,128)(2,1)S(1)} collective-permute-done((bf16[256,192]{1,0:T(8,128)(2,1)}, bf16[256,192]{1,0:T(8,128)(2,1)S(1)}, u32[]{:S(2)}, u32[]{:S(2)}) %collective-permute-start.25) | collective-permute-done | bytes 98336 | tf_op jit(solution)/shard_map/ppermute | solution.py:85
  108.7 3.0 %collective-permute-done.26.refs_3_ = bf16[256,192]{1,0:T(8,128)(2,1)S(1)} collective-permute-done((bf16[256,192]{1,0:T(8,128)(2,1)}, bf16[256,192]{1,0:T(8,128)(2,1)S(1)}, u32[]{:S(2)}, u32[]{:S(2)}) %collective-permute-start.26) | collective-permute-done | bytes 98336 | tf_op jit(solution)/shard_map/ppermute | solution.py:85
  112.3 6.2 %all-to-all-start = ((bf16[4,2,192,768]{3,2,1,0:T(8,128)(2,1)}), bf16[4,2,192,768]{3,2,1,0:T(8,128)(2,1)S(1)}, u32[]{:S(2)}, u32[]{:S(2)}) async-start(bf16[4,2,192,768]{3,2,1,0:T(8,128)(2,1)} %feed_forward_weights.1), calls=%async_computation | async-start | bytes 4718592 | tf_op jit(solution)/shard_map/all_to_all | solution.py:1080
  121.4 21.1 %attend_backward.1 = (f32[1,768]{1,0:T(1,128)}, f32[2,768]{1,0:T(2,128)}, bf16[256,768]{1,0:T(8,128)(2,1)}, bf16[256,768]{1,0:T(8,128)(2,1)}, bf16[256,768]{1,0:...) custom-call(s32[6]{0:T(128)} %stack.27.place_ref, ...), custom_call_target="tpu_custom_call" | custom-call | bytes 10642476 | tf_op jit(solution)/shard_map/attend_backward/pallas_call | solution.py:121
  144.3 1.9 pack_vectors.1.refs_4_
  146.2 2.5 %finish_middle.1 = (bf16[128,768]{1,0:T(8,128)(2,1)}, bf16[128,768]{1,0:T(8,128)(2,1)}) custom-call(bf16[256,768]{1,0:T(8,128)(2,1)} %get-tuple-element.213.refs_0_, bf16[256,768]{1,0:T(8,128)(2,1)} %copy-done.15, bf16[256,768]{1,0:T(8,128)(2,1)} %copy-done.16, bf16[256,768]{1,0:T(8,128)(2,1)} %copy-done.18, f32[256,768]{1,0:T(8,128)} %get-tuple-element.189.refs_8_.refs_4_, ...), custom_call_target="tpu_custom_call" | custom-call | bytes 2755584 | tf_op jit(solution)/shard_map/finish_middle/pallas_call | solution.py:121
  149.1 8.8 %collective-permute-done.34.refs_1_ = bf16[8,48,768]{2,1,0:T(8,128)(2,1)S(1)} collective-permute-done((bf16[8,48,768]{2,1,0:T(8,128)(2,1)}, bf16[8,48,768]{2,1,0:T(8,128)(2,1)S(1)}, u32[]{:S(2)}, u32[]{:S(2)}) %collective-permute-start.34) | collective-permute-done | bytes 589856 | tf_op jit(solution)/shard_map/ppermute | solution.py:74
  158.7 3.0 %pack_sums.1 = (bf16[4,112,768]{2,1,0:T(8,128)(2,1)}, bf16[4,112,768]{2,1,0:T(8,128)(2,1)}) custom-call(s32[6]{0:T(128)} %stack.27.place_ref, bf16[8,48,768]{2,1,0:T(8,128)(2,1)} %get-tuple-element.211.refs_0_, bf16[8,48,768]{2,1,0:T(8,128)(2,1)} %copy-done.11, bf16[8,96,384]{2,1,0:T(8,128)(2,1)} %bitcast.12, bf16[8,96,384]{2,1,0:T(8,128)(2,1)} %bitcast.13, ...), custom_call_target="tpu_custom_call" | custom-call | bytes 3932184 | tf_op jit(solution)/shard_map/pack_sums/pallas_call | solution.py:121
  162.8 7.0 %all-to-all-done.got_ref = bf16[4,2,192,768]{3,2,1,0:T(8,128)(2,1)S(1)} async-done(((bf16[4,2,192,768]{3,2,1,0:T(8,128)(2,1)}), bf16[4,2,192,768]{3,2,1,0:T(8,128)(2,1)S(1)}, u32[]{:S(2)}, u32[]{:S(2)}) %all-to-all-start) | async-done | bytes 2359328 | tf_op jit(solution)/shard_map/all_to_all | solution.py:1080
  169.8 1.4 copy-done
  171.2 2.7 %sum_groups.1 = (bf16[192,768]{1,0:T(8,128)(2,1)}, bf16[192,768]{1,0:T(8,128)(2,1)}) custom-call(s32[6]{0:T(128)} %stack.27.place_ref, bf16[4,2,192,768]{3,2,1,0:T(8,128)(2,1)} %copy-done), custom_call_target="tpu_custom_call" | custom-call | bytes 2949144 | tf_op jit(solution)/shard_map/sum_groups/pallas_call | solution.py:121
  173.9 4.8 %collective-permute-start.27 = (bf16[128,768]{1,0:T(8,128)(2,1)S(1)}, bf16[128,768]{1,0:T(8,128)(2,1)S(1)}, u32[]{:S(2)}, u32[]{:S(2)}) collective-permute-start(bf16[128,768]{1,0:T(8,128)(2,1)S(1)} %copy-done.53), channel_id=1, source_target_pairs={{0,0},{4,1},{8,2},{12,3},{2,4},{6,5},{10,6},{14,7},{1,8},{5,9},{9,... | collective-permute-start | bytes 589832 | tf_op jit(solution)/shard_map/ppermute | solution.py:107
  179.5 2.9 %finish_tokens.1 = (bf16[128,768]{1,0:T(8,128)(2,1)}, bf16[128,768]{1,0:T(8,128)(2,1)}) custom-call(bf16[256,768]{1,0:T(8,128)(2,1)} %get-tuple-element.219.refs_0_, bf16[256,768]{1,0:T(8,128)(2,1)} %copy-done.17, bf16[256,768]{1,0:T(8,128)(2,1)} %collective-permute-done.31.refs_2_, bf16[256,768]{1,0:T(8,128)(2,1)} %copy-done.2, ...), custom_call_target="tpu_custom_call" | custom-call | bytes 2755584 | tf_op jit(solution)/shard_map/finish_tokens/pallas_call | solution.py:121
  182.4 2.0 collective-permute-start.32
  184.4 3.3 %collective-permute-done.27.refs_0_ = bf16[128,768]{1,0:T(8,128)(2,1)S(1)} collective-permute-done((bf16[128,768]{1,0:T(8,128)(2,1)S(1)}, bf16[128,768]{1,0:T(8,128)(2,1)S(1)}, u32[]{:S(2)}, u32[]{:S(2)}) %collective-permute-start.27) | collective-permute-done | bytes 196640 | tf_op jit(solution)/shard_map/ppermute | solution.py:107
  187.7 3.0 %collective-permute-done.28.refs_1_ = bf16[128,768]{1,0:T(8,128)(2,1)S(1)} collective-permute-done((bf16[128,768]{1,0:T(8,128)(2,1)S(1)}, bf16[128,768]{1,0:T(8,128)(2,1)S(1)}, u32[]{:S(2)}, u32[]{:S(2)}) %collective-permute-start.28) | collective-permute-done | bytes 196640 | tf_op jit(solution)/shard_map/ppermute | solution.py:107
  191.5 2.2 sum_packed.1
  193.7 1.6 collective-permute-start.37
  195.4 1.5 collective-permute-start.38
  196.8 1.9 sum_parts.1.refs_0_
  199.8 13.0 %collective-permute-done.37.refs_2_ = bf16[112,768]{1,0:T(8,128)(2,1)S(1)} collective-permute-done((bf16[112,768]{1,0:T(8,128)(2,1)}, bf16[112,768]{1,0:T(8,128)(2,1)S(1)}, u32[]{:S(2)}, u32[]{:S(2)}) %collective-permute-start.37) | collective-permute-done | bytes 172064 | tf_op jit(solution)/shard_map/ppermute | solution.py:74
  214.2 2.0 unpack_sums.1.refs_0_
  218.0 2.6 %unsort_rows.1 = (f32[8,32,768]{2,1,0:T(8,128)}, f32[8,32,768]{2,1,0:T(8,128)}) custom-call(s32[6]{0:T(128)} %stack.27.place_ref, s32[1,5]{1,0:T(1,128)} %doc_ref.3, bf16[128,768]{1,0:T(8,128)(2,1)} %copy-done.29, bf16[128,768]{1,0:T(8,128)(2,1)} %copy-done.30, bf16[128,768]{1,0:T(8,128)(2,1)} %copy-done.31, bf16[128,768]{1,0:T(8,128)(2,1)} %copy-done.32), custom_call_target="tpu_custom_call" | custom-call | bytes 2359340 | tf_op jit(solution)/shard_map/unsort_rows/pallas_call | solution.py:121
  220.6 2.9 %collective-permute-done.39.refs_1_ = bf16[160,768]{1,0:T(8,128)(2,1)S(1)} collective-permute-done((bf16[160,768]{1,0:T(8,128)(2,1)}, bf16[160,768]{1,0:T(8,128)(2,1)S(1)}, u32[]{:S(2)}, u32[]{:S(2)}) %collective-permute-start.39) | collective-permute-done | bytes 245792 | tf_op jit(solution)/shard_map/ppermute | solution.py:74
  224.7 1.7 collective-permute-done.40.refs_2_
  227.7 2.6 %join_heads.1 = (f32[96,2304]{1,0:T(8,128)}, f32[96,768]{1,0:T(8,128)}, f32[96]{0:T(128)}, f32[96]{0:T(128)}, f32[288]{0:T(512)}, /*index=5*/f32[96]{0:T(128)}, ...) custom-call(s32[6]{0:T(128)} %stack.27.place_ref, bf16[160,768]{1,0:T(8,128)(2,1)} %unpack_sums.1.refs_0_, ...), custom_call_target="tpu_custom_call" | custom-call | bytes 2167704 | tf_op jit(solution)/shard_map/join_heads/pallas_call | solution.py:121
  231.8 3.1 %join_shares.1 = (f32[96,3072]{1,0:T(8,128)}, f32[384,768]{1,0:T(8,128)}) custom-call(s32[6]{0:T(128)} %stack.27.place_ref, bf16[192,768]{1,0:T(8,128)(2,1)} %sum_parts.1.refs_0_, bf16[192,768]{1,0:T(8,128)(2,1)} %copy-done.23, bf16[192,768]{1,0:T(8,128)(2,1)} %copy-done.24, bf16[192,768]{1,0:T(8,128)(2,1)} %copy-done.25), custom_call_target="tpu_custom_call" | custom-call | bytes 3538968 | tf_op jit(solution)/shard_map/join_shares/pallas_call | solution.py:121
  (200 shorter events, 37.8 us)
Async XLA Ops:
  0.7 32.5 %collective-permute-start.4 = (s32[1,5]{1,0:T(1,128)}, s32[1,5]{1,0:T(1,128)S(1)}, u32[]{:S(2)}, u32[]{:S(2)}) collective-permute-start(s32[1,5]{1,0:T(1,128)} %doc_ref.3), channel_id=1, source_target_pairs={{0,8},{8,0},{1,9},{9,1},{2,10},{10,2},{3,11},{11,3},{4,12},{12,4},... | collective-permute-start | bytes 68 | tf_op jit(solution)/shard_map/ppermute | solution.py:74
  4.3 8.8 %collective-permute-start = (bf16[128,768]{1,0:T(8,128)(2,1)}, bf16[128,768]{1,0:T(8,128)(2,1)S(1)}, u32[]{:S(2)}, u32[]{:S(2)}) collective-permute-start(bf16[128,768]{1,0:T(8,128)(2,1)} %get-tuple-element.141), channel_id=1, source_target_pairs={{0,0},{1,4},{2,8},{3,12},{4,2},{5,6},{6,10},{7,14},{8,1},{9,5},{10... | collective-permute-start | bytes 589832 | tf_op jit(solution)/shard_map/ppermute | solution.py:102
  7.2 5.9 %collective-permute-start.1 = (bf16[128,768]{1,0:T(8,128)(2,1)}, bf16[128,768]{1,0:T(8,128)(2,1)S(1)}, u32[]{:S(2)}, u32[]{:S(2)}) collective-permute-start(bf16[128,768]{1,0:T(8,128)(2,1)} %get-tuple-element.142), channel_id=1, source_target_pairs={{0,4},{1,0},{2,12},{3,8},{4,6},{5,2},{6,14},{7,10},{8,5},{9,1},{10... | collective-permute-start | bytes 589832 | tf_op jit(solution)/shard_map/ppermute | solution.py:102
  13.2 19.9 %collective-permute-start.6 = (bf16[256,768]{1,0:T(8,128)(2,1)S(1)}, bf16[256,768]{1,0:T(8,128)(2,1)S(1)}, u32[]{:S(2)}, u32[]{:S(2)}) collective-permute-start(bf16[256,768]{1,0:T(8,128)(2,1)S(1)} %constant_dynamic-update-slice_fusion.refs_0_.refs_4_.refs_3_), channel_id=1, source_target_pairs={{0,2},{2,0},{4,6},{6,4},{8,10},{10,8},{12,14},{14,12},{1,3},{3,1},... | collective-permute-start | bytes 1179656 | tf_op jit(solution)/shard_map/ppermute | solution.py:85
  20.9 12.9 %collective-permute-start.5 = (bf16[256,768]{1,0:T(8,128)(2,1)S(1)}, bf16[256,768]{1,0:T(8,128)(2,1)S(1)}, u32[]{:S(2)}, u32[]{:S(2)}) collective-permute-start(bf16[256,768]{1,0:T(8,128)(2,1)S(1)} %constant_dynamic-update-slice_fusion.refs_0_.refs_4_.refs_3_), channel_id=1, source_target_pairs={{0,8},{2,10},{4,12},{6,14},{8,0},{10,2},{12,4},{14,6},{1,9},{3,11}... | collective-permute-start | bytes 1179656 | tf_op jit(solution)/shard_map/ppermute | solution.py:85
  20.9 12.8 %collective-permute-start.2 = (bf16[128,768]{1,0:T(8,128)(2,1)}, bf16[128,768]{1,0:T(8,128)(2,1)S(1)}, u32[]{:S(2)}, u32[]{:S(2)}) collective-permute-start(bf16[128,768]{1,0:T(8,128)(2,1)} %get-tuple-element.145), channel_id=1, source_target_pairs={{0,0},{1,4},{2,8},{3,12},{4,2},{5,6},{6,10},{7,14},{8,1},{9,5},{10... | collective-permute-start | bytes 589832 | tf_op jit(solution)/shard_map/ppermute | solution.py:102
  24.6 9.1 %collective-permute-start.3 = (bf16[128,768]{1,0:T(8,128)(2,1)}, bf16[128,768]{1,0:T(8,128)(2,1)S(1)}, u32[]{:S(2)}, u32[]{:S(2)}) collective-permute-start(bf16[128,768]{1,0:T(8,128)(2,1)} %get-tuple-element.146), channel_id=1, source_target_pairs={{0,4},{1,0},{2,12},{3,8},{4,6},{5,2},{6,14},{7,10},{8,5},{9,1},{10... | collective-permute-start | bytes 589832 | tf_op jit(solution)/shard_map/ppermute | solution.py:102
  33.0 1.8 collective-permute-start.7
  46.6 6.6 %collective-permute-start.10 = (bf16[256,192]{1,0:T(8,128)(2,1)}, bf16[256,192]{1,0:T(8,128)(2,1)S(1)}, u32[]{:S(2)}, u32[]{:S(2)}) collective-permute-start(bf16[256,192]{1,0:T(8,128)(2,1)} %get-tuple-element.159), channel_id=1, source_target_pairs={{0,10},{2,8},{4,14},{6,12},{8,2},{10,0},{12,6},{14,4},{1,11},{3,9}... | collective-permute-start | bytes 294920 | tf_op jit(solution)/shard_map/ppermute | solution.py:85
  48.1 5.1 %collective-permute-start.8 = (bf16[256,192]{1,0:T(8,128)(2,1)}, bf16[256,192]{1,0:T(8,128)(2,1)S(1)}, u32[]{:S(2)}, u32[]{:S(2)}) collective-permute-start(bf16[256,192]{1,0:T(8,128)(2,1)} %get-tuple-element.157), channel_id=1, source_target_pairs={{0,8},{2,10},{4,12},{6,14},{8,0},{10,2},{12,4},{14,6},{1,9},{3,11}... | collective-permute-start | bytes 294920 | tf_op jit(solution)/shard_map/ppermute | solution.py:85
  49.7 5.8 %collective-permute-start.9 = (bf16[256,192]{1,0:T(8,128)(2,1)}, bf16[256,192]{1,0:T(8,128)(2,1)S(1)}, u32[]{:S(2)}, u32[]{:S(2)}) collective-permute-start(bf16[256,192]{1,0:T(8,128)(2,1)} %get-tuple-element.158), channel_id=1, source_target_pairs={{0,2},{2,0},{4,6},{6,4},{8,10},{10,8},{12,14},{14,12},{1,3},{3,1},... | collective-permute-start | bytes 294920 | tf_op jit(solution)/shard_map/ppermute | solution.py:85
  51.5 12.2 %collective-permute-start.12 = (bf16[256,768]{1,0:T(8,128)(2,1)S(1)}, bf16[256,768]{1,0:T(8,128)(2,1)S(1)}, u32[]{:S(2)}, u32[]{:S(2)}) collective-permute-start(bf16[256,768]{1,0:T(8,128)(2,1)S(1)} %constant_dynamic-update-slice_fusion.2.refs_2_.refs_12_.refs_7_), channel_id=1, source_target_pairs={{0,8},{8,0},{1,9},{9,1},{2,10},{10,2},{3,11},{11,3},{4,12},{12,4},... | collective-permute-start | bytes 1179656 | tf_op jit(solution)/shard_map/ppermute | solution.py:74
  51.9 10.7 %collective-permute-start.16 = (bf16[256,768]{1,0:T(8,128)(2,1)S(1)}, bf16[256,768]{1,0:T(8,128)(2,1)S(1)}, u32[]{:S(2)}, u32[]{:S(2)}) collective-permute-start(bf16[256,768]{1,0:T(8,128)(2,1)S(1)} %constant_dynamic-update-slice_fusion.2.refs_2_.refs_12_.refs_7_), channel_id=1, source_target_pairs={{0,16},{16,0},{1,17},{17,1},{2,18},{18,2},{3,19},{19,3},{4,20},{20... | collective-permute-start | bytes 1179656 | tf_op jit(solution)/shard_map/ppermute | solution.py:74
  59.3 4.3 %collective-permute-start.11 = (bf16[256,768]{1,0:T(8,128)(2,1)}, bf16[256,768]{1,0:T(8,128)(2,1)S(1)}, u32[]{:S(2)}, u32[]{:S(2)}) collective-permute-start(bf16[256,768]{1,0:T(8,128)(2,1)} %get-tuple-element.160.refs_0_), channel_id=1, source_target_pairs={{0,8},{8,0},{1,9},{9,1},{2,10},{10,2},{3,11},{11,3},{4,12},{12,4},... | collective-permute-start | bytes 1179656 | tf_op jit(solution)/shard_map/ppermute | solution.py:74
  60.0 14.0 %collective-permute-start.14 = (bf16[256,768]{1,0:T(8,128)(2,1)}, bf16[256,768]{1,0:T(8,128)(2,1)S(1)}, u32[]{:S(2)}, u32[]{:S(2)}) collective-permute-start(bf16[256,768]{1,0:T(8,128)(2,1)} %get-tuple-element.160.refs_0_), channel_id=1, source_target_pairs={{0,16},{16,0},{1,17},{17,1},{2,18},{18,2},{3,19},{19,3},{4,20},{20... | collective-permute-start | bytes 1179656 | tf_op jit(solution)/shard_map/ppermute | solution.py:74
  62.7 11.4 %collective-permute-start.17 = (bf16[256,768]{1,0:T(8,128)(2,1)S(1)}, bf16[256,768]{1,0:T(8,128)(2,1)S(1)}, u32[]{:S(2)}, u32[]{:S(2)}) collective-permute-start(bf16[256,768]{1,0:T(8,128)(2,1)S(1)} %collective-permute-done.16.refs_2_.refs_14_), channel_id=1, source_target_pairs={{0,8},{8,0},{1,9},{9,1},{2,10},{10,2},{3,11},{11,3},{4,12},{12,4},... | collective-permute-start | bytes 1179656 | tf_op jit(solution)/shard_map/ppermute | solution.py:74
  74.0 1.8 collective-permute-start.15
  82.3 1.9 collective-permute-start.18
  82.4 14.0 %collective-permute-start.21 = (bf16[256,768]{1,0:T(8,128)(2,1)S(1)}, bf16[256,768]{1,0:T(8,128)(2,1)S(1)}, u32[]{:S(2)}, u32[]{:S(2)}) collective-permute-start(bf16[256,768]{1,0:T(8,128)(2,1)S(1)} %copy-done.49), channel_id=1, source_target_pairs={{0,8},{8,0},{1,9},{9,1},{2,10},{10,2},{3,11},{11,3},{4,12},{12,4},... | collective-permute-start | bytes 1179656 | tf_op jit(solution)/shard_map/ppermute | solution.py:74
  85.3 11.1 %collective-permute-start.22 = (bf16[256,768]{1,0:T(8,128)(2,1)S(1)}, bf16[256,768]{1,0:T(8,128)(2,1)S(1)}, u32[]{:S(2)}, u32[]{:S(2)}) collective-permute-start(bf16[256,768]{1,0:T(8,128)(2,1)S(1)} %add_convert_fusion.1), channel_id=1, source_target_pairs={{0,16},{16,0},{1,17},{17,1},{2,18},{18,2},{3,19},{19,3},{4,20},{20... | collective-permute-start | bytes 1179656 | tf_op jit(solution)/shard_map/ppermute | solution.py:74
  102.9 2.2 collective-permute-start.24
  103.4 5.3 %collective-permute-start.25 = (bf16[256,192]{1,0:T(8,128)(2,1)}, bf16[256,192]{1,0:T(8,128)(2,1)S(1)}, u32[]{:S(2)}, u32[]{:S(2)}) collective-permute-start(bf16[256,192]{1,0:T(8,128)(2,1)} %get-tuple-element.200), channel_id=1, source_target_pairs={{0,2},{2,0},{4,6},{6,4},{8,10},{10,8},{12,14},{14,12},{1,3},{3,1},... | collective-permute-start | bytes 294920 | tf_op jit(solution)/shard_map/ppermute | solution.py:85
  104.8 6.9 %collective-permute-start.26 = (bf16[256,192]{1,0:T(8,128)(2,1)}, bf16[256,192]{1,0:T(8,128)(2,1)S(1)}, u32[]{:S(2)}, u32[]{:S(2)}) collective-permute-start(bf16[256,192]{1,0:T(8,128)(2,1)} %get-tuple-element.201), channel_id=1, source_target_pairs={{0,10},{2,8},{4,14},{6,12},{8,2},{10,0},{12,6},{14,4},{1,11},{3,9}... | collective-permute-start | bytes 294920 | tf_op jit(solution)/shard_map/ppermute | solution.py:85
  112.3 57.5 %all-to-all-start = ((bf16[4,2,192,768]{3,2,1,0:T(8,128)(2,1)}), bf16[4,2,192,768]{3,2,1,0:T(8,128)(2,1)S(1)}, u32[]{:S(2)}, u32[]{:S(2)}) async-start(bf16[4,2,192,768]{3,2,1,0:T(8,128)(2,1)} %feed_forward_weights.1), calls=%async_computation | async-start | bytes 4718592 | tf_op jit(solution)/shard_map/all_to_all | solution.py:1080
  118.5 24.0 %collective-permute-start.23 = (bf16[768,384]{1,0:T(8,128)(2,1)S(1)}, bf16[768,384]{1,0:T(8,128)(2,1)S(1)}, u32[]{:S(2)}, u32[]{:S(2)}) collective-permute-start(bf16[768,384]{1,0:T(8,128)(2,1)S(1)} %copy-done.47), channel_id=1, source_target_pairs={{0,8},{8,0},{1,9},{9,1},{2,10},{10,2},{3,11},{11,3},{4,12},{12,4},... | collective-permute-start | bytes 1769480 | tf_op jit(solution)/shard_map/ppermute | solution.py:74
  119.2 23.2 %collective-permute-start.13 = (bf16[256,768]{1,0:T(8,128)(2,1)}, bf16[256,768]{1,0:T(8,128)(2,1)S(1)}, u32[]{:S(2)}, u32[]{:S(2)}) collective-permute-start(bf16[256,768]{1,0:T(8,128)(2,1)} %get-tuple-element.166), channel_id=1, source_target_pairs={{0,8},{8,0},{1,9},{9,1},{2,10},{10,2},{3,11},{11,3},{4,12},{12,4},... | collective-permute-start | bytes 1179656 | tf_op jit(solution)/shard_map/ppermute | solution.py:74
  119.3 23.1 %collective-permute-start.19 = (bf16[256,768]{1,0:T(8,128)(2,1)}, bf16[256,768]{1,0:T(8,128)(2,1)S(1)}, u32[]{:S(2)}, u32[]{:S(2)}) collective-permute-start(bf16[256,768]{1,0:T(8,128)(2,1)} %get-tuple-element.183), channel_id=1, source_target_pairs={{0,16},{8,24},{16,0},{24,8},{1,17},{9,25},{17,1},{25,9},{2,18},{10... | collective-permute-start | bytes 1179656 | tf_op jit(solution)/shard_map/ppermute | solution.py:911
  120.4 22.1 %collective-permute-start.20 = (bf16[256,768]{1,0:T(8,128)(2,1)}, bf16[256,768]{1,0:T(8,128)(2,1)S(1)}, u32[]{:S(2)}, u32[]{:S(2)}) collective-permute-start(bf16[256,768]{1,0:T(8,128)(2,1)} %get-tuple-element.184), channel_id=1, source_target_pairs={{0,24},{8,16},{16,8},{24,0},{1,25},{9,17},{17,9},{25,1},{2,26},{10... | collective-permute-start | bytes 1179656 | tf_op jit(solution)/shard_map/ppermute | solution.py:911
  142.5 15.4 %collective-permute-start.34 = (bf16[8,48,768]{2,1,0:T(8,128)(2,1)}, bf16[8,48,768]{2,1,0:T(8,128)(2,1)S(1)}, u32[]{:S(2)}, u32[]{:S(2)}) collective-permute-start(bf16[8,48,768]{2,1,0:T(8,128)(2,1)} %get-tuple-element.212), channel_id=1, source_target_pairs={{0,16},{16,0},{1,17},{17,1},{2,18},{18,2},{3,19},{19,3},{4,20},{20... | collective-permute-start | bytes 1769480 | tf_op jit(solution)/shard_map/ppermute | solution.py:74
  143.6 18.1 %collective-permute-start.30 = (bf16[256,768]{1,0:T(8,128)(2,1)}, bf16[256,768]{1,0:T(8,128)(2,1)S(1)}, u32[]{:S(2)}, u32[]{:S(2)}) collective-permute-start(bf16[256,768]{1,0:T(8,128)(2,1)} %get-tuple-element.222), channel_id=1, source_target_pairs={{0,8},{2,10},{4,12},{6,14},{8,0},{10,2},{12,4},{14,6},{1,9},{3,11}... | collective-permute-start | bytes 1179656 | tf_op jit(solution)/shard_map/ppermute | solution.py:85
  148.8 30.0 %collective-permute-start.29 = (bf16[256,768]{1,0:T(8,128)(2,1)}, bf16[256,768]{1,0:T(8,128)(2,1)S(1)}, u32[]{:S(2)}, u32[]{:S(2)}) collective-permute-start(bf16[256,768]{1,0:T(8,128)(2,1)} %get-tuple-element.220), channel_id=1, source_target_pairs={{0,8},{2,10},{4,12},{6,14},{8,0},{10,2},{12,4},{14,6},{1,9},{3,11}... | collective-permute-start | bytes 1179656 | tf_op jit(solution)/shard_map/ppermute | solution.py:85
  161.6 29.0 %collective-permute-start.35 = (bf16[4,112,768]{2,1,0:T(8,128)(2,1)}, bf16[4,112,768]{2,1,0:T(8,128)(2,1)S(1)}, u32[]{:S(2)}, u32[]{:S(2)}) collective-permute-start(bf16[4,112,768]{2,1,0:T(8,128)(2,1)} %get-tuple-element.235), channel_id=1, source_target_pairs={{0,1},{1,0},{2,3},{3,2},{4,5},{5,4},{6,7},{7,6},{8,9},{9,8},{10,11... | collective-permute-start | bytes 2064392 | tf_op jit(solution)/shard_map/ppermute | solution.py:74
  162.5 16.5 %collective-permute-start.31 = (bf16[256,768]{1,0:T(8,128)(2,1)}, bf16[256,768]{1,0:T(8,128)(2,1)}, u32[]{:S(2)}, u32[]{:S(2)}) collective-permute-start(bf16[256,768]{1,0:T(8,128)(2,1)} %add_convert_fusion), channel_id=1, source_target_pairs={{0,2},{2,0},{4,6},{6,4},{8,10},{10,8},{12,14},{14,12},{1,3},{3,1},... | collective-permute-start | bytes 1179656 | tf_op jit(solution)/shard_map/ppermute | solution.py:85
  173.9 21.5 %collective-permute-start.42 = (bf16[192,768]{1,0:T(8,128)(2,1)}, bf16[192,768]{1,0:T(8,128)(2,1)S(1)}, u32[]{:S(2)}, u32[]{:S(2)}) collective-permute-start(bf16[192,768]{1,0:T(8,128)(2,1)} %get-tuple-element.259), channel_id=1, source_target_pairs={{0,1},{1,0},{2,3},{3,2},{4,5},{5,4},{6,7},{7,6},{8,9},{9,8},{10,11... | collective-permute-start | bytes 884744 | tf_op jit(solution)/shard_map/ppermute | solution.py:74
  173.9 13.8 %collective-permute-start.27 = (bf16[128,768]{1,0:T(8,128)(2,1)S(1)}, bf16[128,768]{1,0:T(8,128)(2,1)S(1)}, u32[]{:S(2)}, u32[]{:S(2)}) collective-permute-start(bf16[128,768]{1,0:T(8,128)(2,1)S(1)} %copy-done.53), channel_id=1, source_target_pairs={{0,0},{4,1},{8,2},{12,3},{2,4},{6,5},{10,6},{14,7},{1,8},{5,9},{9,... | collective-permute-start | bytes 589832 | tf_op jit(solution)/shard_map/ppermute | solution.py:107
  178.8 11.9 %collective-permute-start.28 = (bf16[128,768]{1,0:T(8,128)(2,1)S(1)}, bf16[128,768]{1,0:T(8,128)(2,1)S(1)}, u32[]{:S(2)}, u32[]{:S(2)}) collective-permute-start(bf16[128,768]{1,0:T(8,128)(2,1)S(1)} %copy-done.52), channel_id=1, source_target_pairs={{4,0},{0,1},{12,2},{8,3},{6,4},{2,5},{14,6},{10,7},{5,8},{1,9},{13... | collective-permute-start | bytes 589832 | tf_op jit(solution)/shard_map/ppermute | solution.py:107
  182.4 16.3 %collective-permute-start.32 = (bf16[128,768]{1,0:T(8,128)(2,1)}, bf16[128,768]{1,0:T(8,128)(2,1)S(1)}, u32[]{:S(2)}, u32[]{:S(2)}) collective-permute-start(bf16[128,768]{1,0:T(8,128)(2,1)} %get-tuple-element.224), channel_id=1, source_target_pairs={{0,0},{4,1},{8,2},{12,3},{2,4},{6,5},{10,6},{14,7},{1,8},{5,9},{9,... | collective-permute-start | bytes 589832 | tf_op jit(solution)/shard_map/ppermute | solution.py:107
  187.7 30.3 %copy-start.29 = (bf16[128,768]{1,0:T(8,128)(2,1)}, bf16[128,768]{1,0:T(8,128)(2,1)S(1)}, u32[]{:S(2)}) copy-start(bf16[128,768]{1,0:T(8,128)(2,1)S(1)} %collective-permute-done.27.refs_0_) | copy-start | bytes 589828
  187.7 12.1 %collective-permute-start.33 = (bf16[128,768]{1,0:T(8,128)(2,1)}, bf16[128,768]{1,0:T(8,128)(2,1)S(1)}, u32[]{:S(2)}, u32[]{:S(2)}) collective-permute-start(bf16[128,768]{1,0:T(8,128)(2,1)} %get-tuple-element.225), channel_id=1, source_target_pairs={{4,0},{0,1},{12,2},{8,3},{6,4},{2,5},{14,6},{10,7},{5,8},{1,9},{13... | collective-permute-start | bytes 589832 | tf_op jit(solution)/shard_map/ppermute | solution.py:107
  193.7 6.0 %collective-permute-start.36 = (bf16[112,768]{1,0:T(8,128)(2,1)}, bf16[112,768]{1,0:T(8,128)(2,1)S(1)}, u32[]{:S(2)}, u32[]{:S(2)}) collective-permute-start(bf16[112,768]{1,0:T(8,128)(2,1)} %get-tuple-element.239), channel_id=1, source_target_pairs={{0,2},{2,4},{4,6},{6,0},{1,3},{3,5},{5,7},{7,1},{8,10},{10,12},{12... | collective-permute-start | bytes 516104 | tf_op jit(solution)/shard_map/ppermute | solution.py:74
  193.7 19.1 %collective-permute-start.37 = (bf16[112,768]{1,0:T(8,128)(2,1)}, bf16[112,768]{1,0:T(8,128)(2,1)S(1)}, u32[]{:S(2)}, u32[]{:S(2)}) collective-permute-start(bf16[112,768]{1,0:T(8,128)(2,1)} %get-tuple-element.240), channel_id=1, source_target_pairs={{0,4},{2,6},{4,0},{6,2},{1,5},{3,7},{5,1},{7,3},{8,12},{10,14},{12... | collective-permute-start | bytes 516104 | tf_op jit(solution)/shard_map/ppermute | solution.py:74
  195.4 17.5 %collective-permute-start.38 = (bf16[112,768]{1,0:T(8,128)(2,1)}, bf16[112,768]{1,0:T(8,128)(2,1)S(1)}, u32[]{:S(2)}, u32[]{:S(2)}) collective-permute-start(bf16[112,768]{1,0:T(8,128)(2,1)} %get-tuple-element.241), channel_id=1, source_target_pairs={{0,6},{2,0},{4,2},{6,4},{1,7},{3,1},{5,3},{7,5},{8,14},{10,8},{12,... | collective-permute-start | bytes 516104 | tf_op jit(solution)/shard_map/ppermute | solution.py:74
  198.7 18.5 %collective-permute-start.43 = (bf16[192,768]{1,0:T(8,128)(2,1)}, bf16[192,768]{1,0:T(8,128)(2,1)S(1)}, u32[]{:S(2)}, u32[]{:S(2)}) collective-permute-start(bf16[192,768]{1,0:T(8,128)(2,1)} %sum_parts.1.refs_0_), channel_id=1, source_target_pairs={{0,16},{16,0},{1,17},{17,1},{2,18},{18,2},{3,19},{19,3},{4,20},{20... | collective-permute-start | bytes 884744 | tf_op jit(solution)/shard_map/ppermute | solution.py:74
  216.1 7.4 %collective-permute-start.39 = (bf16[160,768]{1,0:T(8,128)(2,1)}, bf16[160,768]{1,0:T(8,128)(2,1)S(1)}, u32[]{:S(2)}, u32[]{:S(2)}) collective-permute-start(bf16[160,768]{1,0:T(8,128)(2,1)} %unpack_sums.1.refs_0_), channel_id=1, source_target_pairs={{0,16},{16,0},{1,17},{17,1},{2,18},{18,2},{3,19},{19,3},{4,20},{20... | collective-permute-start | bytes 737288 | tf_op jit(solution)/shard_map/ppermute | solution.py:74
  217.2 13.1 %collective-permute-start.44 = (bf16[192,768]{1,0:T(8,128)(2,1)}, bf16[192,768]{1,0:T(8,128)(2,1)S(1)}, u32[]{:S(2)}, u32[]{:S(2)}) collective-permute-start(bf16[192,768]{1,0:T(8,128)(2,1)} %sum_parts.1.refs_0_), channel_id=1, source_target_pairs={{0,8},{8,0},{1,9},{9,1},{2,10},{10,2},{3,11},{11,3},{4,12},{12,4},... | collective-permute-start | bytes 884744 | tf_op jit(solution)/shard_map/ppermute | solution.py:74
  217.9 12.5 %collective-permute-start.45 = (bf16[192,768]{1,0:T(8,128)(2,1)S(1)}, bf16[192,768]{1,0:T(8,128)(2,1)S(1)}, u32[]{:S(2)}, u32[]{:S(2)}) collective-permute-start(bf16[192,768]{1,0:T(8,128)(2,1)S(1)} %collective-permute-done.43.refs_1_), channel_id=1, source_target_pairs={{0,8},{8,0},{1,9},{9,1},{2,10},{10,2},{3,11},{11,3},{4,12},{12,4},... | collective-permute-start | bytes 884744 | tf_op jit(solution)/shard_map/ppermute | solution.py:74
  223.5 2.9 %collective-permute-start.40 = (bf16[160,768]{1,0:T(8,128)(2,1)}, bf16[160,768]{1,0:T(8,128)(2,1)S(1)}, u32[]{:S(2)}, u32[]{:S(2)}) collective-permute-start(bf16[160,768]{1,0:T(8,128)(2,1)} %unpack_sums.1.refs_0_), channel_id=1, source_target_pairs={{0,8},{8,0},{1,9},{9,1},{2,10},{10,2},{3,11},{11,3},{4,12},{12,4},... | collective-permute-start | bytes 737288 | tf_op jit(solution)/shard_map/ppermute | solution.py:74
  224.7 1.7 collective-permute-start.41
  (53 other events, 392.1 us)
